TPU v7x, 128 devices: a whole 4x4x4 slice. The times are simulated.
128 devices in a mesh: dp: 4 (over x), fsdp: 32 (over z, y, core).
Axes of the slice: x: 4, y: 4, z: 4, core: 2. Of those that a mesh axis runs over, the one named last changes fastest.
Arguments:
- features: bfloat16 [98304, 512], P(('dp', 'fsdp')), may hold values from -1200 to 1200
- bn_gain: float32 [512], replicated, may hold values from 0.5 to 1.5
- bn_bias: float32 [512], replicated, may hold values from -3 to 3
- gate_weights: bfloat16 [6, 1024, 1536], P(None, 'fsdp'), may hold values from -0.1875 to 0.1875
- feature_masks: int32 [6, 512], replicated, may hold values 0 or 1
- head_first: bfloat16 [512, 256], P('fsdp'), may hold values from -0.25 to 0.25
- head_first_bias: float32 [256], replicated, may hold values from -3 to 3
- head_second: bfloat16 [256, 10], P('fsdp'), may hold values from -0.75 to 0.75
- head_second_bias: float32 [10], replicated, may hold values from -3 to 3
- labels: int32 [98304], P(('dp', 'fsdp')), may hold values from 0 to 9
Outputs:
- features_grad: float32 [98304, 512], P(('dp', 'fsdp'))
- bn_gain_grad: float32 [512], replicated
- bn_bias_grad: float32 [512], replicated
- gate_weights_grad: float32 [6, 1024, 1536], P(None, 'fsdp')
- head_first_grad: float32 [512, 256], P('fsdp')
- head_first_bias_grad: float32 [256], replicated
- head_second_grad: float32 [256, 10], P('fsdp')
- head_second_bias_grad: float32 [10], replicated
All inputs are finite; a program needn't handle non-finite values.
Results may differ from a plain program's by a relative error of at most 0.0095.
Values may be sent and summed in bfloat16 or wider, within the bound.
No kernel may reach another device: no remote copies, remote signals or barrier semaphores. Data moves between devices by JAX's collectives and lax.ppermute only.
A program may use at most 192 MiB of HBM per device.

v0:
```python
import jax
import jax.numpy as jnp
from jax import lax
from jax.sharding import PartitionSpec as P

epsilon = 1e-05


def exact_gelu(value):
    return jax.nn.gelu(value, approximate=False)


def inner_rows(left, right):
    return lax.dot_general(
        left, right, (((0,), (0,)), ((), ())), preferred_element_type=jnp.float32
    )


def inner_cols(left, right):
    return lax.dot_general(
        left, right, (((1,), (1,)), ((), ())), preferred_element_type=jnp.float32
    )


def on_device(
    features,
    bn_gain,
    bn_bias,
    gate_weights,
    feature_masks,
    head_first,
    head_first_bias,
    head_second,
    head_second_bias,
    labels,
):
    row_count = features.shape[0]
    width = features.shape[1]
    section_count = gate_weights.shape[0]
    classes = head_second.shape[1]
    groups = lax.axis_size("dp")
    owners = lax.axis_size("fsdp")
    total_rows = row_count * groups * owners
    inputs = features.astype(jnp.float32)
    sum_first, sum_square = lax.psum(
        (jnp.sum(inputs, 0), jnp.sum(inputs * inputs, 0)), ("dp", "fsdp")
    )
    feature_mean = sum_first / total_rows
    inv_scale = lax.rsqrt(sum_square / total_rows - feature_mean * feature_mean + epsilon)
    normed = (inputs - feature_mean) * inv_scale
    scaled = normed * bn_gain + bn_bias
    mask_rows = feature_masks.astype(jnp.float32)
    hidden_state = scaled
    stored = []
    for layer_index in range(section_count):
        weight = lax.all_gather(gate_weights[layer_index], "fsdp", axis=0, tiled=True)
        masked_low = (scaled * mask_rows[layer_index]).astype(jnp.bfloat16)
        joined = jnp.concatenate([hidden_state.astype(jnp.bfloat16), masked_low], 1)
        gate_pair = jnp.dot(joined, weight[:, : 2 * width], preferred_element_type=jnp.float32)
        update = jax.nn.sigmoid(gate_pair[:, :width])
        reset_gate = jax.nn.sigmoid(gate_pair[:, width:])
        second = jnp.concatenate([(reset_gate * hidden_state).astype(jnp.bfloat16), masked_low], 1)
        output = jnp.tanh(
            jnp.dot(second, weight[:, 2 * width :], preferred_element_type=jnp.float32)
        )
        kept_weight = None
        stored.append((hidden_state, update, reset_gate, output, joined, second, kept_weight))
        hidden_state = hidden_state + update * (output - hidden_state)
    first_full, second_full = (
        lax.all_gather(head_first, "fsdp", axis=0, tiled=True),
        lax.all_gather(head_second, "fsdp", axis=0, tiled=True),
    )
    head_in = hidden_state.astype(jnp.bfloat16)
    pre_first = jnp.dot(head_in, first_full, preferred_element_type=jnp.float32) + head_first_bias
    activation, gelu_back = jax.vjp(exact_gelu, pre_first)
    activation_low = activation.astype(jnp.bfloat16)
    logits = (
        jnp.dot(activation_low, second_full, preferred_element_type=jnp.float32) + head_second_bias
    )
    probabilities = jax.nn.softmax(logits, axis=1)
    onehot = (labels[:, None] == jnp.arange(classes, dtype=jnp.int32)[None, :]).astype(jnp.float32)
    grad_logits = ((probabilities - onehot) * (1.0 / row_count)).astype(jnp.bfloat16)
    first_full, second_full = (
        lax.all_gather(head_first, "fsdp", axis=0, tiled=True),
        lax.all_gather(head_second, "fsdp", axis=0, tiled=True),
    )
    grad_second_full = inner_rows(activation_low, grad_logits)
    grad_activation = inner_cols(grad_logits, second_full)
    grad_pre = gelu_back(grad_activation)[0].astype(jnp.bfloat16)
    grad_first_full = inner_rows(head_in, grad_pre)
    grad_state = inner_cols(grad_pre, first_full)
    first_bias_part = jnp.sum(grad_pre.astype(jnp.float32), 0)
    second_bias_part = jnp.sum(grad_logits.astype(jnp.float32), 0)
    head_first_grad, head_second_grad = (
        lax.psum_scatter(
            grad_first_full.astype(jnp.bfloat16), "fsdp", scatter_dimension=0, tiled=True
        ).astype(jnp.float32),
        lax.psum_scatter(
            grad_second_full.astype(jnp.bfloat16), "fsdp", scatter_dimension=0, tiled=True
        ).astype(jnp.float32),
    )
    head_first_grad, head_second_grad = lax.psum((head_first_grad, head_second_grad), "dp")
    grad_scaled = jnp.zeros_like(scaled)
    shard_grads = [None] * section_count
    for layer_index in reversed(range(section_count)):
        prior_state, update, reset_gate, output, joined, second, kept_weight = stored[layer_index]
        weight = lax.all_gather(gate_weights[layer_index], "fsdp", axis=0, tiled=True)
        grad_out_pre = (grad_state * update * (1.0 - output * output)).astype(jnp.bfloat16)
        back_second = inner_cols(grad_out_pre, weight[:, 2 * width :])
        grad_reset_input = back_second[:, :width]
        grad_update = grad_state * (output - prior_state) * update * (1.0 - update)
        grad_reset = grad_reset_input * prior_state * reset_gate * (1.0 - reset_gate)
        grad_pair = jnp.concatenate([grad_update, grad_reset], 1).astype(jnp.bfloat16)
        back_first = inner_cols(grad_pair, weight[:, : 2 * width])
        grad_prev = (
            grad_state * (1.0 - update) + grad_reset_input * reset_gate + back_first[:, :width]
        )
        grad_scaled = (
            grad_scaled + (back_first[:, width:] + back_second[:, width:]) * mask_rows[layer_index]
        )
        left_first = joined
        left_second = second

        def weight_term(
            start,
            count,
            left_first=left_first,
            left_second=left_second,
            grad_pair=grad_pair,
            grad_out_pre=grad_out_pre,
        ):
            return jnp.concatenate(
                [inner_rows(left_first, grad_pair), inner_rows(left_second, grad_out_pre)], 1
            )

        grad_shard = lax.psum_scatter(
            weight_term(jnp.int32(0), gate_weights.shape[1] * lax.axis_size("fsdp")).astype(
                jnp.bfloat16
            ),
            "fsdp",
            scatter_dimension=0,
            tiled=True,
        ).astype(jnp.float32)
        grad_shard = lax.psum(grad_shard.astype(jnp.bfloat16), "dp").astype(jnp.float32)
        shard_grads[layer_index] = grad_shard
        grad_state = grad_prev
    grad_scaled = grad_scaled + grad_state
    stacked = jnp.stack(shard_grads, 0)
    sum_grad, sum_cross, first_bias_grad, second_bias_grad = lax.psum(
        (
            jnp.sum(grad_scaled, 0),
            jnp.sum(grad_scaled * normed, 0),
            first_bias_part,
            second_bias_part,
        ),
        ("dp", "fsdp"),
    )
    features_grad = (
        inv_scale
        * bn_gain
        * (grad_scaled - sum_grad / total_rows - normed * sum_cross / total_rows)
    )
    return (
        features_grad,
        sum_cross,
        sum_grad,
        stacked,
        head_first_grad,
        first_bias_grad,
        head_second_grad,
        second_bias_grad,
    )


def solution(mesh):
    placed = (
        P(("dp", "fsdp"), None),
        P(),
        P(),
        P(None, "fsdp", None),
        P(),
        P("fsdp", None),
        P(),
        P("fsdp", None),
        P(),
        P(("dp", "fsdp")),
    )
    return jax.shard_map(
        on_device,
        mesh=mesh,
        in_specs=placed,
        out_specs=(
            P(("dp", "fsdp"), None),
            P(),
            P(),
            P(None, "fsdp", None),
            P("fsdp", None),
            P(),
            P("fsdp", None),
            P(),
        ),
        check_vma=False,
    )
```

profile of v0, /device:TPU:0, one launch (start us, length us, event | category | flops | bytes accessed | tf_op | source)
XLA Modules:
  0.0 976.4 jit_solution(14910623888085264708)
XLA Ops:
  12.9 28.0 %all_gather.39 = bf16[256,10]{1,0:T(8,128)(2,1)} all-gather(bf16[8,10]{1,0:T(8,128)(2,1)S(1)} %copy-done.126), channel_id=1, replica_groups=mesh['dp'=4,'fsdp'=32] {'fsdp'}, dimensions={0}, use_global_device_ids=true | all-gather | bytes 5280 | tf_op jit(solution)/shard_map/all_gather | solution.py:71
  40.9 25.9 %all_gather.38 = bf16[512,256]{1,0:T(8,128)(2,1)} all-gather(bf16[16,256]{1,0:T(8,128)(2,1)S(1)} %copy-done.122), channel_id=1, replica_groups=mesh['dp'=4,'fsdp'=32] {'fsdp'}, dimensions={0}, use_global_device_ids=true | all-gather | bytes 270336 | tf_op jit(solution)/shard_map/all_gather | solution.py:70
  66.8 65.7 %all-reduce.2 = (f32[512]{0:T(512)S(1)}, f32[512]{0:T(512)S(1)}) all-reduce(f32[512]{0:T(512)S(1)} %get-tuple-element.19, f32[512]{0:T(512)S(1)} %get-tuple-element.18), channel_id=1, replica_groups=mesh['dp'=4,'fsdp'=32] {'dp','fsdp'}, use_global_device_ids=true, to_apply=%region_1.0 | all-reduce | flops 1024 | bytes 8192 | tf_op jit(solution)/shard_map/psum | solution.py:45
  133.6 3.9 fusion.22
  137.6 2.9 fusion.47
  141.4 4.6 fusion.166
  146.0 4.0 fusion.18
  151.8 5.0 fusion.165
  156.8 4.0 fusion.14
  163.3 5.0 fusion.164
  168.3 30.7 %all-gather.19.cloned.1.call-done = bf16[1,1024,1536]{2,1,0:T(8,128)(2,1)} async-done(((bf16[1,32,1536]{2,1,0:T(8,128)(2,1)}), bf16[1,1024,1536]{2,1,0:T(8,128)(2,1)}) %all-gather.19.cloned.1.call-update) | async-done | bytes 3145744 | tf_op jit(solution)/shard_map/all_gather | solution.py:56
  199.0 4.0 fusion.10
  205.5 5.4 fusion.163
  210.9 34.7 %all-gather.21.cloned.1.call-done = bf16[1,1024,1536]{2,1,0:T(8,128)(2,1)} async-done(((bf16[1,32,1536]{2,1,0:T(8,128)(2,1)}), bf16[1,1024,1536]{2,1,0:T(8,128)(2,1)}) %all-gather.21.cloned.1.call-update) | async-done | bytes 3145744 | tf_op jit(solution)/shard_map/all_gather | solution.py:56
  245.6 4.0 fusion.6
  252.1 5.0 fusion.162
  257.1 35.1 %all-gather.23.cloned.1.call-done = bf16[1,1024,1536]{2,1,0:T(8,128)(2,1)} async-done(((bf16[1,32,1536]{2,1,0:T(8,128)(2,1)}), bf16[1,1024,1536]{2,1,0:T(8,128)(2,1)}) %all-gather.23.cloned.1.call-update) | async-done | bytes 3145744 | tf_op jit(solution)/shard_map/all_gather | solution.py:56
  292.2 4.0 fusion.2
  311.5 2.0 convolution_convert_fusion
  315.4 4.7 copy.60
  320.2 4.0 fusion
  329.7 2.4 fusion.106
  339.5 4.7 copy.58
  344.5 4.1 fusion.4
  354.3 2.4 fusion.109
  362.1 2.0 pad_maximum_fusion.3
  364.1 4.7 copy.56
  369.2 4.1 fusion.8
  378.8 2.4 fusion.112
  388.6 4.7 copy.54
  393.9 4.0 fusion.12
  401.3 2.4 fusion.115
  409.5 3.0 copy.52
  413.9 3.6 fusion.16
  422.9 2.3 fusion.118
  430.6 2.0 pad_maximum_fusion
  432.6 4.8 copy.50
  439.3 2.4 convolution_convert_fusion.12
  441.7 5.4 fusion.20
  447.2 11.2 %fusion.159 = (f32[512]{0:T(512)S(1)}, f32[512]{0:T(512)S(1)}, f32[768,512]{1,0:T(8,128)}) fusion(f32[512]{0:T(512)S(1)} %copy-done.103, f32[512]{0:T(512)S(1)} %copy-done.105, bf16[768,512]{1,0:T(8,128)(2,1)S(1)} %copy-done.1, f32[768,1024]{1,0:T(8,128)} %fusion.20, f32[768,1024]{1,0:T(8,128)} %copy-done.2, f32[768,1024]{1,0:T(8,128)} %copy-done.25, ...), kind=kLoop, calls=%fused_computation.285 | loop fusion | flops 13761536 | bytes 29118464 | tf_op jit(solution)/shard_map/reduce_sum | solution.py:151
  458.7 126.7 %all-reduce = bf16[256,10]{1,0:T(8,128)(2,1)S(1)} all-reduce(bf16[256,10]{1,0:T(8,128)(2,1)S(1)} %convolution_convert_fusion.13), channel_id=15, replica_groups=mesh['dp'=4,'fsdp'=32] {'fsdp'}, use_global_device_ids=true, to_apply=%region_26.0.clone | all-reduce | flops 2560 | bytes 10240
  590.8 60.3 %reduce-scatter.26.cloned.1.call-done = bf16[32,1536]{1,0:T(8,128)(2,1)} async-done(((bf16[1024,1536]{1,0:T(8,128)(2,1)}), bf16[32,1536]{1,0:T(8,128)(2,1)}) %reduce-scatter.26.cloned.1.call-update) | async-done | bytes 98320
  653.0 81.6 %reduce-scatter.24.cloned.1.call-done = bf16[32,1536]{1,0:T(8,128)(2,1)} async-done(((bf16[1024,1536]{1,0:T(8,128)(2,1)}), bf16[32,1536]{1,0:T(8,128)(2,1)}) %reduce-scatter.24.cloned.1.call-update) | async-done | bytes 98320
  736.4 81.9 %reduce-scatter.22.cloned.1.call-done = bf16[32,1536]{1,0:T(8,128)(2,1)} async-done(((bf16[1024,1536]{1,0:T(8,128)(2,1)}), bf16[32,1536]{1,0:T(8,128)(2,1)}) %reduce-scatter.22.cloned.1.call-update) | async-done | bytes 98320
  820.2 64.8 %all-reduce.1 = (f32[512]{0:T(512)S(1)}, f32[512]{0:T(512)S(1)}, f32[256]{0:T(256)}, f32[10]{0:T(128)}) all-reduce(f32[512]{0:T(512)S(1)} %get-tuple-element.17, f32[512]{0:T(512)S(1)} %get-tuple-element.16, f32[256]{0:T(256)S(1)} %copy-done.128, f32[10]{0:T(128)S(1)} %copy-done.125), channel_id=1, replica_groups=mesh['dp'=4,'fsdp'=32] {'dp','fsdp'}, use_global_device_ids=true, to_apply=%region_9.0 | all-reduce | flops 1290 | bytes 10320 | tf_op jit(solution)/shard_map/psum | solution.py:149
  886.6 11.5 %reduce-scatter.20.cloned.1.call-done = bf16[16,256]{1,0:T(8,128)(2,1)} async-done(((bf16[512,256]{1,0:T(8,128)(2,1)}), bf16[16,256]{1,0:T(8,128)(2,1)}) %reduce-scatter.20.cloned.1.call-update) | async-done | bytes 8208 | tf_op jit(solution)/shard_map/reduce_scatter | solution.py:95
  898.1 17.6 %all-reduce.3 = (f32[16,256]{1,0:T(8,128)}, f32[8,10]{1,0:T(8,128)}) all-reduce(bf16[16,256]{1,0:T(8,128)(2,1)} %reduce-scatter.20.cloned.1.call-done, f32[8,10]{1,0:T(8,128)S(1)} %dynamic-slice_convert_fusion), channel_id=1, replica_groups=mesh['dp'=4,'fsdp'=32] {'dp'}, use_global_device_ids=true, to_apply=%region_23.0 | all-reduce | flops 4176 | bytes 25216 | tf_op jit(solution)/shard_map/psum | solution.py:102
  915.7 48.7 %all-reduce.7.cloned.1.call-done = (bf16[1,32,1536]{1,2,0:T(8,128)(2,1)}, bf16[1,32,1536]{1,2,0:T(8,128)(2,1)}, bf16[1,32,1536]{1,2,0:T(8,128)(2,1)}, bf16[1,32,...) async-done(((bf16[1,32,1536]{1,2,0:T(8,128)(2,1)}, bf16[1,32,1536]{1,2,0:T(8,128)(2,1)}, bf16[1,32,1536]{1,2,0:T(8,128)(2,1)}, ...) | async-done | bytes 589840 | tf_op jit(solution)/shard_map/psum | solution.py:144
  (388 shorter events, 111.8 us)
Async XLA Ops:
  7.2 5.4 copy-start
  7.2 5.7 copy-start.120
  7.2 5.7 copy-start.126
  7.2 33.7 %copy-start.122 = (bf16[16,256]{1,0:T(8,128)(2,1)S(1)}, bf16[16,256]{1,0:T(8,128)(2,1)}, u32[]{:S(2)}) copy-start(bf16[16,256]{1,0:T(8,128)(2,1)} %param.15) | copy-start | bytes 24580
  7.2 125.3 %copy-start.108 = (f32[512]{0:T(512)S(1)}, f32[512]{0:T(512)}, u32[]{:S(2)}) copy-start(f32[512]{0:T(512)} %param.11) | copy-start | bytes 6148
  7.2 125.9 %copy-start.110 = (f32[512]{0:T(512)S(1)}, f32[512]{0:T(512)}, u32[]{:S(2)}) copy-start(f32[512]{0:T(512)} %param.12) | copy-start | bytes 6148
  7.2 126.4 %all-gather.13.cloned.1.call-start = ((), (), s32[]{:S(2)}) async-start(), calls=%async_computation.8 | async-start | bytes 3244032 | tf_op jit(solution)/shard_map/all_gather | solution.py:56
  9.3 136.7 %all-gather.15.cloned.1.call-start = ((), (), s32[]{:S(2)}) async-start(), calls=%async_computation.9 | async-start | bytes 3244032 | tf_op jit(solution)/shard_map/all_gather | solution.py:56
  10.1 146.7 %all-gather.17.cloned.1.call-start = ((), (), s32[]{:S(2)}) async-start(), calls=%async_computation.10 | async-start | bytes 3244032 | tf_op jit(solution)/shard_map/all_gather | solution.py:56
  10.8 188.2 %all-gather.19.cloned.1.call-start = ((), (), s32[]{:S(2)}) async-start(), calls=%async_computation.11 | async-start | bytes 3244032 | tf_op jit(solution)/shard_map/all_gather | solution.py:56
  11.4 234.2 %all-gather.21.cloned.1.call-start = ((), (), s32[]{:S(2)}) async-start(), calls=%async_computation.12 | async-start | bytes 3244032 | tf_op jit(solution)/shard_map/all_gather | solution.py:56
  11.9 280.3 %all-gather.23.cloned.1.call-start = ((), (), s32[]{:S(2)}) async-start(), calls=%async_computation.13 | async-start | bytes 3244032 | tf_op jit(solution)/shard_map/all_gather | solution.py:56
  12.5 572.8 %reduce-scatter.32.cloned.1.call-start = ((), (), s32[]{:S(2)}) async-start(), calls=%async_computation.19 | async-start | bytes 3244032
  12.9 124.6 %copy-start.112 = (f32[1,512]{1,0:T(1,128)}, f32[1,512]{1,0:T(1,128)S(1)}, u32[]{:S(2)}) copy-start(f32[1,512]{1,0:T(1,128)S(1)} %get-tuple-element.86) | copy-start | bytes 6148
  12.9 124.7 %copy-start.114 = (f32[1,512]{1,0:T(1,128)}, f32[1,512]{1,0:T(1,128)S(1)}, u32[]{:S(2)}) copy-start(f32[1,512]{1,0:T(1,128)S(1)} %get-tuple-element.81) | copy-start | bytes 6148
  12.9 124.7 %copy-start.116 = (f32[1,512]{1,0:T(1,128)}, f32[1,512]{1,0:T(1,128)S(1)}, u32[]{:S(2)}) copy-start(f32[1,512]{1,0:T(1,128)S(1)} %get-tuple-element.82) | copy-start | bytes 6148
  12.9 124.7 %copy-start.117 = (f32[1,512]{1,0:T(1,128)}, f32[1,512]{1,0:T(1,128)S(1)}, u32[]{:S(2)}) copy-start(f32[1,512]{1,0:T(1,128)S(1)} %get-tuple-element.83) | copy-start | bytes 6148
  12.9 124.7 %copy-start.118 = (f32[1,512]{1,0:T(1,128)}, f32[1,512]{1,0:T(1,128)S(1)}, u32[]{:S(2)}) copy-start(f32[1,512]{1,0:T(1,128)S(1)} %get-tuple-element.84) | copy-start | bytes 6148
  12.9 124.7 %copy-start.119 = (f32[1,512]{1,0:T(1,128)}, f32[1,512]{1,0:T(1,128)S(1)}, u32[]{:S(2)}) copy-start(f32[1,512]{1,0:T(1,128)S(1)} %get-tuple-element.85) | copy-start | bytes 6148
  133.2 7.3 copy-start.102
  133.2 7.3 copy-start.104
  133.6 6.9 copy-start.67
  150.0 253.7 %copy-start.4 = (f32[768,1024]{1,0:T(8,128)}, f32[768,1024]{1,0:T(8,128)S(1)}, u32[]{:S(2)}) copy-start(f32[768,1024]{1,0:T(8,128)S(1)} %fusion.18) | copy-start | bytes 9437188
  296.2 12.7 %copy-start.34 = (f32[768,1024]{1,0:T(8,128)}, f32[768,1024]{1,0:T(8,128)S(1)}, u32[]{:S(2)}) copy-start(f32[768,1024]{1,0:T(8,128)S(1)} %fusion.2) | copy-start | bytes 9437188
  320.1 267.0 %reduce-scatter.30.cloned.1.call-start = ((), (), s32[]{:S(2)}) async-start(), calls=%async_computation.18 | async-start | bytes 3244032
  320.2 5.7 copy-start.55
  320.2 6.8 copy-start.56
  328.5 5.2 copy-start.62
  344.2 244.8 %reduce-scatter.28.cloned.1.call-start = ((), (), s32[]{:S(2)}) async-start(), calls=%async_computation.17 | async-start | bytes 3244032
  344.5 6.6 copy-start.27
  344.5 7.2 copy-start.54
  353.2 5.2 copy-start.63
  368.8 282.3 %reduce-scatter.26.cloned.1.call-start = ((), (), s32[]{:S(2)}) async-start(), calls=%async_computation.16 | async-start | bytes 3244032
  369.2 6.1 copy-start.29
  369.2 7.0 copy-start.53
  393.3 341.3 %reduce-scatter.24.cloned.1.call-start = ((), (), s32[]{:S(2)}) async-start(), calls=%async_computation.15 | async-start | bytes 3244032
  412.6 405.8 %reduce-scatter.22.cloned.1.call-start = ((), (), s32[]{:S(2)}) async-start(), calls=%async_computation.14 | async-start | bytes 3244032
  413.9 6.2 copy-start.33
  413.9 6.7 copy-start.37
  437.4 460.7 %reduce-scatter.20.cloned.1.call-start = ((), (), s32[]{:S(2)}) async-start(), calls=%async_computation.7 | async-start | bytes 270336 | tf_op jit(solution)/shard_map/reduce_scatter | solution.py:95
  441.7 5.5 copy-start.113
  441.7 5.5 copy-start.115
  447.1 11.2 %copy-start.107 = (bf16[768,10]{0,1:T(8,128)(2,1)S(1)}, bf16[768,10]{0,1:T(8,128)(2,1)}, u32[]{:S(2)}) copy-start(bf16[768,10]{0,1:T(8,128)(2,1)} %copy-done.106) | copy-start | bytes 46084
  447.1 517.3 %all-reduce.7.cloned.1.call-start = ((), (), s32[]{:S(2)}) async-start(), calls=%async_computation.20 | async-start | bytes 4718592 | tf_op jit(solution)/shard_map/psum | solution.py:144
  653.0 167.2 %copy-start.125 = (f32[10]{0:T(128)S(1)}, f32[10]{0:T(128)}, u32[]{:S(2)}) copy-start(f32[10]{0:T(128)} %get-tuple-element.34) | copy-start | bytes 124
  653.0 167.2 %copy-start.128 = (f32[256]{0:T(256)S(1)}, f32[256]{0:T(256)}, u32[]{:S(2)}) copy-start(f32[256]{0:T(256)} %get-tuple-element.100) | copy-start | bytes 3076
  736.4 148.6 %copy-start.36 = (f32[768,512]{1,0:T(8,128)S(1)}, f32[768,512]{1,0:T(8,128)}, u32[]{:S(2)}) copy-start(f32[768,512]{1,0:T(8,128)} %get-tuple-element.36) | copy-start | bytes 4718596
  736.4 148.6 %copy-start.121 = (f32[512]{0:T(512)S(1)}, f32[512]{0:T(512)}, u32[]{:S(2)}) copy-start(f32[512]{0:T(512)} %get-tuple-element.87) | copy-start | bytes 6148
  (106 other events, 285.3 us)
Sparse Core Ops, SparseCore 0:
  10.9 47.7 all-gather.12
  61.0 44.7 all-gather.14
  108.0 44.3 all-gather.16
  154.5 44.4 all-gather.18
  201.1 44.4 all-gather.20
  247.7 44.4 all-gather.22
  320.2 79.8 reduce-scatter.31
  404.2 79.7 reduce-scatter.29
  487.6 79.7 reduce-scatter.27
  571.3 79.7 reduce-scatter.25
  654.8 79.7 reduce-scatter.23
  738.5 79.7 reduce-scatter.21
  821.8 76.2 reduce-scatter.19
  901.3 63.0 all-reduce.6
where the time goes:
time: 982 us; the launch traced here: 976 us
  waiting for transfers between devices  388 us (40%)
  blocking collectives  329 us (34%)
  matrix products  114 us (12%)
  local copies, waits for them, and re-layouts  82.6 us (8%)
  other arithmetic  45.6 us (5%)
  between operations  16.6 us (2%)
    unnamed x20, waiting for transfers between devices  227 us
    unnamed x1, blocking collectives  127 us
    all_gather x6, waiting for transfers between devices, on_device(): lax.all_gather(gate_weights[layer_index], 'fsdp', axis=0, tiled=True)  101 us
    unnamed x298, local copies, waits for them, and re-layouts  76.7 us
    psum x1, blocking collectives, on_device(): lax.psum((jnp.sum(inputs, 0), jnp.sum(inputs * inputs, 0)), ('dp', 'fsdp'))  65.7 us
    psum x1, blocking collectives, on_device(): lax.psum((jnp.sum(grad_scaled, 0), jnp.sum(grad_scaled * normed, 0), firs...  64.8 us
    psum x1, waiting for transfers between devices, on_device(): lax.psum(grad_shard.astype(jnp.bfloat16), 'dp').astype(jnp.float32)  48.7 us
    dot_general x14, matrix products, inner_cols(): lax.dot_general(left, right, (((1,), (1,)), ((), ())), preferred_element_...  41 us
  transfers between devices with their start and end apart: 14, of which 8 were waited for; matrix products, arithmetic and copies ran while one was open for 18% of the time, Pallas kernels for 0%

commit v1 on v0

v1 whole, which is shorter than its diff:
```python
import functools
import math

import jax
import jax.numpy as jnp
import numpy as np
from jax import lax
from jax.experimental import pallas as pl
from jax.experimental.pallas import tpu as pltpu
from jax.sharding import PartitionSpec as P

epsilon = 1e-05
F32 = jnp.float32
BF16 = jnp.bfloat16
VMEM_LIMIT = 60 * 1024 * 1024
GROUPS = ((5, 4, 3), (2, 1, 0))
HEAD_ROWS = 16
LANES = 128


def sigmoid(value):
    return 0.5 * jnp.tanh(0.5 * value) + 0.5


def dot(left, right):
    return jnp.dot(left, right, preferred_element_type=F32)


def dot_cols(left, right):
    return lax.dot_general(left, right, (((1,), (1,)), ((), ())), preferred_element_type=F32)


def erf(value):
    value = jnp.clip(value, -4.0, 4.0)
    square = value * value
    top = jnp.full_like(square, -2.72614225801306e-10)
    for term in (
        2.77068142495902e-08,
        -2.10102402082508e-06,
        -5.69250639462346e-05,
        -7.34990630326855e-04,
        -2.95459980854025e-03,
        -1.60960333262415e-02,
    ):
        top = top * square + term
    low = jnp.full_like(square, -1.45660718464996e-05)
    for term in (
        -2.13374055278905e-04,
        -1.68282697438203e-03,
        -7.37332916720468e-03,
        -1.42647390514189e-02,
    ):
        low = low * square + term
    return value * top / low


def normalise(total_rows, features, stats):
    mean = stats[0:1] / total_rows
    scale = lax.rsqrt(stats[1:2] / total_rows - mean * mean + epsilon)
    return (features.astype(F32) - mean) * scale, scale


def halves(rows):
    return [slice(0, rows // 2), slice(rows // 2, rows)]


def forward_kernel(
    total_rows, x_ref, stat_ref, gain_ref, bias_ref, mask_ref, w_ref,
    s_ref, u_ref, r_ref, o_ref, last_ref, turned_ref, low_ref, state_ref,
):
    n = pl.program_id(0)
    rows, width = x_ref.shape
    half = w_ref.shape[0] // 2

    @pl.when(n == 0)
    def _():
        for part in halves(rows):
            normed, _ = normalise(total_rows, x_ref[part], stat_ref[...])
            scaled = normed * gain_ref[...] + bias_ref[...]
            state_ref[part] = scaled
            low = scaled.astype(BF16)
            low_ref[part] = low
            turned_ref[:, part] = low.T

    mask = mask_ref[0].astype(BF16)

    def weight(lower, start):
        at = w_ref[0:half, :, start : start + width] if lower else w_ref[half:, :, start : start + width]
        return at.reshape(width, width)

    for part in halves(rows):
        state = state_ref[part]
        state_low = state.astype(BF16)
        masked = low_ref[part] * mask
        s_ref[0, part] = state
        reset = sigmoid(dot(state_low, weight(True, width)) + dot(masked, weight(False, width)))
        r_ref[0, part] = reset
        second = (reset * state).astype(BF16)
        update = sigmoid(dot(state_low, weight(True, 0)) + dot(masked, weight(False, 0)))
        u_ref[0, part] = update
        output = jnp.tanh(
            dot(second, weight(True, 2 * width)) + dot(masked, weight(False, 2 * width))
        )
        o_ref[0, part] = output
        state_ref[part] = state + update * (output - state)

    @pl.when(n == pl.num_programs(0) - 1)
    def _():
        last_ref[...] = state_ref[...]


def run_forward(features, stats, gain, bias, masks, weights, total_rows):
    rows, width = features.shape
    sections = masks.shape[0]
    owners = weights.shape[0]
    depth = 2 * width // owners
    whole = lambda n: (0, 0)
    saved = jax.ShapeDtypeStruct((sections, rows, width), F32)
    saved_spec = pl.BlockSpec((1, rows, width), lambda n: (n, 0, 0))
    return pl.pallas_call(
        functools.partial(forward_kernel, total_rows),
        grid=(sections,),
        in_specs=[
            pl.BlockSpec((rows, width), whole),
            pl.BlockSpec((2, width), whole),
            pl.BlockSpec((1, width), whole),
            pl.BlockSpec((1, width), whole),
            pl.BlockSpec((1, 1, width), lambda n: (n, 0, 0)),
            pl.BlockSpec((owners, depth, 3 * width), lambda n: (0, n, 0)),
        ],
        out_specs=[saved_spec] * 4
        + [pl.BlockSpec((rows, width), whole), pl.BlockSpec((width, rows), whole)],
        out_shape=[saved] * 4
        + [jax.ShapeDtypeStruct((rows, width), F32), jax.ShapeDtypeStruct((width, rows), BF16)],
        scratch_shapes=[pltpu.VMEM((rows, width), BF16), pltpu.VMEM((rows, width), F32)],
        compiler_params=pltpu.CompilerParams(vmem_limit_bytes=VMEM_LIMIT),
        name="sections_forward",
    )(features, stats, gain, bias, masks, weights)


def head_kernel(
    row_scale, classes, state_ref, w_ref, b1_ref, b2_ref, label_ref,
    grad_ref, share_ref, sum1_ref, sum2_ref,
):
    rows, width = state_ref.shape
    owners = w_ref.shape[0]
    hidden = b1_ref.shape[1]
    first = w_ref[:, :, 0:hidden].reshape(width, hidden)
    second = w_ref[:, :, hidden : hidden + LANES].astype(F32)[:, 0 : hidden // owners]
    second = second.reshape(hidden, LANES).astype(BF16)
    head_in = state_ref[...].astype(BF16)
    pre = dot(head_in, first) + b1_ref[...]
    phi = 0.5 + 0.5 * erf(pre * math.sqrt(0.5))
    activation = (pre * phi).astype(BF16)
    slope = phi + pre * (jnp.exp(-0.5 * pre * pre) * (1.0 / math.sqrt(2.0 * math.pi)))
    lane = lax.broadcasted_iota(jnp.int32, (rows, LANES), 1)
    logits = dot(activation, second) + b2_ref[...]
    logits = jnp.where(lane < classes, logits, -1e30)
    powers = jnp.exp(logits - jnp.max(logits, 1, keepdims=True))
    chance = powers / jnp.sum(powers, 1, keepdims=True)
    hit = jnp.where(lane == label_ref[...], 1.0, 0.0)
    grad_logits = ((chance - hit) * row_scale).astype(BF16)
    sum2_ref[...] = jnp.sum(grad_logits.astype(F32), 0, keepdims=True)
    grad_second = dot(activation.T, grad_logits)
    grad_pre = (dot_cols(grad_logits, second) * slope).astype(BF16)
    sum1_ref[...] = jnp.sum(grad_pre.astype(F32), 0, keepdims=True)
    grad_first = dot(head_in.T, grad_pre)
    grad_ref[...] = dot_cols(grad_pre, first)
    grad_second = grad_second.reshape(owners, hidden // owners, LANES)
    grad_second = jnp.concatenate([grad_second, jnp.zeros_like(grad_second)], 1)
    share_ref[:, :, 0:hidden] = grad_first.reshape(owners, HEAD_ROWS, hidden).astype(BF16)
    share_ref[:, :, hidden : hidden + LANES] = grad_second.astype(BF16)
    tail = share_ref.shape[2] - hidden - LANES
    share_ref[:, :, hidden + LANES :] = jnp.zeros((owners, HEAD_ROWS, tail), BF16)


def run_head(state, weights, block_at, b1, b2, labels, classes):
    rows, width = state.shape
    owners, _, columns = weights.shape
    hidden = b1.shape[1]
    taken = hidden + LANES
    whole = lambda i: (0, 0)
    return pl.pallas_call(
        functools.partial(head_kernel, 1.0 / rows, classes),
        grid=(1,),
        in_specs=[
            pl.BlockSpec((rows, width), whole),
            pl.BlockSpec((owners, HEAD_ROWS, taken), lambda i: (0, block_at, 0)),
            pl.BlockSpec((1, hidden), whole),
            pl.BlockSpec((1, LANES), whole),
            pl.BlockSpec((rows, 1), whole),
        ],
        out_specs=[
            pl.BlockSpec((rows, width), whole),
            pl.BlockSpec((owners, HEAD_ROWS, columns), lambda i: (0, 0, 0)),
            pl.BlockSpec((1, hidden), whole),
            pl.BlockSpec((1, LANES), whole),
        ],
        out_shape=[
            jax.ShapeDtypeStruct((rows, width), F32),
            jax.ShapeDtypeStruct((owners, HEAD_ROWS, columns), BF16),
            jax.ShapeDtypeStruct((1, hidden), F32),
            jax.ShapeDtypeStruct((1, LANES), F32),
        ],
        compiler_params=pltpu.CompilerParams(vmem_limit_bytes=VMEM_LIMIT),
        name="head",
    )(state, weights, b1, b2, labels)


def backward_kernel(
    total_rows, opening, closing, *refs
):
    refs = list(refs)
    s_ref, u_ref, r_ref, o_ref, w_ref, turned_ref, row_ref, column_ref, g_ref = refs[:9]
    refs = refs[9:]
    if opening:
        share_ref = refs.pop(0)
    else:
        gs_ref = refs.pop(0)
    if closing:
        x_ref, stat_ref = refs.pop(0), refs.pop(0)
    dw_ref, gout_ref, gsout_ref = refs.pop(0), refs.pop(0), refs.pop(0)
    if closing:
        sums_ref = refs.pop(0)
    made_ref, left_ref, grads_ref, dw_sem, share_sem = refs
    step = pl.program_id(0)
    steps = pl.num_programs(0)
    rows, width = g_ref.shape
    owners, depth = w_ref.shape[0], w_ref.shape[1]
    half = owners // 2

    def share_copy():
        return pltpu.make_async_copy(
            share_ref, dw_ref.at[:, pl.ds(dw_ref.shape[1] - HEAD_ROWS, HEAD_ROWS), :], share_sem
        )

    def dw_copy(at, slot):
        return pltpu.make_async_copy(
            made_ref.at[slot],
            dw_ref.at[:, pl.ds(pl.multiple_of(at * depth, depth), depth), :],
            dw_sem.at[slot],
        )

    slot = lax.rem(step, 2)

    @pl.when(step == 0)
    def _():
        if opening:
            share_copy().start()
            gsout_ref[...] = jnp.zeros_like(gsout_ref)
        else:
            gsout_ref[...] = gs_ref[...]
        gout_ref[...] = g_ref[...]

    def weight(lower, start, count):
        at = w_ref[0:half, :, start : start + count] if lower else w_ref[half:, :, start : start + count]
        return at.reshape(width, count)

    for part in halves(rows):
        grad = gout_ref[part]
        state, update, reset, output = s_ref[0, part], u_ref[0, part], r_ref[0, part], o_ref[0, part]
        left_ref[0, :, part] = state.astype(BF16).T
        left_ref[1, :, part] = (reset * state).astype(BF16).T
        grad_out = (grad * update * (1.0 - output * output)).astype(BF16)
        grads_ref[part, 2 * width :] = grad_out
        through = dot_cols(grad_out, weight(True, 2 * width, width))
        grad_update = (grad * (output - state) * update * (1.0 - update)).astype(BF16)
        grads_ref[part, 0:width] = grad_update
        grad_reset = (through * state * reset * (1.0 - reset)).astype(BF16)
        grads_ref[part, width : 2 * width] = grad_reset
        gout_ref[part] = (
            grad * (1.0 - update)
            + through * reset
            + dot_cols(grad_update, weight(True, 0, width))
            + dot_cols(grad_reset, weight(True, width, width))
        )
        gsout_ref[part] += row_ref[0] * (
            dot_cols(grad_update, weight(False, 0, width))
            + dot_cols(grad_reset, weight(False, width, width))
            + dot_cols(grad_out, weight(False, 2 * width, width))
        )

    @pl.when(step >= 2)
    def _():
        dw_copy(step - 2, slot).wait()

    for at in range(3):
        columns = slice(at * width, (at + 1) * width)
        made = dot(left_ref[at // 2], grads_ref[:, columns])
        made_ref[slot, 0:half, :, columns] = made.astype(BF16).reshape(half, depth, width)
        made = column_ref[0] * dot(turned_ref[...], grads_ref[:, columns])
        made_ref[slot, half:, :, columns] = made.astype(BF16).reshape(half, depth, width)
    dw_copy(step, slot).start()

    @pl.when(step == steps - 1)
    def _():
        dw_copy(step, slot).wait()

        @pl.when(steps > 1)
        def _():
            dw_copy(step - 1, 1 - slot).wait()

        if opening:
            share_copy().wait()
        if closing:
            total = gsout_ref[...] + gout_ref[...]
            gsout_ref[...] = total
            normed, _ = normalise(total_rows, x_ref[...], stat_ref[...])
            sums_ref[0:1] = jnp.sum(total, 0, keepdims=True)
            sums_ref[1:2] = jnp.sum(total * normed, 0, keepdims=True)


def run_backward(
    group, saved, weights, turned, masks, grad_state, grad_scaled, share, features, stats, total_rows
):
    opening, closing = share is not None, features is not None
    top, count = group[0], len(group)
    rows, width = grad_state.shape
    owners = weights.shape[0]
    depth = 2 * width // owners
    whole = lambda i: (0, 0)
    section = lambda i: (top - i, 0, 0)
    saved_spec = pl.BlockSpec((1, rows, width), section)
    tall_spec = pl.BlockSpec((rows, width), whole)
    in_specs = [saved_spec] * 4 + [
        pl.BlockSpec((owners, depth, 3 * width), lambda i: (0, top - i, 0)),
        pl.BlockSpec((width, rows), whole),
        pl.BlockSpec((1, 1, width), section),
        pl.BlockSpec((1, width, 1), section),
        tall_spec,
    ]
    operands = [*saved, weights, turned, masks, masks.reshape(-1, width, 1), grad_state]
    if opening:
        in_specs.append(pl.BlockSpec(share.shape, lambda i: (0, 0, 0)))
        operands.append(share)
    else:
        in_specs.append(tall_spec)
        operands.append(grad_scaled)
    if closing:
        in_specs += [tall_spec, pl.BlockSpec((2, width), whole)]
        operands += [features, stats]
    out_specs = [pl.BlockSpec(memory_space=pl.ANY), tall_spec, tall_spec]
    made_rows = count * depth + (HEAD_ROWS if opening else 0)
    out_shape = [
        jax.ShapeDtypeStruct((owners, made_rows, 3 * width), BF16),
        jax.ShapeDtypeStruct((rows, width), F32),
        jax.ShapeDtypeStruct((rows, width), F32),
    ]
    if closing:
        out_specs.append(pl.BlockSpec((2, width), whole))
        out_shape.append(jax.ShapeDtypeStruct((2, width), F32))
    return pl.pallas_call(
        functools.partial(backward_kernel, total_rows, opening, closing),
        grid=(count,),
        in_specs=in_specs,
        out_specs=out_specs,
        out_shape=out_shape,
        scratch_shapes=[
            pltpu.VMEM((2, owners, depth, 3 * width), BF16),
            pltpu.VMEM((2, width, rows), BF16),
            pltpu.VMEM((rows, 3 * width), BF16),
            pltpu.SemaphoreType.DMA((2,)),
            pltpu.SemaphoreType.DMA,
        ],
        compiler_params=pltpu.CompilerParams(vmem_limit_bytes=VMEM_LIMIT),
        name="sections_backward",
    )(*operands)


def pairs(sizes, axis, flip):
    table = []
    for source in range(math.prod(sizes)):
        place = list(np.unravel_index(source, sizes))
        place[axis] ^= flip
        table.append((source, int(np.ravel_multi_index(place, sizes))))
    return table


def everywhere_sum(value, sizes, names):
    for axis in reversed(range(len(sizes))):
        for flip in (1, 3) if sizes[axis] == 4 else (1,):
            value = value + lax.ppermute(value, names, pairs(sizes, axis, flip))
    return value


def on_device(
    sizes,
    features,
    bn_gain,
    bn_bias,
    gate_weights,
    feature_masks,
    head_first,
    head_first_bias,
    head_second,
    head_second_bias,
    labels,
):
    names = ("dp", "fsdp")
    rows, width = features.shape
    sections, depth, columns = gate_weights.shape
    hidden = head_first.shape[1]
    classes = head_second.shape[1]
    total_rows = rows * math.prod(sizes)
    gain, bias = bn_gain[None], bn_bias[None]
    masks = feature_masks.astype(F32)[:, None, :]
    b1 = head_first_bias[None]
    b2 = jnp.pad(head_second_bias, (0, LANES - classes))[None]

    inputs = features.astype(F32)
    stats = jnp.stack([jnp.sum(inputs, 0), jnp.sum(inputs * inputs, 0)])
    stats = everywhere_sum(stats.reshape(-1, LANES), sizes, names).reshape(2, width)

    extra = jnp.pad(head_first, ((0, 0), (0, columns - hidden))) + jnp.pad(
        head_second, ((0, HEAD_ROWS - head_second.shape[0]), (hidden, columns - hidden - classes))
    )
    shard = jnp.concatenate([gate_weights.reshape(sections * depth, columns), extra], 0)
    weights = lax.all_gather(shard, "fsdp", axis=0)

    *saved, state, turned = run_forward(features, stats, gain, bias, masks, weights, total_rows)
    grad_state, share, sum1, sum2 = run_head(
        state, weights, sections * depth // HEAD_ROWS, b1, b2, labels[:, None], classes
    )
    grad_scaled = None
    parts = []
    for group in GROUPS:
        opening, closing = group is GROUPS[0], group is GROUPS[-1]
        made, grad_state, grad_scaled, *sums = run_backward(
            group, saved, weights, turned, masks, grad_state, grad_scaled,
            share if opening else None, features if closing else None, stats, total_rows,
        )
        parts.append(lax.psum_scatter(made, "fsdp", scatter_dimension=0))
    mine = [None] * sections
    for group, part in zip(GROUPS, parts):
        for at, n in enumerate(group):
            mine[n] = part[at * depth : (at + 1) * depth]
    mine = jnp.concatenate(mine + [parts[0][-HEAD_ROWS:]], 0)
    for flip in (1, 3):
        other = lax.ppermute(mine, names, pairs(sizes, 0, flip))
        mine = mine.astype(F32) + other.astype(F32)
        if flip == 1:
            mine = mine.astype(BF16)
    gate_grad = mine[: sections * depth].reshape(sections, depth, columns)
    head_grad = mine[sections * depth :]
    head_first_grad = head_grad[:, :hidden]
    head_second_grad = head_grad[: head_second.shape[0], hidden : hidden + classes]

    small = jnp.concatenate([sums[0].reshape(-1), sum1[0], sum2[0]])
    small = jnp.pad(small, (0, -small.size % 1024)).reshape(-1, LANES)
    small = everywhere_sum(small, sizes, names).reshape(-1)
    sum_grad, sum_cross = small[:width], small[width : 2 * width]
    first_bias_grad = small[2 * width : 2 * width + hidden]
    second_bias_grad = small[2 * width + hidden : 2 * width + hidden + classes]
    normed, scale = normalise(total_rows, features, stats)
    features_grad = (
        scale * gain * (grad_scaled - sum_grad / total_rows - normed * (sum_cross / total_rows))
    )
    return (
        features_grad,
        sum_cross,
        sum_grad,
        gate_grad,
        head_first_grad,
        first_bias_grad,
        head_second_grad,
        second_bias_grad,
    )


def solution(mesh):
    placed = (
        P(("dp", "fsdp"), None),
        P(),
        P(),
        P(None, "fsdp", None),
        P(),
        P("fsdp", None),
        P(),
        P("fsdp", None),
        P(),
        P(("dp", "fsdp")),
    )
    sizes = (mesh.shape["dp"], 4, 4, mesh.shape["fsdp"] // 16)
    return jax.shard_map(
        functools.partial(on_device, sizes),
        mesh=mesh,
        in_specs=placed,
        out_specs=(
            P(("dp", "fsdp"), None),
            P(),
            P(),
            P(None, "fsdp", None),
            P("fsdp", None),
            P(),
            P("fsdp", None),
            P(),
        ),
        check_vma=False,
    )
```

time: 982 us -> 426 us (0.43)
  blocking collectives: 329 us -> 0 us
  matrix products: 114 us -> 0 us
  waiting for transfers between devices: 388 us -> 277 us
  Pallas kernels: 0 us -> 84.2 us
  local copies, waits for them, and re-layouts: 82.6 us -> 14.2 us
  other arithmetic: 45.6 us -> 5.47 us
  starting transfers between devices: 1.66 us -> 29.7 us
    unnamed x20 -> x3, waiting for transfers between devices: 227 us -> 0.67 us
    reduce_scatter x1 -> x2, waiting for transfers between devices: 11.5 us -> 192 us  [on_device(): parts.append(lax.psum_scatter(made, 'fsdp', scatter_dimension=0))]
    psum x3 -> x0, blocking collectives: 148 us -> none  [the longest x1 65.7 us: on_device(): lax.psum((jnp.sum(inputs, 0), jnp.sum(inputs * inputs, 0)), ('dp', 'fsdp'))]
    unnamed x1 -> x0, blocking collectives: 127 us -> none
    dot_general x42 -> x0, matrix products: 114 us -> none  [the longest x14 41 us: inner_cols(): lax.dot_general(left, right, (((1,), (1,)), ((), ())), preferred_element_...]
    pallas_call x0 -> x4, Pallas kernels: none -> 84.2 us  [the longest x2 52.7 us: run_backward(): pl.pallas_call(functools.partial(backward_kernel, total_rows, opening, cl...]
    unnamed x298 -> x27, local copies, waits for them, and re-layouts: 76.7 us -> 5.6 us
    all_gather x2 -> x0, blocking collectives: 53.9 us -> none  [the longest x1 28 us: on_device(): lax.all_gather(head_second, 'fsdp', axis=0, tiled=True)]
  transfers between devices with their start and end apart: 14 -> 19, of which waited for: 8 -> 16; matrix products, arithmetic and copies ran while one was open for 18% -> 3% of each run, Pallas kernels for 0% -> 0%
where the time goes in v1:
time: 426 us; the launch traced here: 425 us
  waiting for transfers between devices  277 us (65%)
  Pallas kernels  84.2 us (20%)
  starting transfers between devices  29.7 us (7%)
  local copies, waits for them, and re-layouts  14.2 us (3%)
  between operations  14 us (3%)
  other arithmetic  5.47 us (1%)
    reduce_scatter x2, waiting for transfers between devices, on_device(): parts.append(lax.psum_scatter(made, 'fsdp', scatter_dimension=0))  192 us
    all_gather x1, waiting for transfers between devices, on_device(): weights = lax.all_gather(shard, 'fsdp', axis=0)  54.5 us
    pallas_call x2, Pallas kernels, run_backward(): pl.pallas_call(functools.partial(backward_kernel, total_rows, opening, cl...  52.7 us
    ppermute x14, starting transfers between devices, everywhere_sum(): value = value + lax.ppermute(value, names, pairs(sizes, axis, flip))  26 us
    pallas_call x1, Pallas kernels, run_forward(): pl.pallas_call(functools.partial(forward_kernel, total_rows), grid=(secti...  25.9 us
    ppermute x14, waiting for transfers between devices, everywhere_sum(): value = value + lax.ppermute(value, names, pairs(sizes, axis, flip))  24.3 us
  transfers between devices with their start and end apart: 19, of which 16 were waited for; matrix products, arithmetic and copies ran while one was open for 3% of the time, Pallas kernels for 0%

profile of v1, /device:TPU:0, one launch (start us, length us, event | category | flops | bytes accessed | tf_op | source)
XLA Modules:
  0.0 425.0 jit_solution(9869684561767855338)
XLA Ops:
  7.3 0.8 pad_add_fusion
  8.0 1.9 pad_maximum_fusion
  10.4 1.2 collective-permute-done
  11.6 1.7 collective-permute-start.1
  13.2 1.9 collective-permute-done.1
  15.2 3.1 collective-permute-start.2
  18.3 1.7 collective-permute-done.2
  20.0 2.0 collective-permute-start.3
  22.0 1.6 collective-permute-done.3
  23.6 4.1 collective-permute-start.4
  27.8 1.6 collective-permute-done.4
  29.3 1.5 collective-permute-start.5
  30.8 2.1 collective-permute-done.5
  33.0 2.8 collective-permute-start.6
  36.2 0.6 broadcast_in_dim.22.mask_ref.refs_6_
  36.8 0.9 broadcast_in_dim.26.label_ref
  37.7 1.8 copy.23.refs_7_
  40.2 54.5 %all-gather.3.cloned.1.call-done = bf16[6656,1536]{1,0:T(8,128)(2,1)} async-done(((bf16[208,1536]{1,0:T(8,128)(2,1)}), bf16[6656,1536]{1,0:T(8,128)(2,1)}) %all-gather.3.cloned.1.call-update) | async-done | bytes 20447248 | tf_op jit(solution)/shard_map/all_gather | solution.py:418
  94.6 25.9 %sections_forward.1 = (f32[6,768,512]{2,1,0:T(8,128)}, f32[6,768,512]{2,1,0:T(8,128)}, f32[6,768,512]{2,1,0:T(8,128)}, f32[6,768,512]{2,1,0:T(8,128)}, f32[768,512]{1,0:T(8,128)}, /*index=5*/bf16[512,768]{1,0:T(8,128)(2,1)}) custom-call(bf16[768,512]{1,0:T(8,128)(2,1)} %refs_10_.1, f32[2,512]{1,0:T(2,128)} %reshape.91.stat_ref.refs_11_, f32[1,512]{1,0:T(1,128)} %bitcast.84, ...), custom_call_target="tpu_custom_call" | custom-call | tf_op jit(solution)/shard_map/sections_forward/pallas_call | solution.py:120
  120.6 5.6 %head.1 = (f32[768,512]{1,0:T(8,128)}, bf16[32,16,1536]{2,1,0:T(8,128)(2,1)}, f32[1,256]{1,0:T(1,128)}, f32[1,128]{1,0:T(1,128)}) custom-call(f32[768,512]{1,0:T(8,128)} %get-tuple-element.29.state_ref, bf16[32,208,1536]{2,1,0:T(8,128)(2,1)} %bitcast.72, f32[1,256]{1,0:T(1,128)} %bitcast.92, f32[1,128]{1,0:T(1,128)} %pad_bitcast_fusion.b2_ref, ...), custom_call_target="tpu_custom_call" | custom-call | tf_op jit(solution)/shard_map/head/pallas_call | solution.py:183
  126.1 25.9 %sections_backward.2 = (bf16[32,112,1536]{2,1,0:T(8,128)(2,1)}, f32[768,512]{1,0:T(8,128)}, f32[768,512]{1,0:T(8,128)}) custom-call(f32[6,768,512]{2,1,0:T(8,128)} %get-tuple-element.24.refs_0_, f32[6,768,512]{2,1,0:T(8,128)} %get-tuple-element.25.refs_1_, f32[6,768,512]{2,1,0:T(8,128)} %get-tuple-element.26.refs_2_, ...), custom_call_target="tpu_custom_call" | custom-call | tf_op jit(solution)/shard_map/sections_backward/pallas_call | solution.py:352
  152.0 26.8 %sections_backward.3 = (bf16[32,96,1536]{2,1,0:T(8,128)(2,1)}, f32[768,512]{1,0:T(8,128)}, f32[768,512]{1,0:T(8,128)}, f32[2,512]{1,0:T(2,128)}) custom-call(f32[6,768,512]{2,1,0:T(8,128)} %get-tuple-element.24.refs_0_, f32[6,768,512]{2,1,0:T(8,128)} %get-tuple-element.25.refs_1_, f32[6,768,512]{2,1,0:T(8,128)} %get-tuple-element.26.refs_2_, ...), custom_call_target="tpu_custom_call" | custom-call | tf_op jit(solution)/shard_map/sections_backward/pallas_call | solution.py:352
  179.0 0.6 reduce-scatter.5.cloned.1.call-update
  180.0 0.9 collective-permute-done.7
  180.9 1.6 collective-permute-start.8
  182.5 91.5 %reduce-scatter.3.cloned.1.call-done = bf16[1,96,1536]{2,1,0:T(8,128)(2,1)} async-done(((bf16[32,96,1536]{2,1,0:T(8,128)(2,1)}), bf16[1,96,1536]{2,1,0:T(8,128)(2,1)}) %reduce-scatter.3.cloned.1.call-update) | async-done | bytes 294928 | tf_op jit(solution)/shard_map/reduce_scatter | solution.py:432
  274.0 0.9 fusion.10
  274.9 1.1 fusion.9
  275.9 0.9 fusion.8
  276.8 100.2 %reduce-scatter.5.cloned.1.call-done = bf16[1,112,1536]{2,1,0:T(8,128)(2,1)} async-done(((bf16[32,112,1536]{2,1,0:T(8,128)(2,1)}), bf16[1,112,1536]{2,1,0:T(8,128)(2,1)}) %reduce-scatter.5.cloned.1.call-update) | async-done | bytes 344080 | tf_op jit(solution)/shard_map/reduce_scatter | solution.py:432
  377.1 0.9 fusion.7
  378.0 0.9 fusion.6
  378.9 0.9 fusion.5
  379.8 0.8 fusion.11
  380.6 1.5 collective-permute-start.14
  382.0 2.5 collective-permute-start.9
  384.6 2.4 collective-permute-done.9
  387.0 1.2 collective-permute-start.10
  388.2 2.4 collective-permute-done.10
  390.6 2.5 collective-permute-start.11
  393.1 2.4 collective-permute-done.11
  396.1 3.1 collective-permute-done.12
  399.2 2.1 collective-permute-start.13
  401.2 2.9 collective-permute-done.13
  404.3 2.1 collective-permute-start.15
  408.2 1.5 fusion.4
  409.7 6.4 %collective-permute-done.15 = bf16[208,1536]{1,0:T(8,128)(2,1)S(1)} collective-permute-done((bf16[208,1536]{1,0:T(8,128)(2,1)S(1)}, bf16[208,1536]{1,0:T(8,128)(2,1)S(1)}, u32[]{:S(2)}, u32[]{:S(2)}) %collective-permute-start.15) | collective-permute-done | bytes 639008 | tf_op jit(solution)/shard_map/ppermute | solution.py:439
  416.2 1.1 slice.118
  (62 shorter events, 5.8 us)
Async XLA Ops:
  7.2 2.9 copy-start
  7.2 23.7 %copy-start.3 = (s32[6,512]{1,0:T(8,128)S(1)}, s32[6,512]{1,0:T(8,128)}, u32[]{:S(2)}) copy-start(s32[6,512]{1,0:T(8,128)} %param.14) | copy-start | bytes 36868
  7.2 28.5 %copy-start.9 = (f32[10]{0:T(128)S(1)}, f32[10]{0:T(128)}, u32[]{:S(2)}) copy-start(f32[10]{0:T(128)} %param.18) | copy-start | bytes 124
  7.2 29.6 %copy-start.7 = (s32[768]{0:T(1024)S(1)}, s32[768]{0:T(1024)}, u32[]{:S(2)}) copy-start(s32[768]{0:T(1024)} %param.19) | copy-start | bytes 9220
  7.2 87.4 %all-gather.3.cloned.1.call-start = ((), (), s32[]{:S(2)}) async-start(), calls=%async_computation.4 | async-start | bytes 21086208 | tf_op jit(solution)/shard_map/all_gather | solution.py:418
  10.0 264.0 %reduce-scatter.3.cloned.1.call-start = ((), (), s32[]{:S(2)}) async-start(), calls=%async_computation.2 | async-start | bytes 9732096 | tf_op jit(solution)/shard_map/reduce_scatter | solution.py:432
  10.3 1.2 collective-permute-start
  11.6 3.6 collective-permute-start.1
  15.2 4.8 %collective-permute-start.2 = (f32[8,128]{1,0:T(8,128)S(1)}, f32[8,128]{1,0:T(8,128)S(1)}, u32[]{:S(2)}, u32[]{:S(2)}) collective-permute-start(f32[8,128]{1,0:T(8,128)S(1)} %add.75), channel_id=1, source_target_pairs={{0,6},{1,7},{2,4},{3,5},{4,2},{5,3},{6,0},{7,1},{8,14},{9,15},{10,... | collective-permute-start | bytes 12296 | tf_op jit(solution)/shard_map/ppermute | solution.py:382
  20.0 3.6 collective-permute-start.3
  23.6 5.7 %collective-permute-start.4 = (f32[8,128]{1,0:T(8,128)S(1)}, f32[8,128]{1,0:T(8,128)S(1)}, u32[]{:S(2)}, u32[]{:S(2)}) collective-permute-start(f32[8,128]{1,0:T(8,128)S(1)} %add.77), channel_id=1, source_target_pairs={{0,24},{1,25},{2,26},{3,27},{4,28},{5,29},{6,30},{7,31},{8,16},{9,... | collective-permute-start | bytes 12296 | tf_op jit(solution)/shard_map/ppermute | solution.py:382
  29.3 3.6 collective-permute-start.5
  33.0 6.6 %collective-permute-start.6 = (f32[8,128]{1,0:T(8,128)S(1)}, f32[8,128]{1,0:T(8,128)S(1)}, u32[]{:S(2)}, u32[]{:S(2)}) collective-permute-start(f32[8,128]{1,0:T(8,128)S(1)} %add.79), channel_id=1, source_target_pairs={{0,96},{1,97},{2,98},{3,99},{4,100},{5,101},{6,102},{7,103},{8,104... | collective-permute-start | bytes 12296 | tf_op jit(solution)/shard_map/ppermute | solution.py:382
  178.9 198.2 %reduce-scatter.5.cloned.1.call-start = ((), (), s32[]{:S(2)}) async-start(), calls=%async_computation.3 | async-start | bytes 11354112 | tf_op jit(solution)/shard_map/reduce_scatter | solution.py:432
  178.9 0.7 copy-start.8
  178.9 0.7 copy-start.4
  179.0 0.7 copy-start.6
  179.0 217.1 %copy-start.5 = (f32[512]{0:T(512)S(1)}, f32[512]{0:T(512)}, u32[]{:S(2)}) copy-start(f32[512]{0:T(512)} %param.11) | copy-start | bytes 6148
  179.7 1.3 collective-permute-start.7
  180.9 201.1 %collective-permute-start.8 = (f32[16,128]{1,0:T(8,128)S(1)}, f32[16,128]{1,0:T(8,128)S(1)}, u32[]{:S(2)}, u32[]{:S(2)}) collective-permute-start(f32[16,128]{1,0:T(8,128)S(1)} %fusion.15), channel_id=1, source_target_pairs={{0,2},{1,3},{2,0},{3,1},{4,6},{5,7},{6,4},{7,5},{8,10},{9,11},{10,... | collective-permute-start | bytes 24584 | tf_op jit(solution)/shard_map/ppermute | solution.py:382
  274.9 133.3 %copy-start.1 = (bf16[768,512]{1,0:T(8,128)(2,1)S(1)}, bf16[768,512]{1,0:T(8,128)(2,1)}, u32[]{:S(2)}) copy-start(bf16[768,512]{1,0:T(8,128)(2,1)} %refs_10_.1) | copy-start | bytes 2359300
  274.9 133.3 %copy-start.2 = (f32[768,512]{1,0:T(8,128)S(1)}, f32[768,512]{1,0:T(8,128)}, u32[]{:S(2)}) copy-start(f32[768,512]{1,0:T(8,128)} %get-tuple-element.34) | copy-start | bytes 4718596
  380.6 23.6 %collective-permute-start.14 = (bf16[208,1536]{1,0:T(8,128)(2,1)S(1)}, bf16[208,1536]{1,0:T(8,128)(2,1)S(1)}, u32[]{:S(2)}, u32[]{:S(2)}) collective-permute-start(bf16[208,1536]{1,0:T(8,128)(2,1)S(1)} %fusion.11), channel_id=1, source_target_pairs={{0,32},{1,33},{2,34},{3,35},{4,36},{5,37},{6,38},{7,39},{8,40},{9,... | collective-permute-start | bytes 1916936 | tf_op jit(solution)/shard_map/ppermute | solution.py:439
  382.0 4.9 %collective-permute-start.9 = (f32[16,128]{1,0:T(8,128)S(1)}, f32[16,128]{1,0:T(8,128)S(1)}, u32[]{:S(2)}, u32[]{:S(2)}) collective-permute-start(f32[16,128]{1,0:T(8,128)S(1)} %fusion.18), channel_id=1, source_target_pairs={{0,6},{1,7},{2,4},{3,5},{4,2},{5,3},{6,0},{7,1},{8,14},{9,15},{10,... | collective-permute-start | bytes 24584 | tf_op jit(solution)/shard_map/ppermute | solution.py:382
  387.0 3.7 collective-permute-start.10
  390.6 4.9 %collective-permute-start.11 = (f32[16,128]{1,0:T(8,128)S(1)}, f32[16,128]{1,0:T(8,128)S(1)}, u32[]{:S(2)}, u32[]{:S(2)}) collective-permute-start(f32[16,128]{1,0:T(8,128)S(1)} %add.87), channel_id=1, source_target_pairs={{0,24},{1,25},{2,26},{3,27},{4,28},{5,29},{6,30},{7,31},{8,16},{9,... | collective-permute-start | bytes 24584 | tf_op jit(solution)/shard_map/ppermute | solution.py:382
  395.5 3.7 collective-permute-start.12
  399.2 5.0 %collective-permute-start.13 = (f32[16,128]{1,0:T(8,128)S(1)}, f32[16,128]{1,0:T(8,128)S(1)}, u32[]{:S(2)}, u32[]{:S(2)}) collective-permute-start(f32[16,128]{1,0:T(8,128)S(1)} %add.89), channel_id=1, source_target_pairs={{0,96},{1,97},{2,98},{3,99},{4,100},{5,101},{6,102},{7,103},{8,104... | collective-permute-start | bytes 24584 | tf_op jit(solution)/shard_map/ppermute | solution.py:382
  404.3 11.7 %collective-permute-start.15 = (bf16[208,1536]{1,0:T(8,128)(2,1)S(1)}, bf16[208,1536]{1,0:T(8,128)(2,1)S(1)}, u32[]{:S(2)}, u32[]{:S(2)}) collective-permute-start(bf16[208,1536]{1,0:T(8,128)(2,1)S(1)} %add_convert_fusion), channel_id=1, source_target_pairs={{0,96},{1,97},{2,98},{3,99},{4,100},{5,101},{6,102},{7,103},{8,104... | collective-permute-start | bytes 1916936 | tf_op jit(solution)/shard_map/ppermute | solution.py:439
Sparse Core Ops, SparseCore 0:
  10.9 83.6 all-gather.2
  179.0 94.9 reduce-scatter.2
  278.3 98.7 reduce-scatter.4

commit v2 on v1

v2 whole, which is shorter than its diff:
```python
import functools
import math

import jax
import jax.numpy as jnp
import numpy as np
from jax import lax
from jax.experimental import pallas as pl
from jax.experimental.pallas import tpu as pltpu
from jax.sharding import PartitionSpec as P

epsilon = 1e-05
F32 = jnp.float32
BF16 = jnp.bfloat16
VMEM_LIMIT = 60 * 1024 * 1024
HEAD_ROWS = 16
OPENING = 3
COLUMN = 2
LANES = 128


def sigmoid(value):
    return 0.5 * jnp.tanh(0.5 * value) + 0.5


def dot(left, right):
    return jnp.dot(left, right, preferred_element_type=F32)


def dot_cols(left, right):
    return lax.dot_general(left, right, (((1,), (1,)), ((), ())), preferred_element_type=F32)


def erf(value):
    value = jnp.clip(value, -4.0, 4.0)
    square = value * value
    top = jnp.full_like(square, -2.72614225801306e-10)
    for term in (
        2.77068142495902e-08,
        -2.10102402082508e-06,
        -5.69250639462346e-05,
        -7.34990630326855e-04,
        -2.95459980854025e-03,
        -1.60960333262415e-02,
    ):
        top = top * square + term
    low = jnp.full_like(square, -1.45660718464996e-05)
    for term in (
        -2.13374055278905e-04,
        -1.68282697438203e-03,
        -7.37332916720468e-03,
        -1.42647390514189e-02,
    ):
        low = low * square + term
    return value * top / low


def normalise(total_rows, features, stats):
    mean = stats[0:1] / total_rows
    scale = lax.rsqrt(stats[1:2] / total_rows - mean * mean + epsilon)
    return (features.astype(F32) - mean) * scale, scale


def halves(rows):
    return [slice(0, rows // 2), slice(rows // 2, rows)]


def section_weight(w_ref, slot, width):
    half = w_ref.shape[1] // 2

    def weight(lower, start):
        place = slice(0, half) if lower else slice(half, 2 * half)
        return w_ref[slot, place, :, :, start : start + width].reshape(width, width)

    return weight


def forward_section(mask, weight, slot, wide_ref, held_ref, state_ref, low_ref):
    rows, width = state_ref.shape
    mask = mask.astype(BF16)
    for part in halves(rows):
        state = state_ref[part]
        state_low = state.astype(BF16)
        masked = low_ref[part] * mask
        wide_ref[slot, part] = state
        reset = sigmoid(dot(state_low, weight(True, width)) + dot(masked, weight(False, width)))
        held_ref[slot, 1, part] = reset.astype(BF16)
        second = (reset * state).astype(BF16)
        update = sigmoid(dot(state_low, weight(True, 0)) + dot(masked, weight(False, 0)))
        held_ref[slot, 0, part] = update.astype(BF16)
        output = jnp.tanh(
            dot(second, weight(True, 2 * width)) + dot(masked, weight(False, 2 * width))
        )
        held_ref[slot, 2, part] = output.astype(BF16)
        state_ref[part] = state + update * (output - state)


def backward_rows(mask, weight, slot, wide_ref, held_ref, left_ref, grads_ref, grad_ref, scaled_ref):
    rows, width = grad_ref.shape
    for part in halves(rows):
        grad = grad_ref[part]
        state = wide_ref[slot, part]
        update, reset, output = [held_ref[slot, which, part].astype(F32) for which in range(3)]
        left_ref[0, :, part] = state.astype(BF16).T
        left_ref[1, :, part] = (reset * state).astype(BF16).T
        grad_output = (grad * update * (1.0 - output * output)).astype(BF16)
        grads_ref[part, 2 * width :] = grad_output
        grad_update = (grad * (output - state) * update * (1.0 - update)).astype(BF16)
        grads_ref[part, 0:width] = grad_update
        through = dot_cols(grad_output, weight(True, 2 * width))
        grad_reset = (through * state * reset * (1.0 - reset)).astype(BF16)
        grads_ref[part, width : 2 * width] = grad_reset
        grad_ref[part] = (
            grad * (1.0 - update)
            + through * reset
            + dot_cols(grad_update, weight(True, 0))
            + dot_cols(grad_reset, weight(True, width))
        )
        scaled_ref[part] += mask * (
            dot_cols(grad_update, weight(False, 0))
            + dot_cols(grad_reset, weight(False, width))
            + dot_cols(grad_output, weight(False, 2 * width))
        )


def backward_weights(mask, slot, left_ref, grads_ref, turned_ref, made_ref):
    width = turned_ref.shape[0]
    blocks, depth = made_ref.shape[1], made_ref.shape[3]
    column = jnp.broadcast_to(mask, (8, width)).T[:, 0:1]

    def put(place, columns, value):
        value = value.astype(BF16).reshape(blocks // 2, 2, depth, width)
        made_ref[slot, place, :, :, columns] = value

    for gate in range(3):
        columns = slice(gate * width, (gate + 1) * width)
        put(slice(0, blocks // 2), columns, dot(left_ref[gate // 2], grads_ref[:, columns]))
        put(
            slice(blocks // 2, blocks),
            columns,
            column * dot(turned_ref[...], grads_ref[:, columns]),
        )


def head_rows(
    row_scale, classes, state_ref, head_ref, b1_ref, b2_ref, label_ref,
    grad_ref, share_ref, sum1_ref, sum2_ref,
):
    rows, width = state_ref.shape
    blocks = head_ref.shape[0]
    owners = 2 * blocks
    hidden = b1_ref.shape[1]
    first = head_ref[:, :, :, 0:hidden].reshape(width, hidden)
    second = head_ref[:, :, :, hidden : hidden + LANES].astype(F32)[:, :, 0 : hidden // owners]
    second = second.reshape(hidden, LANES).astype(BF16)
    head_in = state_ref[...].astype(BF16)
    pre = dot(head_in, first) + b1_ref[...]
    phi = 0.5 + 0.5 * erf(pre * math.sqrt(0.5))
    activation = (pre * phi).astype(BF16)
    slope = phi + pre * (jnp.exp(-0.5 * pre * pre) * (1.0 / math.sqrt(2.0 * math.pi)))
    lane = lax.broadcasted_iota(jnp.int32, (rows, LANES), 1)
    logits = dot(activation, second) + b2_ref[...]
    logits = jnp.where(lane < classes, logits, -1e30)
    powers = jnp.exp(logits - jnp.max(logits, 1, keepdims=True))
    chance = powers / jnp.sum(powers, 1, keepdims=True)
    hit = jnp.where(lane == label_ref[...], 1.0, 0.0)
    grad_logits = ((chance - hit) * row_scale).astype(BF16)
    sum2_ref[...] = jnp.sum(grad_logits.astype(F32), 0, keepdims=True)
    grad_second = dot(activation.T, grad_logits)
    grad_pre = (dot_cols(grad_logits, second) * slope).astype(BF16)
    sum1_ref[...] = jnp.sum(grad_pre.astype(F32), 0, keepdims=True)
    grad_first = dot(head_in.T, grad_pre)
    grad_ref[...] = dot_cols(grad_pre, first)
    grad_second = grad_second.reshape(blocks, 2, hidden // owners, LANES)
    grad_second = jnp.concatenate([grad_second, jnp.zeros_like(grad_second)], 2)
    share_ref[:, :, :, 0:hidden] = grad_first.reshape(blocks, 2, HEAD_ROWS, hidden).astype(BF16)
    share_ref[:, :, :, hidden : hidden + LANES] = grad_second.astype(BF16)
    tail = share_ref.shape[3] - hidden - LANES
    share_ref[:, :, :, hidden + LANES :] = jnp.zeros((blocks, 2, HEAD_ROWS, tail), BF16)


def upper_kernel(
    total_rows, classes,
    x_ref, stat_ref, gain_ref, bias_ref, mask_ref, b1_ref, b2_ref, label_ref, weights,
    s_out, u_out, r_out, o_out, turned_out, grad_out, scaled_out, made_out, sum1_ref, sum2_ref,
    wide_ref, held_ref, w_ref, head_ref, low_ref, turned_ref, state_ref, scaled_ref,
    share_ref, made_ref, left_ref, grads_ref, w_sem, save_sem, made_sem, out_sem,
):
    rows, width = x_ref.shape
    sections = mask_ref.shape[0]
    depth = w_ref.shape[3]
    stored = sections - OPENING

    def slot_of(n):
        return jnp.where(n < stored, lax.rem(n, 2), n - stored + 2)

    def w_copy(n):
        rows_at = pl.ds(pl.multiple_of(n * depth, depth), depth)
        slot = slot_of(n)
        return pltpu.make_async_copy(weights.at[:, :, rows_at, :], w_ref.at[slot], w_sem.at[slot])

    head_copy = pltpu.make_async_copy(
        weights.at[:, :, pl.ds(sections * depth, HEAD_ROWS), pl.ds(0, head_ref.shape[3])],
        head_ref,
        out_sem.at[0],
    )

    def save_copies(n, slot):
        return [pltpu.make_async_copy(wide_ref.at[slot], s_out.at[n], save_sem.at[slot, 0])] + [
            pltpu.make_async_copy(held_ref.at[slot, at], out.at[n], save_sem.at[slot, at + 1])
            for at, out in enumerate((u_out, r_out, o_out))
        ]

    def made_copy(at):
        rows_at = pl.ds(pl.multiple_of(at * depth, depth), depth)
        slot = lax.rem(at, 2)
        return pltpu.make_async_copy(
            made_ref.at[slot], made_out.at[:, :, rows_at, :], made_sem.at[slot]
        )

    share_copy = pltpu.make_async_copy(
        share_ref, made_out.at[:, :, pl.ds(OPENING * depth, HEAD_ROWS), :], out_sem.at[1]
    )
    turned_copy = pltpu.make_async_copy(turned_ref, turned_out, out_sem.at[2])
    last_copies = [
        pltpu.make_async_copy(state_ref, grad_out, out_sem.at[3]),
        pltpu.make_async_copy(scaled_ref, scaled_out, out_sem.at[4]),
    ]

    w_copy(0).start()
    w_copy(1).start()
    head_copy.start()
    for part in halves(rows):
        normed, _ = normalise(total_rows, x_ref[part], stat_ref[...])
        scaled = normed * gain_ref[...] + bias_ref[...]
        state_ref[part] = scaled
        low = scaled.astype(BF16)
        low_ref[part] = low
        turned_ref[:, part] = low.T
    turned_copy.start()

    def forward(n, carry):
        slot = slot_of(n)
        w_copy(n).wait()

        @pl.when((n >= 1) & (n + 1 < sections))
        def _():
            w_copy(n + 1).start()

        @pl.when((n >= 2) & (n < stored))
        def _():
            for copy in save_copies(n - 2, slot):
                copy.wait()

        forward_section(
            mask_ref[n], section_weight(w_ref, slot, width), slot,
            wide_ref, held_ref, state_ref, low_ref,
        )

        @pl.when(n < stored)
        def _():
            for copy in save_copies(n, slot):
                copy.start()

        return carry

    lax.fori_loop(0, sections, forward, 0)
    head_copy.wait()
    head_rows(
        1.0 / rows, classes, state_ref, head_ref, b1_ref, b2_ref, label_ref,
        state_ref, share_ref, sum1_ref, sum2_ref,
    )
    share_copy.start()
    scaled_ref[...] = jnp.zeros_like(scaled_ref)

    def backward(at, carry):
        n = sections - 1 - at
        slot = slot_of(n)
        backward_rows(
            mask_ref[n], section_weight(w_ref, slot, width), slot,
            wide_ref, held_ref, left_ref, grads_ref, state_ref, scaled_ref,
        )

        @pl.when(at == OPENING - 1)
        def _():
            for copy in last_copies:
                copy.start()

        @pl.when(at >= 2)
        def _():
            made_copy(at - 2).wait()

        backward_weights(
            mask_ref[n], lax.rem(at, 2), left_ref, grads_ref, turned_ref, made_ref
        )
        made_copy(at).start()
        return carry

    lax.fori_loop(0, OPENING, backward, 0)
    for n in range(max(stored - 2, 0), stored):
        for copy in save_copies(n, n % 2):
            copy.wait()
    for at in (OPENING - 2, OPENING - 1):
        made_copy(at).wait()
    for copy in [share_copy, turned_copy, *last_copies]:
        copy.wait()


def run_upper(features, stats, gain, bias, masks, b1, b2, labels, weights, classes, total_rows):
    rows, width = features.shape
    sections = masks.shape[0]
    blocks = weights.shape[0]
    depth = width // blocks
    hidden = b1.shape[1]
    stored = sections - OPENING
    slots = 2 + OPENING
    anywhere = pl.BlockSpec(memory_space=pl.ANY)
    inside = pl.BlockSpec(memory_space=pltpu.VMEM)
    tall = jax.ShapeDtypeStruct((rows, width), F32)
    saved = [jax.ShapeDtypeStruct((stored, rows, width), kind) for kind in (F32, BF16, BF16, BF16)]
    return pl.pallas_call(
        functools.partial(upper_kernel, total_rows, classes),
        in_specs=[inside] * 8 + [anywhere],
        out_specs=[anywhere] * 8 + [inside] * 2,
        out_shape=saved
        + [
            jax.ShapeDtypeStruct((width, rows), BF16),
            tall,
            tall,
            jax.ShapeDtypeStruct((blocks, 2, OPENING * depth + HEAD_ROWS, 3 * width), BF16),
            jax.ShapeDtypeStruct((1, hidden), F32),
            jax.ShapeDtypeStruct((1, LANES), F32),
        ],
        scratch_shapes=[
            pltpu.VMEM((slots, rows, width), F32),
            pltpu.VMEM((slots, 3, rows, width), BF16),
            pltpu.VMEM((slots, blocks, 2, depth, 3 * width), BF16),
            pltpu.VMEM((blocks, 2, HEAD_ROWS, hidden + LANES), BF16),
            pltpu.VMEM((rows, width), BF16),
            pltpu.VMEM((width, rows), BF16),
            pltpu.VMEM((rows, width), F32),
            pltpu.VMEM((rows, width), F32),
            pltpu.VMEM((blocks, 2, HEAD_ROWS, 3 * width), BF16),
            pltpu.VMEM((2, blocks, 2, depth, 3 * width), BF16),
            pltpu.VMEM((2, width, rows), BF16),
            pltpu.VMEM((rows, 3 * width), BF16),
            pltpu.SemaphoreType.DMA((slots,)),
            pltpu.SemaphoreType.DMA((2, 4)),
            pltpu.SemaphoreType.DMA((2,)),
            pltpu.SemaphoreType.DMA((5,)),
        ],
        compiler_params=pltpu.CompilerParams(vmem_limit_bytes=VMEM_LIMIT),
        name="sections_and_head",
    )(features, stats, gain, bias, masks, b1, b2, labels, weights)


def lower_kernel(
    total_rows,
    place_ref, mask_ref, x_ref, stat_ref, s_in, u_in, r_in, o_in, weights, turned_in, grad_in, scaled_in,
    own_x, pass_x, own_zy, pass_zy, total_out, sums_ref,
    wide_ref, held_ref, w_ref, turned_ref, grad_ref, scaled_ref,
    made_ref, left_ref, grads_ref, load_sem, in_sem, made_sem, out_sem,
):
    rows, width = grad_ref.shape
    depth = w_ref.shape[3]
    count = s_in.shape[0]
    core = place_ref[2]
    quarter = own_x.shape[3]

    def load_copies(at):
        n, slot = count - 1 - at, lax.rem(at, 2)
        rows_at = pl.ds(pl.multiple_of(n * depth, depth), depth)
        return [
            pltpu.make_async_copy(s_in.at[n], wide_ref.at[slot], load_sem.at[slot, 0]),
            *[
                pltpu.make_async_copy(array.at[n], held_ref.at[slot, which], load_sem.at[slot, 1 + which])
                for which, array in enumerate((u_in, r_in, o_in))
            ],
            pltpu.make_async_copy(weights.at[:, :, rows_at, :], w_ref.at[slot], load_sem.at[slot, 4]),
        ]

    def column_copies(at, slot):
        rows_at = pl.ds(pl.multiple_of(at * depth, depth), depth)
        return [
            pltpu.make_async_copy(
                made_ref.at[slot, :, side, :, pl.ds(q * quarter, quarter)],
                out.at[q, :, rows_at, :],
                made_sem.at[slot, which, q],
            )
            for which, (side, out) in enumerate(((core, own_x), (1 - core, pass_x)))
            for q in range(4)
        ]

    def plane_copies(at, slot):
        rows_at = pl.ds(pl.multiple_of(at * depth, depth), depth)
        return [
            pltpu.make_async_copy(
                made_ref.at[slot, :, side], out.at[:, rows_at, :], made_sem.at[slot, which, 0]
            )
            for which, (side, out) in enumerate(((core, own_zy), (1 - core, pass_zy)))
        ]

    grad_copy = pltpu.make_async_copy(grad_in, grad_ref, in_sem.at[0])
    scaled_copy = pltpu.make_async_copy(scaled_in, scaled_ref, in_sem.at[1])
    turned_copy = pltpu.make_async_copy(turned_in, turned_ref, in_sem.at[2])
    total_copy = pltpu.make_async_copy(scaled_ref, total_out, out_sem.at[0])
    grad_copy.start()
    for copy in load_copies(0):
        copy.start()
    scaled_copy.start()
    turned_copy.start()
    grad_copy.wait()

    def backward(at, carry):
        n, slot = count - 1 - at, lax.rem(at, 2)
        for copy in load_copies(at):
            copy.wait()

        @pl.when(at == 0)
        def _():
            scaled_copy.wait()

        @pl.when(at + 1 < count)
        def _():
            for copy in load_copies(at + 1):
                copy.start()

        backward_rows(
            mask_ref[n], section_weight(w_ref, slot, width), slot,
            wide_ref, held_ref, left_ref, grads_ref, grad_ref, scaled_ref,
        )

        @pl.when(at == 0)
        def _():
            turned_copy.wait()

        @pl.when((at >= 2) & (at - 2 < COLUMN))
        def _():
            for copy in column_copies(at - 2, slot):
                copy.wait()

        @pl.when(at - 2 >= COLUMN)
        def _():
            for copy in plane_copies(at - 2 - COLUMN, slot):
                copy.wait()

        @pl.when(at == count - 1)
        def _():
            total = scaled_ref[...] + grad_ref[...]
            scaled_ref[...] = total
            normed, _ = normalise(total_rows, x_ref[...], stat_ref[...])
            sums_ref[0:1] = jnp.sum(total, 0, keepdims=True)
            sums_ref[1:2] = jnp.sum(total * normed, 0, keepdims=True)
            total_copy.start()

        backward_weights(mask_ref[n], slot, left_ref, grads_ref, turned_ref, made_ref)

        @pl.when(at < COLUMN)
        def _():
            for copy in column_copies(at, slot):
                copy.start()

        @pl.when(at >= COLUMN)
        def _():
            for copy in plane_copies(at - COLUMN, slot):
                copy.start()

        return carry

    lax.fori_loop(0, count, backward, 0)
    for at in range(max(count - 2, 0), count):
        copies = column_copies(at, at % 2) if at < COLUMN else plane_copies(at - COLUMN, at % 2)
        for copy in copies:
            copy.wait()
    total_copy.wait()


def run_lower(place, masks, features, stats, saved, weights, turned, grad_state, grad_scaled, total_rows):
    rows, width = features.shape
    blocks = weights.shape[0]
    depth = width // blocks
    count = saved[0].shape[0]
    columns = 3 * width
    anywhere = pl.BlockSpec(memory_space=pl.ANY)
    inside = pl.BlockSpec(memory_space=pltpu.VMEM)
    across = jax.ShapeDtypeStruct((4, blocks, COLUMN * depth, columns // 4), BF16)
    plane = jax.ShapeDtypeStruct((blocks, (count - COLUMN) * depth, columns), BF16)
    return pl.pallas_call(
        functools.partial(lower_kernel, total_rows),
        in_specs=[pl.BlockSpec(memory_space=pltpu.SMEM)] + [inside] * 3 + [anywhere] * 8,
        out_specs=[anywhere] * 5 + [inside],
        out_shape=[
            across,
            across,
            plane,
            plane,
            jax.ShapeDtypeStruct((rows, width), F32),
            jax.ShapeDtypeStruct((2, width), F32),
        ],
        scratch_shapes=[
            pltpu.VMEM((2, rows, width), F32),
            pltpu.VMEM((2, 3, rows, width), BF16),
            pltpu.VMEM((2, blocks, 2, depth, columns), BF16),
            pltpu.VMEM((width, rows), BF16),
            pltpu.VMEM((rows, width), F32),
            pltpu.VMEM((rows, width), F32),
            pltpu.VMEM((2, blocks, 2, depth, columns), BF16),
            pltpu.VMEM((2, width, rows), BF16),
            pltpu.VMEM((rows, columns), BF16),
            pltpu.SemaphoreType.DMA((2, 5)),
            pltpu.SemaphoreType.DMA((3,)),
            pltpu.SemaphoreType.DMA((2, 2, 4)),
            pltpu.SemaphoreType.DMA((1,)),
        ],
        compiler_params=pltpu.CompilerParams(vmem_limit_bytes=VMEM_LIMIT),
        name="sections_backward",
    )(place, masks, features, stats, *saved, weights, turned, grad_state, grad_scaled)


def pairs(sizes, axis, flip):
    table = []
    for source in range(math.prod(sizes)):
        place = list(np.unravel_index(source, sizes))
        place[axis] ^= flip
        table.append((source, int(np.ravel_multi_index(place, sizes))))
    return table


def everywhere_sum(value, sizes, names):
    for axis in reversed(range(len(sizes))):
        for flip in (1, 3) if sizes[axis] == 4 else (1,):
            value = value + lax.ppermute(value, names, pairs(sizes, axis, flip))
    return value


def add(*parts):
    return functools.reduce(lambda a, b: a + b, [part.astype(F32) for part in parts])


def shifted(sizes, axis, by):
    table = []
    for source in range(math.prod(sizes)):
        place = list(np.unravel_index(source, sizes))
        place[axis] = (place[axis] + by) % sizes[axis]
        table.append((source, int(np.ravel_multi_index(place, sizes))))
    return table


def in_order(parts, at):
    turned = jnp.stack(parts[::-1] * 2, 0)
    return lax.dynamic_slice_in_dim(turned, 3 - at, 4, 0)


def column_scatter(total):
    got = lax.all_to_all(total, "dp", 0, 0)
    return jnp.sum(got.astype(F32), 0).astype(BF16)


def plane_scatter(total):
    groups = [[2 * at + core for at in range(total.shape[0])] for core in range(2)]
    got = lax.all_to_all(total, "fsdp", 0, 0, axis_index_groups=groups)
    return jnp.sum(got.astype(F32), 0).astype(BF16)


def column_gather(part, sizes, names, place):
    parts = [part] + [lax.ppermute(part, names, shifted(sizes, 0, by)) for by in (1, 2, 3)]
    return jnp.concatenate(list(in_order(parts, place[3])), 1).astype(F32)


def permute_scatter(total, sizes, names, place):
    total = total.reshape(sizes[1], sizes[2], *total.shape[1:])
    for axis in (1, 2):
        pick = lambda by: lax.dynamic_index_in_dim(
            total, (place[axis - 1] + by) % sizes[axis], 0, keepdims=False
        )
        arrived = [lax.ppermute(pick(by), names, shifted(sizes, axis, by)) for by in (1, 3, 2)]
        total = add(pick(0), *arrived).astype(BF16)
    return total


def column_sum(value, sizes, names):
    for flip in (1, 3):
        other = lax.ppermute(value, names, pairs(sizes, 0, flip))
        value = add(value, other)
        if flip == 1:
            value = value.astype(BF16)
    return value


def on_device(
    sizes,
    features,
    bn_gain,
    bn_bias,
    gate_weights,
    feature_masks,
    head_first,
    head_first_bias,
    head_second,
    head_second_bias,
    labels,
):
    names = ("dp", "fsdp")
    rows, width = features.shape
    sections, depth, columns = gate_weights.shape
    hidden = head_first.shape[1]
    classes = head_second.shape[1]
    total_rows = rows * math.prod(sizes)
    gain, bias = bn_gain[None], bn_bias[None]
    masks = feature_masks.astype(F32)[:, None, :]
    b1 = head_first_bias[None]
    b2 = jnp.pad(head_second_bias, (0, LANES - classes))[None]

    inputs = features.astype(F32)
    stats = jnp.stack([jnp.sum(inputs, 0), jnp.sum(inputs * inputs, 0)])
    stats = everywhere_sum(stats.reshape(-1, LANES), sizes, names).reshape(2, width)

    extra = jnp.pad(head_first, ((0, 0), (0, columns - hidden))) + jnp.pad(
        head_second, ((0, HEAD_ROWS - head_second.shape[0]), (hidden, columns - hidden - classes))
    )
    weights = lax.all_gather(
        jnp.concatenate([gate_weights.reshape(sections * depth, columns), extra], 0), "fsdp", axis=0
    )
    weights = weights.reshape(-1, 2, *weights.shape[1:])
    fsdp = lax.axis_index("fsdp")
    place = jnp.stack([fsdp // 8, fsdp // 2 % 4, fsdp % 2, lax.axis_index("dp")])
    *saved, turned, grad_state, grad_scaled, top, sum1, sum2 = run_upper(
        features, stats, gain, bias, masks, b1, b2, labels[:, None], weights, classes, total_rows
    )
    top = lax.psum_scatter(top.reshape(-1, *top.shape[2:]), "fsdp", scatter_dimension=0)
    own_x, pass_x, own_zy, pass_zy, grad_scaled, *sums = run_lower(
        place, masks, features, stats, saved, weights, turned, grad_state, grad_scaled, total_rows
    )
    across = add(own_x, lax.ppermute(pass_x, names, pairs(sizes, 3, 1))).astype(BF16)
    plane = add(own_zy, lax.ppermute(pass_zy, names, pairs(sizes, 3, 1))).astype(BF16)
    across, plane, sums = lax.optimization_barrier((across, plane, sums))
    across = column_scatter(across)
    plane = permute_scatter(plane, sizes, names, place)
    small = jnp.concatenate([sums[0].reshape(-1), sum1[0], sum2[0]])
    small = jnp.pad(small, (0, -small.size % 1024)).reshape(-1, LANES)
    small = everywhere_sum(small, sizes, names).reshape(-1)
    across = column_gather(plane_scatter(across), sizes, names, place)
    plane = column_sum(plane, sizes, names)
    small, top = lax.optimization_barrier((small, top))
    top = column_sum(top, sizes, names)
    finished = [None] * sections
    order = list(range(sections))[::-1]
    cuts = (OPENING, OPENING + COLUMN, sections)
    for part, start, stop in zip((top, across, plane), (0, *cuts), cuts):
        for at, n in enumerate(order[start:stop]):
            finished[n] = part[at * depth : (at + 1) * depth]
    head_grad = top[OPENING * depth :]
    gate_grad = jnp.stack(finished, 0)
    head_first_grad = head_grad[:, :hidden]
    head_second_grad = head_grad[: head_second.shape[0], hidden : hidden + classes]

    sum_grad, sum_cross = small[:width], small[width : 2 * width]
    first_bias_grad = small[2 * width : 2 * width + hidden]
    second_bias_grad = small[2 * width + hidden : 2 * width + hidden + classes]
    normed, scale = normalise(total_rows, features, stats)
    features_grad = (
        scale * gain * (grad_scaled - sum_grad / total_rows - normed * (sum_cross / total_rows))
    )
    return (
        features_grad,
        sum_cross,
        sum_grad,
        gate_grad,
        head_first_grad,
        first_bias_grad,
        head_second_grad,
        second_bias_grad,
    )


def solution(mesh):
    placed = (
        P(("dp", "fsdp"), None),
        P(),
        P(),
        P(None, "fsdp", None),
        P(),
        P("fsdp", None),
        P(),
        P("fsdp", None),
        P(),
        P(("dp", "fsdp")),
    )
    sizes = (mesh.shape["dp"], 4, 4, mesh.shape["fsdp"] // 16)
    return jax.shard_map(
        functools.partial(on_device, sizes),
        mesh=mesh,
        in_specs=placed,
        out_specs=(
            P(("dp", "fsdp"), None),
            P(),
            P(),
            P(None, "fsdp", None),
            P("fsdp", None),
            P(),
            P("fsdp", None),
            P(),
        ),
        check_vma=False,
    )
```

time: 426 us -> 294 us (0.69)
  waiting for transfers between devices: 277 us -> 133 us
  starting transfers between devices: 29.7 us -> 50.6 us
  Pallas kernels: 84.2 us -> 67.3 us
  other arithmetic: 5.47 us -> 17.8 us
    reduce_scatter x2 -> x1, waiting for transfers between devices: 192 us -> 0.01 us  [on_device(): lax.psum_scatter(top.reshape(-1, *top.shape[2:]), 'fsdp', scatter_dimensi...]
    ppermute x2 -> x15, waiting for transfers between devices: 6.38 us -> 26 us  [the longest x4 10.3 us: column_sum(): other = lax.ppermute(value, names, pairs(sizes, 0, flip))]
    pallas_call x4 -> x2, Pallas kernels: 84.2 us -> 67.3 us  [the longest x1 42 us: run_upper(): pl.pallas_call(functools.partial(upper_kernel, total_rows, classes), in_s...]
    ppermute x2 -> x15, starting transfers between devices: 3.62 us -> 18.4 us  [the longest x6 8.19 us: permute_scatter(): lax.ppermute(pick(by), names, shifted(sizes, axis, by))]
    ppermute x14, waiting for transfers between devices: 24.3 us -> 38.5 us  [everywhere_sum(): value = value + lax.ppermute(value, names, pairs(sizes, axis, flip))]
    all_to_all x0 -> x2, waiting for transfers between devices: none -> 12 us  [the longest x1 12 us: plane_scatter(): got = lax.all_to_all(total, 'fsdp', 0, 0, axis_index_groups=groups)]
    all_to_all x0 -> x2, starting transfers between devices: none -> 9.09 us  [the longest x1 4.61 us: plane_scatter(): got = lax.all_to_all(total, 'fsdp', 0, 0, axis_index_groups=groups)]
    convert_element_type x1 -> x8, other arithmetic: 0.15 us -> 8.88 us  [the longest x1 3.21 us: on_device(): add(own_zy, lax.ppermute(pass_zy, names, pairs(sizes, 3, 1))).astype(BF16)]
  transfers between devices with their start and end apart: 19 -> 33, of which waited for: 16 -> 19; matrix products, arithmetic and copies ran while one was open for 3% -> 7% of each run, Pallas kernels for 0% -> 9%
where the time goes in v2:
time: 294 us
  waiting for transfers between devices  133 us (45%)
  Pallas kernels  67.3 us (23%)
  starting transfers between devices  50.6 us (17%)
  other arithmetic  17.8 us (6%)
  between operations  14.4 us (5%)
  local copies, waits for them, and re-layouts  10.8 us (4%)
    all_gather x1, waiting for transfers between devices, on_device(): lax.all_gather(jnp.concatenate([gate_weights.reshape(sections * depth, co...  56.2 us
    pallas_call x1, Pallas kernels, run_upper(): pl.pallas_call(functools.partial(upper_kernel, total_rows, classes), in_s...  42 us
    ppermute x14, waiting for transfers between devices, everywhere_sum(): value = value + lax.ppermute(value, names, pairs(sizes, axis, flip))  38.5 us
    pallas_call x1, Pallas kernels, run_lower(): pl.pallas_call(functools.partial(lower_kernel, total_rows), in_specs=[pl....  25.3 us
    ppermute x14, starting transfers between devices, everywhere_sum(): value = value + lax.ppermute(value, names, pairs(sizes, axis, flip))  23.1 us
    all_to_all x1, waiting for transfers between devices, plane_scatter(): got = lax.all_to_all(total, 'fsdp', 0, 0, axis_index_groups=groups)  12 us
    ppermute x4, waiting for transfers between devices, column_sum(): other = lax.ppermute(value, names, pairs(sizes, 0, flip))  10.3 us
    ppermute x6, starting transfers between devices, permute_scatter(): lax.ppermute(pick(by), names, shifted(sizes, axis, by))  8.19 us
  transfers between devices with their start and end apart: 33, of which 19 were waited for; matrix products, arithmetic and copies ran while one was open for 7% of the time, Pallas kernels for 9%

profile of v2, /device:TPU:0, one launch (start us, length us, event | category | flops | bytes accessed | tf_op | source)
XLA Modules:
  0.0 293.8 jit_solution(2499420202129291287)
XLA Ops:
  8.0 1.9 pad_maximum_fusion
  10.4 1.2 collective-permute-done
  11.6 1.7 collective-permute-start.1
  13.2 1.9 collective-permute-done.1
  15.2 3.1 %collective-permute-start.2 = (f32[8,128]{1,0:T(8,128)S(1)}, f32[8,128]{1,0:T(8,128)S(1)}, u32[]{:S(2)}, u32[]{:S(2)}) collective-permute-start(f32[8,128]{1,0:T(8,128)S(1)} %add.184), channel_id=1, source_target_pairs={{0,6},{1,7},{2,4},{3,5},{4,2},{5,3},{6,0},{7,1},{8,14},{9,15},{10,... | collective-permute-start | bytes 12296 | tf_op jit(solution)/shard_map/ppermute | solution.py:532
  18.3 1.7 collective-permute-done.2
  20.0 2.0 collective-permute-start.3
  22.0 1.6 collective-permute-done.3
  23.6 4.1 %collective-permute-start.4 = (f32[8,128]{1,0:T(8,128)S(1)}, f32[8,128]{1,0:T(8,128)S(1)}, u32[]{:S(2)}, u32[]{:S(2)}) collective-permute-start(f32[8,128]{1,0:T(8,128)S(1)} %add.186), channel_id=1, source_target_pairs={{0,24},{1,25},{2,26},{3,27},{4,28},{5,29},{6,30},{7,31},{8,16},{9,... | collective-permute-start | bytes 12296 | tf_op jit(solution)/shard_map/ppermute | solution.py:532
  27.8 1.6 collective-permute-done.4
  29.3 1.5 collective-permute-start.5
  30.8 2.1 collective-permute-done.5
  33.0 2.8 collective-permute-start.6
  38.4 56.2 %all-gather.3.cloned.1.call-done = bf16[6656,1536]{1,0:T(8,128)(2,1)} async-done(((bf16[208,1536]{1,0:T(8,128)(2,1)}), bf16[6656,1536]{1,0:T(8,128)(2,1)}) %all-gather.3.cloned.1.call-update) | async-done | bytes 20447248 | tf_op jit(solution)/shard_map/all_gather | solution.py:621
  94.6 42.0 %sections_and_head.1 = (f32[3,768,512]{2,1,0:T(8,128)}, bf16[3,768,512]{2,1,0:T(8,128)(2,1)}, bf16[3,768,512]{2,1,0:T(8,128)(2,1)}, bf16[3,768,512]{2,1,0:T(8,12...) custom-call(bf16[768,512]{1,0:T(8,128)(2,1)} %x_ref.3, ...), custom_call_target="tpu_custom_call" | custom-call | tf_op jit(solution)/shard_map/sections_and_head/pallas_call | solution.py:321
  137.3 25.3 %sections_backward.1 = (bf16[4,16,64,384]{3,2,1,0:T(8,128)(2,1)}, bf16[4,16,64,384]{3,2,1,0:T(8,128)(2,1)}, bf16[16,32,1536]{2,1,0:T(8,128)(2,1)}, bf16[16,32,15...) custom-call(s32[4]{0:T(128)} %pad_add_fusion.1.place_ref, f32[6,1,512]{2,1,0:T(1,128)} %broadcast_in_dim.20.mask_ref, ...), custom_call_target="tpu_custom_call" | custom-call | tf_op jit(solution)/shard_map/sections_backward/pallas_call | solution.py:488
  163.2 8.1 %collective-permute-done.8 = bf16[16,32,1536]{2,1,0:T(8,128)(2,1)S(1)} collective-permute-done((bf16[16,32,1536]{2,1,0:T(8,128)(2,1)}, bf16[16,32,1536]{2,1,0:T(8,128)(2,1)S(1)}, u32[]{:S(2)}, u32[]{:S(2)}) %collective-permute-start.8) | collective-permute-done | bytes 1572896 | tf_op jit(solution)/shard_map/ppermute | solution.py:635
  171.3 3.2 %add_convert_fusion.1 = bf16[16,32,1536]{2,1,0:T(8,128)(2,1)} fusion(bf16[16,32,1536]{2,1,0:T(8,128)(2,1)S(1)} %collective-permute-done.8, bf16[16,32,1536]{2,1,0:T(8,128)(2,1)} %get-tuple-element.39), kind=kLoop, calls=%fused_computation.1 | loop fusion | flops 3145728 | bytes 4718592 | tf_op jit(solution)/shard_map/convert_element_type | solution.py:635
  174.5 2.9 add_convert_fusion
  177.4 4.5 %all-to-all-start = ((bf16[4,16,64,384]{3,2,1,0:T(8,128)(2,1)}), bf16[4,16,64,384]{3,2,1,0:T(8,128)(2,1)S(1)}, u32[]{:S(2)}, u32[]{:S(2)}) async-start(bf16[4,16,64,384]{3,2,1,0:T(8,128)(2,1)} %add_convert_fusion), calls=%async_computation.1 | async-start | bytes 6291456 | tf_op jit(solution)/shard_map/all_to_all | solution.py:555
  182.0 2.2 dynamic-slice_bitcast_fusion.2
  184.2 1.3 collective-permute-start.16
  185.5 1.9 collective-permute-start.17
  187.5 1.7 collective-permute-start.18
  189.2 3.6 %collective-permute-done.10 = f32[16,128]{1,0:T(8,128)S(1)} collective-permute-done((f32[16,128]{1,0:T(8,128)S(1)}, f32[16,128]{1,0:T(8,128)S(1)}, u32[]{:S(2)}, u32[]{:S(2)}) %collective-permute-start.10) | collective-permute-done | bytes 8224 | tf_op jit(solution)/shard_map/ppermute | solution.py:532
  192.9 1.5 collective-permute-start.11
  194.3 3.6 %collective-permute-done.11 = f32[16,128]{1,0:T(8,128)S(1)} collective-permute-done((f32[16,128]{1,0:T(8,128)S(1)}, f32[16,128]{1,0:T(8,128)S(1)}, u32[]{:S(2)}, u32[]{:S(2)}) %collective-permute-start.11) | collective-permute-done | bytes 8224 | tf_op jit(solution)/shard_map/ppermute | solution.py:532
  198.6 19.6 %collective-permute-done.12 = f32[16,128]{1,0:T(8,128)} collective-permute-done((f32[16,128]{1,0:T(8,128)S(1)}, f32[16,128]{1,0:T(8,128)}, u32[]{:S(2)}, u32[]{:S(2)}) %collective-permute-start.12) | collective-permute-done | bytes 8224 | tf_op jit(solution)/shard_map/ppermute | solution.py:532
  219.8 1.6 fusion.7
  221.5 3.2 %collective-permute-start.20 = (bf16[32,1536]{1,0:T(8,128)(2,1)S(1)}, bf16[32,1536]{1,0:T(8,128)(2,1)S(1)}, u32[]{:S(2)}, u32[]{:S(2)}) collective-permute-start(bf16[32,1536]{1,0:T(8,128)(2,1)S(1)} %get-tuple-element.67), channel_id=1, source_target_pairs={{0,6},{1,7},{2,0},{3,1},{4,2},{5,3},{6,4},{7,5},{8,14},{9,15},{10,... | collective-permute-start | bytes 294920 | tf_op jit(solution)/shard_map/ppermute | solution.py:576
  224.8 2.6 collective-permute-start.14
  227.4 2.1 collective-permute-done.19
  229.5 1.5 collective-permute-done.21
  231.1 2.7 collective-permute-start.22
  233.8 1.6 reduce_sum.44
  235.4 4.6 %all-to-all-start.1 = ((bf16[16,64,384]{2,1,0:T(8,128)(2,1)}), bf16[16,64,384]{2,1,0:T(8,128)(2,1)S(1)}, u32[]{:S(2)}, u32[]{:S(2)}) async-start(bf16[16,64,384]{2,1,0:T(8,128)(2,1)} %reduce_sum.44), calls=%async_computation.2 | async-start | bytes 1572864 | tf_op jit(solution)/shard_map/all_to_all | solution.py:561
  240.1 2.2 collective-permute-start.15
  242.3 1.2 collective-permute-start.23
  243.5 1.5 collective-permute-done.15
  245.0 12.0 %all-to-all-done.1 = bf16[16,64,384]{2,1,0:T(8,128)(2,1)S(1)} async-done(((bf16[16,64,384]{2,1,0:T(8,128)(2,1)}), bf16[16,64,384]{2,1,0:T(8,128)(2,1)S(1)}, u32[]{:S(2)}, u32[]{:S(2)}) %all-to-all-start.1) | async-done | bytes 786464 | tf_op jit(solution)/shard_map/all_to_all | solution.py:561
  257.2 1.6 collective-permute-start.24
  260.2 1.4 collective-permute-start.26
  261.6 3.5 %collective-permute-done.25 = bf16[64,384]{1,0:T(8,128)(2,1)S(1)} collective-permute-done((bf16[64,384]{1,0:T(8,128)(2,1)S(1)}, bf16[64,384]{1,0:T(8,128)(2,1)S(1)}, u32[]{:S(2)}, u32[]{:S(2)}) %collective-permute-start.25) | collective-permute-done | bytes 49184 | tf_op jit(solution)/shard_map/ppermute | solution.py:566
  267.4 6.5 %collective-permute-done.27 = bf16[112,1536]{1,0:T(8,128)(2,1)S(1)} collective-permute-done((bf16[112,1536]{1,0:T(8,128)(2,1)}, bf16[112,1536]{1,0:T(8,128)(2,1)S(1)}, u32[]{:S(2)}, u32[]{:S(2)}) %collective-permute-start.27) | collective-permute-done | bytes 344096 | tf_op jit(solution)/shard_map/ppermute | solution.py:583
  274.0 1.1 add_convert_fusion.2
  275.0 1.6 collective-permute-start.28
  278.3 1.5 fusion.4
  279.8 3.7 %collective-permute-done.28 = bf16[112,1536]{1,0:T(8,128)(2,1)S(1)} collective-permute-done((bf16[112,1536]{1,0:T(8,128)(2,1)S(1)}, bf16[112,1536]{1,0:T(8,128)(2,1)S(1)}, u32[]{:S(2)}, u32[]{:S(2)}) %collective-permute-start.28) | collective-permute-done | bytes 344096 | tf_op jit(solution)/shard_map/ppermute | solution.py:583
  (106 shorter events, 16.6 us)
Async XLA Ops:
  7.2 2.9 copy-start
  7.2 28.5 %copy-start.10 = (f32[10]{0:T(128)S(1)}, f32[10]{0:T(128)}, u32[]{:S(2)}) copy-start(f32[10]{0:T(128)} %param.18) | copy-start | bytes 124
  7.2 29.0 %copy-start.4 = (s32[6,512]{1,0:T(8,128)S(1)}, s32[6,512]{1,0:T(8,128)}, u32[]{:S(2)}) copy-start(s32[6,512]{1,0:T(8,128)} %param.14) | copy-start | bytes 36868
  7.2 29.6 %copy-start.8 = (s32[768]{0:T(1024)S(1)}, s32[768]{0:T(1024)}, u32[]{:S(2)}) copy-start(s32[768]{0:T(1024)} %param.19) | copy-start | bytes 9220
  7.2 87.4 %all-gather.3.cloned.1.call-start = ((), (), s32[]{:S(2)}) async-start(), calls=%async_computation.4 | async-start | bytes 21086208 | tf_op jit(solution)/shard_map/all_gather | solution.py:621
  10.0 256.5 %reduce-scatter.2.cloned.1.call-start = ((), (), s32[]{:S(2)}) async-start(), calls=%async_computation.3 | async-start | bytes 11354112 | tf_op jit(solution)/shard_map/reduce_scatter | solution.py:630
  10.3 1.2 collective-permute-start
  11.6 3.6 %collective-permute-start.1 = (f32[8,128]{1,0:T(8,128)S(1)}, f32[8,128]{1,0:T(8,128)S(1)}, u32[]{:S(2)}, u32[]{:S(2)}) collective-permute-start(f32[8,128]{1,0:T(8,128)S(1)} %add.183), channel_id=1, source_target_pairs={{0,2},{1,3},{2,0},{3,1},{4,6},{5,7},{6,4},{7,5},{8,10},{9,11},{10,... | collective-permute-start | bytes 12296 | tf_op jit(solution)/shard_map/ppermute | solution.py:532
  15.2 4.8 %collective-permute-start.2 = (f32[8,128]{1,0:T(8,128)S(1)}, f32[8,128]{1,0:T(8,128)S(1)}, u32[]{:S(2)}, u32[]{:S(2)}) collective-permute-start(f32[8,128]{1,0:T(8,128)S(1)} %add.184), channel_id=1, source_target_pairs={{0,6},{1,7},{2,4},{3,5},{4,2},{5,3},{6,0},{7,1},{8,14},{9,15},{10,... | collective-permute-start | bytes 12296 | tf_op jit(solution)/shard_map/ppermute | solution.py:532
  20.0 3.6 %collective-permute-start.3 = (f32[8,128]{1,0:T(8,128)S(1)}, f32[8,128]{1,0:T(8,128)S(1)}, u32[]{:S(2)}, u32[]{:S(2)}) collective-permute-start(f32[8,128]{1,0:T(8,128)S(1)} %add.185), channel_id=1, source_target_pairs={{0,8},{1,9},{2,10},{3,11},{4,12},{5,13},{6,14},{7,15},{8,0},{9,1},... | collective-permute-start | bytes 12296 | tf_op jit(solution)/shard_map/ppermute | solution.py:532
  23.6 5.7 %collective-permute-start.4 = (f32[8,128]{1,0:T(8,128)S(1)}, f32[8,128]{1,0:T(8,128)S(1)}, u32[]{:S(2)}, u32[]{:S(2)}) collective-permute-start(f32[8,128]{1,0:T(8,128)S(1)} %add.186), channel_id=1, source_target_pairs={{0,24},{1,25},{2,26},{3,27},{4,28},{5,29},{6,30},{7,31},{8,16},{9,... | collective-permute-start | bytes 12296 | tf_op jit(solution)/shard_map/ppermute | solution.py:532
  29.3 3.6 %collective-permute-start.5 = (f32[8,128]{1,0:T(8,128)S(1)}, f32[8,128]{1,0:T(8,128)S(1)}, u32[]{:S(2)}, u32[]{:S(2)}) collective-permute-start(f32[8,128]{1,0:T(8,128)S(1)} %add.187), channel_id=1, source_target_pairs={{0,32},{1,33},{2,34},{3,35},{4,36},{5,37},{6,38},{7,39},{8,40},{9,... | collective-permute-start | bytes 12296 | tf_op jit(solution)/shard_map/ppermute | solution.py:532
  33.0 4.8 %collective-permute-start.6 = (f32[8,128]{1,0:T(8,128)S(1)}, f32[8,128]{1,0:T(8,128)S(1)}, u32[]{:S(2)}, u32[]{:S(2)}) collective-permute-start(f32[8,128]{1,0:T(8,128)S(1)} %add.188), channel_id=1, source_target_pairs={{0,96},{1,97},{2,98},{3,99},{4,100},{5,101},{6,102},{7,103},{8,104... | collective-permute-start | bytes 12296 | tf_op jit(solution)/shard_map/ppermute | solution.py:532
  162.6 11.9 %collective-permute-start.7 = (bf16[4,16,64,384]{3,2,1,0:T(8,128)(2,1)}, bf16[4,16,64,384]{3,2,1,0:T(8,128)(2,1)S(1)}, u32[]{:S(2)}, u32[]{:S(2)}) collective-permute-start(bf16[4,16,64,384]{3,2,1,0:T(8,128)(2,1)} %get-tuple-element.38), channel_id=1, source_target_pairs={{0,1},{1,0},{2,3},{3,2},{4,5},{5,4},{6,7},{7,6},{8,9},{9,8},{10,11... | collective-permute-start | bytes 9437192 | tf_op jit(solution)/shard_map/ppermute | solution.py:634
  162.9 8.4 %collective-permute-start.8 = (bf16[16,32,1536]{2,1,0:T(8,128)(2,1)}, bf16[16,32,1536]{2,1,0:T(8,128)(2,1)S(1)}, u32[]{:S(2)}, u32[]{:S(2)}) collective-permute-start(bf16[16,32,1536]{2,1,0:T(8,128)(2,1)} %get-tuple-element.40), channel_id=1, source_target_pairs={{0,1},{1,0},{2,3},{3,2},{4,5},{5,4},{6,7},{7,6},{8,9},{9,8},{10,11... | collective-permute-start | bytes 4718600 | tf_op jit(solution)/shard_map/ppermute | solution.py:635
  171.3 3.2 %copy-start.2 = (bf16[4,16,64,384]{3,2,1,0:T(8,128)(2,1)S(1)}, bf16[4,16,64,384]{3,2,1,0:T(8,128)(2,1)}, u32[]{:S(2)}) copy-start(bf16[4,16,64,384]{3,2,1,0:T(8,128)(2,1)} %get-tuple-element.37) | copy-start | bytes 9437188
  177.4 4.5 %copy-start.9 = (f32[2,512]{1,0:T(2,128)S(1)}, f32[2,512]{1,0:T(2,128)}, u32[]{:S(2)}) copy-start(f32[2,512]{1,0:T(2,128)} %get-tuple-element.42) | copy-start | bytes 12292
  177.4 4.5 %copy-start.5 = (f32[1,256]{1,0:T(1,128)S(1)}, f32[1,256]{1,0:T(1,128)}, u32[]{:S(2)}) copy-start(f32[1,256]{1,0:T(1,128)} %get-tuple-element.43) | copy-start | bytes 3076
  177.4 4.5 %copy-start.7 = (f32[1,128]{1,0:T(1,128)S(1)}, f32[1,128]{1,0:T(1,128)}, u32[]{:S(2)}) copy-start(f32[1,128]{1,0:T(1,128)} %get-tuple-element.44) | copy-start | bytes 1540
  177.4 56.4 %all-to-all-start = ((bf16[4,16,64,384]{3,2,1,0:T(8,128)(2,1)}), bf16[4,16,64,384]{3,2,1,0:T(8,128)(2,1)S(1)}, u32[]{:S(2)}, u32[]{:S(2)}) async-start(bf16[4,16,64,384]{3,2,1,0:T(8,128)(2,1)} %add_convert_fusion), calls=%async_computation.1 | async-start | bytes 6291456 | tf_op jit(solution)/shard_map/all_to_all | solution.py:555
  181.9 7.2 %collective-permute-start.9 = (f32[16,128]{1,0:T(8,128)S(1)}, f32[16,128]{1,0:T(8,128)S(1)}, u32[]{:S(2)}, u32[]{:S(2)}) collective-permute-start(f32[16,128]{1,0:T(8,128)S(1)} %fusion.16), channel_id=1, source_target_pairs={{0,1},{1,0},{2,3},{3,2},{4,5},{5,4},{6,7},{7,6},{8,9},{9,8},{10,11... | collective-permute-start | bytes 24584 | tf_op jit(solution)/shard_map/ppermute | solution.py:532
  184.2 40.5 %copy-start.6 = (f32[512]{0:T(512)S(1)}, f32[512]{0:T(512)}, u32[]{:S(2)}) copy-start(f32[512]{0:T(512)} %param.11) | copy-start | bytes 6148
  184.2 35.5 %collective-permute-start.16 = (bf16[4,32,1536]{2,1,0:T(8,128)(2,1)}, bf16[4,32,1536]{2,1,0:T(8,128)(2,1)}, u32[]{:S(2)}, u32[]{:S(2)}) collective-permute-start(bf16[4,32,1536]{2,1,0:T(8,128)(2,1)} %get-tuple-element.58), channel_id=1, source_target_pairs={{0,8},{1,9},{2,10},{3,11},{4,12},{5,13},{6,14},{7,15},{8,16},{9,17... | collective-permute-start | bytes 1179656 | tf_op jit(solution)/shard_map/ppermute | solution.py:576
  185.5 34.2 %collective-permute-start.17 = (bf16[4,32,1536]{2,1,0:T(8,128)(2,1)}, bf16[4,32,1536]{2,1,0:T(8,128)(2,1)}, u32[]{:S(2)}, u32[]{:S(2)}) collective-permute-start(bf16[4,32,1536]{2,1,0:T(8,128)(2,1)} %get-tuple-element.60), channel_id=1, source_target_pairs={{0,24},{1,25},{2,26},{3,27},{4,28},{5,29},{6,30},{7,31},{8,0},{9,1... | collective-permute-start | bytes 1179656 | tf_op jit(solution)/shard_map/ppermute | solution.py:576
  187.5 32.3 %collective-permute-start.18 = (bf16[4,32,1536]{2,1,0:T(8,128)(2,1)S(1)}, bf16[4,32,1536]{2,1,0:T(8,128)(2,1)}, u32[]{:S(2)}, u32[]{:S(2)}) collective-permute-start(bf16[4,32,1536]{2,1,0:T(8,128)(2,1)S(1)} %get-tuple-element.59), channel_id=1, source_target_pairs={{0,16},{1,17},{2,18},{3,19},{4,20},{5,21},{6,22},{7,23},{8,24},{9,... | collective-permute-start | bytes 1179656 | tf_op jit(solution)/shard_map/ppermute | solution.py:576
  189.1 3.7 %collective-permute-start.10 = (f32[16,128]{1,0:T(8,128)S(1)}, f32[16,128]{1,0:T(8,128)S(1)}, u32[]{:S(2)}, u32[]{:S(2)}) collective-permute-start(f32[16,128]{1,0:T(8,128)S(1)} %fusion.19), channel_id=1, source_target_pairs={{0,2},{1,3},{2,0},{3,1},{4,6},{5,7},{6,4},{7,5},{8,10},{9,11},{10,... | collective-permute-start | bytes 24584 | tf_op jit(solution)/shard_map/ppermute | solution.py:532
  192.9 5.1 %collective-permute-start.11 = (f32[16,128]{1,0:T(8,128)S(1)}, f32[16,128]{1,0:T(8,128)S(1)}, u32[]{:S(2)}, u32[]{:S(2)}) collective-permute-start(f32[16,128]{1,0:T(8,128)S(1)} %fusion.22), channel_id=1, source_target_pairs={{0,6},{1,7},{2,4},{3,5},{4,2},{5,3},{6,0},{7,1},{8,14},{9,15},{10,... | collective-permute-start | bytes 24584 | tf_op jit(solution)/shard_map/ppermute | solution.py:532
  198.0 20.2 %collective-permute-start.12 = (f32[16,128]{1,0:T(8,128)S(1)}, f32[16,128]{1,0:T(8,128)}, u32[]{:S(2)}, u32[]{:S(2)}) collective-permute-start(f32[16,128]{1,0:T(8,128)S(1)} %add.199), channel_id=1, source_target_pairs={{0,8},{1,9},{2,10},{3,11},{4,12},{5,13},{6,14},{7,15},{8,0},{9,1},... | collective-permute-start | bytes 24584 | tf_op jit(solution)/shard_map/ppermute | solution.py:532
  218.9 5.8 %collective-permute-start.13 = (f32[16,128]{1,0:T(8,128)S(1)}, f32[16,128]{1,0:T(8,128)S(1)}, u32[]{:S(2)}, u32[]{:S(2)}) collective-permute-start(f32[16,128]{1,0:T(8,128)S(1)} %add.200), channel_id=1, source_target_pairs={{0,24},{1,25},{2,26},{3,27},{4,28},{5,29},{6,30},{7,31},{8,16},{9,... | collective-permute-start | bytes 24584 | tf_op jit(solution)/shard_map/ppermute | solution.py:532
  221.4 8.1 %collective-permute-start.19 = (bf16[32,1536]{1,0:T(8,128)(2,1)S(1)}, bf16[32,1536]{1,0:T(8,128)(2,1)S(1)}, u32[]{:S(2)}, u32[]{:S(2)}) collective-permute-start(bf16[32,1536]{1,0:T(8,128)(2,1)S(1)} %get-tuple-element.65), channel_id=1, source_target_pairs={{0,2},{1,3},{2,4},{3,5},{4,6},{5,7},{6,0},{7,1},{8,10},{9,11},{10,... | collective-permute-start | bytes 294920 | tf_op jit(solution)/shard_map/ppermute | solution.py:576
  221.5 8.0 %collective-permute-start.20 = (bf16[32,1536]{1,0:T(8,128)(2,1)S(1)}, bf16[32,1536]{1,0:T(8,128)(2,1)S(1)}, u32[]{:S(2)}, u32[]{:S(2)}) collective-permute-start(bf16[32,1536]{1,0:T(8,128)(2,1)S(1)} %get-tuple-element.67), channel_id=1, source_target_pairs={{0,6},{1,7},{2,0},{3,1},{4,2},{5,3},{6,4},{7,5},{8,14},{9,15},{10,... | collective-permute-start | bytes 294920 | tf_op jit(solution)/shard_map/ppermute | solution.py:576
  224.7 6.3 %collective-permute-start.21 = (bf16[32,1536]{1,0:T(8,128)(2,1)S(1)}, bf16[32,1536]{1,0:T(8,128)(2,1)S(1)}, u32[]{:S(2)}, u32[]{:S(2)}) collective-permute-start(bf16[32,1536]{1,0:T(8,128)(2,1)S(1)} %get-tuple-element.66), channel_id=1, source_target_pairs={{0,4},{1,5},{2,6},{3,7},{4,0},{5,1},{6,2},{7,3},{8,12},{9,13},{10,... | collective-permute-start | bytes 294920 | tf_op jit(solution)/shard_map/ppermute | solution.py:576
  224.8 15.3 %collective-permute-start.14 = (f32[16,128]{1,0:T(8,128)S(1)}, f32[16,128]{1,0:T(8,128)S(1)}, u32[]{:S(2)}, u32[]{:S(2)}) collective-permute-start(f32[16,128]{1,0:T(8,128)S(1)} %add.201), channel_id=1, source_target_pairs={{0,32},{1,33},{2,34},{3,35},{4,36},{5,37},{6,38},{7,39},{8,40},{9,... | collective-permute-start | bytes 24584 | tf_op jit(solution)/shard_map/ppermute | solution.py:532
  231.1 11.2 %collective-permute-start.22 = (bf16[32,1536]{1,0:T(8,128)(2,1)S(1)}, bf16[32,1536]{1,0:T(8,128)(2,1)S(1)}, u32[]{:S(2)}, u32[]{:S(2)}) collective-permute-start(bf16[32,1536]{1,0:T(8,128)(2,1)S(1)} %fusion.15), channel_id=1, source_target_pairs={{0,32},{1,33},{2,34},{3,35},{4,36},{5,37},{6,38},{7,39},{8,40},{9,... | collective-permute-start | bytes 294920 | tf_op jit(solution)/shard_map/ppermute | solution.py:583
  235.4 21.6 %all-to-all-start.1 = ((bf16[16,64,384]{2,1,0:T(8,128)(2,1)}), bf16[16,64,384]{2,1,0:T(8,128)(2,1)S(1)}, u32[]{:S(2)}, u32[]{:S(2)}) async-start(bf16[16,64,384]{2,1,0:T(8,128)(2,1)} %reduce_sum.44), calls=%async_computation.2 | async-start | bytes 1572864 | tf_op jit(solution)/shard_map/all_to_all | solution.py:561
  240.1 4.9 %collective-permute-start.15 = (f32[16,128]{1,0:T(8,128)S(1)}, f32[16,128]{1,0:T(8,128)S(1)}, u32[]{:S(2)}, u32[]{:S(2)}) collective-permute-start(f32[16,128]{1,0:T(8,128)S(1)} %add.202), channel_id=1, source_target_pairs={{0,96},{1,97},{2,98},{3,99},{4,100},{5,101},{6,102},{7,103},{8,104... | collective-permute-start | bytes 24584 | tf_op jit(solution)/shard_map/ppermute | solution.py:532
  242.3 16.5 %collective-permute-start.23 = (bf16[32,1536]{1,0:T(8,128)(2,1)S(1)}, bf16[32,1536]{1,0:T(8,128)(2,1)S(1)}, u32[]{:S(2)}, u32[]{:S(2)}) collective-permute-start(bf16[32,1536]{1,0:T(8,128)(2,1)S(1)} %add_convert_fusion.3), channel_id=1, source_target_pairs={{0,96},{1,97},{2,98},{3,99},{4,100},{5,101},{6,102},{7,103},{8,104... | collective-permute-start | bytes 294920 | tf_op jit(solution)/shard_map/ppermute | solution.py:583
  257.2 4.4 %collective-permute-start.24 = (bf16[64,384]{1,0:T(8,128)(2,1)S(1)}, bf16[64,384]{1,0:T(8,128)(2,1)S(1)}, u32[]{:S(2)}, u32[]{:S(2)}) collective-permute-start(bf16[64,384]{1,0:T(8,128)(2,1)S(1)} %reduce_sum.45), channel_id=1, source_target_pairs={{0,96},{1,97},{2,98},{3,99},{4,100},{5,101},{6,102},{7,103},{8,104... | collective-permute-start | bytes 147464 | tf_op jit(solution)/shard_map/ppermute | solution.py:566
  259.5 5.6 %collective-permute-start.25 = (bf16[64,384]{1,0:T(8,128)(2,1)S(1)}, bf16[64,384]{1,0:T(8,128)(2,1)S(1)}, u32[]{:S(2)}, u32[]{:S(2)}) collective-permute-start(bf16[64,384]{1,0:T(8,128)(2,1)S(1)} %reduce_sum.45), channel_id=1, source_target_pairs={{0,64},{1,65},{2,66},{3,67},{4,68},{5,69},{6,70},{7,71},{8,72},{9,... | collective-permute-start | bytes 147464 | tf_op jit(solution)/shard_map/ppermute | solution.py:566
  260.2 5.4 %collective-permute-start.26 = (bf16[64,384]{1,0:T(8,128)(2,1)S(1)}, bf16[64,384]{1,0:T(8,128)(2,1)S(1)}, u32[]{:S(2)}, u32[]{:S(2)}) collective-permute-start(bf16[64,384]{1,0:T(8,128)(2,1)S(1)} %reduce_sum.45), channel_id=1, source_target_pairs={{0,32},{1,33},{2,34},{3,35},{4,36},{5,37},{6,38},{7,39},{8,40},{9,... | collective-permute-start | bytes 147464 | tf_op jit(solution)/shard_map/ppermute | solution.py:566
  265.7 12.7 %copy-start.1 = (bf16[768,512]{1,0:T(8,128)(2,1)S(1)}, bf16[768,512]{1,0:T(8,128)(2,1)}, u32[]{:S(2)}) copy-start(bf16[768,512]{1,0:T(8,128)(2,1)} %x_ref.3) | copy-start | bytes 2359300
  265.7 12.7 %copy-start.3 = (f32[768,512]{1,0:T(8,128)S(1)}, f32[768,512]{1,0:T(8,128)}, u32[]{:S(2)}) copy-start(f32[768,512]{1,0:T(8,128)} %get-tuple-element.36) | copy-start | bytes 4718596
  266.5 7.5 %collective-permute-start.27 = (bf16[112,1536]{1,0:T(8,128)(2,1)}, bf16[112,1536]{1,0:T(8,128)(2,1)S(1)}, u32[]{:S(2)}, u32[]{:S(2)}) collective-permute-start(bf16[112,1536]{1,0:T(8,128)(2,1)} %bitcast.106), channel_id=1, source_target_pairs={{0,32},{1,33},{2,34},{3,35},{4,36},{5,37},{6,38},{7,39},{8,40},{9,... | collective-permute-start | bytes 1032200 | tf_op jit(solution)/shard_map/ppermute | solution.py:583
  275.0 8.5 %collective-permute-start.28 = (bf16[112,1536]{1,0:T(8,128)(2,1)S(1)}, bf16[112,1536]{1,0:T(8,128)(2,1)S(1)}, u32[]{:S(2)}, u32[]{:S(2)}) collective-permute-start(bf16[112,1536]{1,0:T(8,128)(2,1)S(1)} %add_convert_fusion.2), channel_id=1, source_target_pairs={{0,96},{1,97},{2,98},{3,99},{4,100},{5,101},{6,102},{7,103},{8,104... | collective-permute-start | bytes 1032200 | tf_op jit(solution)/shard_map/ppermute | solution.py:583
Sparse Core Ops, SparseCore 0:
  10.9 83.6 all-gather.2
  136.8 122.9 reduce-scatter.1

commit v3 on v2

--- a/solution.py
+++ b/solution.py
@@ -14,8 +14,9 @@
 BF16 = jnp.bfloat16
 VMEM_LIMIT = 60 * 1024 * 1024
 HEAD_ROWS = 16
-OPENING = 3
-COLUMN = 2
+OPENING = 4
+QUARTERS = ((0, 0, 4), (1, 0, 4), (3, 0, 4), (2, 0, 2), (2, 2, 4))
+PIECES = 2 * len(QUARTERS)
 LANES = 128
 
 
@@ -70,7 +71,7 @@
 
     def weight(lower, start):
         place = slice(0, half) if lower else slice(half, 2 * half)
-        return w_ref[slot, place, :, :, start : start + width].reshape(width, width)
+        return w_ref[slot, place, ..., start : start + width].reshape(width, width)
 
     return weight
 
@@ -147,11 +148,11 @@
     grad_ref, share_ref, sum1_ref, sum2_ref,
 ):
     rows, width = state_ref.shape
-    blocks = head_ref.shape[0]
+    blocks = share_ref.shape[0]
     owners = 2 * blocks
     hidden = b1_ref.shape[1]
-    first = head_ref[:, :, :, 0:hidden].reshape(width, hidden)
-    second = head_ref[:, :, :, hidden : hidden + LANES].astype(F32)[:, :, 0 : hidden // owners]
+    first = head_ref[..., 0:hidden].reshape(width, hidden)
+    second = head_ref[..., hidden : hidden + LANES].astype(F32)[..., 0 : hidden // owners, :]
     second = second.reshape(hidden, LANES).astype(BF16)
     head_in = state_ref[...].astype(BF16)
     pre = dot(head_in, first) + b1_ref[...]
@@ -179,57 +180,48 @@
     share_ref[:, :, :, hidden + LANES :] = jnp.zeros((blocks, 2, HEAD_ROWS, tail), BF16)
 
 
-def upper_kernel(
-    total_rows, classes,
-    x_ref, stat_ref, gain_ref, bias_ref, mask_ref, b1_ref, b2_ref, label_ref, weights,
-    s_out, u_out, r_out, o_out, turned_out, grad_out, scaled_out, made_out, sum1_ref, sum2_ref,
-    wide_ref, held_ref, w_ref, head_ref, low_ref, turned_ref, state_ref, scaled_ref,
-    share_ref, made_ref, left_ref, grads_ref, w_sem, save_sem, made_sem, out_sem,
+def entry_kernel(
+    total_rows, place_ref, x_ref, stat_ref, gain_ref, bias_ref, mask_ref, *refs,
 ):
+    pieces, refs = refs[:PIECES], refs[PIECES:]
+    s_out, u_out, r_out, o_out, state_out, low_out, turned_out, full_out = refs[:8]
+    wide_ref, held_ref, w_ref, low_ref, turned_ref, state_ref, w_sem, save_sem, out_sem = refs[8:]
     rows, width = x_ref.shape
-    sections = mask_ref.shape[0]
-    depth = w_ref.shape[3]
-    stored = sections - OPENING
-
-    def slot_of(n):
-        return jnp.where(n < stored, lax.rem(n, 2), n - stored + 2)
-
-    def w_copy(n):
-        rows_at = pl.ds(pl.multiple_of(n * depth, depth), depth)
-        slot = slot_of(n)
-        return pltpu.make_async_copy(weights.at[:, :, rows_at, :], w_ref.at[slot], w_sem.at[slot])
-
-    head_copy = pltpu.make_async_copy(
-        weights.at[:, :, pl.ds(sections * depth, HEAD_ROWS), pl.ds(0, head_ref.shape[3])],
-        head_ref,
-        out_sem.at[0],
-    )
-
-    def save_copies(n, slot):
-        return [pltpu.make_async_copy(wide_ref.at[slot], s_out.at[n], save_sem.at[slot, 0])] + [
-            pltpu.make_async_copy(held_ref.at[slot, at], out.at[n], save_sem.at[slot, at + 1])
-            for at, out in enumerate((u_out, r_out, o_out))
+    count, depth = w_ref.shape[0], w_ref.shape[4]
+    quarter = w_ref.shape[5] // 4
+
+    def piece_copies(at):
+        copies = []
+        for which, piece in enumerate(pieces):
+            (by, first, last), side = QUARTERS[which // 2], which % 2
+            core = place_ref[2] if side == 0 else 1 - place_ref[2]
+            start = pl.multiple_of(lax.rem(place_ref[3] + 4 - by, 4) * quarter, LANES)
+            copies.append(
+                pltpu.make_async_copy(
+                    piece.at[:, :, pl.ds(at * depth, depth)],
+                    w_ref.at[at, first:last, :, core, :, pl.ds(start, quarter)],
+                    w_sem.at[at, which],
+                )
+            )
+        return copies
+
+    def save_copies(at):
+        return [
+            pltpu.make_async_copy(w_ref.at[at], full_out.at[:, :, :, at], save_sem.at[at, 0]),
+            pltpu.make_async_copy(wide_ref.at[at], s_out.at[at], save_sem.at[at, 1]),
+        ] + [
+            pltpu.make_async_copy(held_ref.at[at, which], out.at[at], save_sem.at[at, which + 2])
+            for which, out in enumerate((u_out, r_out, o_out))
         ]
 
-    def made_copy(at):
-        rows_at = pl.ds(pl.multiple_of(at * depth, depth), depth)
-        slot = lax.rem(at, 2)
-        return pltpu.make_async_copy(
-            made_ref.at[slot], made_out.at[:, :, rows_at, :], made_sem.at[slot]
-        )
-
-    share_copy = pltpu.make_async_copy(
-        share_ref, made_out.at[:, :, pl.ds(OPENING * depth, HEAD_ROWS), :], out_sem.at[1]
-    )
-    turned_copy = pltpu.make_async_copy(turned_ref, turned_out, out_sem.at[2])
-    last_copies = [
-        pltpu.make_async_copy(state_ref, grad_out, out_sem.at[3]),
-        pltpu.make_async_copy(scaled_ref, scaled_out, out_sem.at[4]),
+    out_copies = [
+        pltpu.make_async_copy(low_ref, low_out, out_sem.at[0]),
+        pltpu.make_async_copy(turned_ref, turned_out, out_sem.at[1]),
+        pltpu.make_async_copy(state_ref, state_out, out_sem.at[2]),
     ]
-
-    w_copy(0).start()
-    w_copy(1).start()
-    head_copy.start()
+    for at in range(count):
+        for copy in piece_copies(at):
+            copy.start()
     for part in halves(rows):
         normed, _ = normalise(total_rows, x_ref[part], stat_ref[...])
         scaled = normed * gain_ref[...] + bias_ref[...]
@@ -237,47 +229,138 @@
         low = scaled.astype(BF16)
         low_ref[part] = low
         turned_ref[:, part] = low.T
-    turned_copy.start()
+    for copy in out_copies[:2]:
+        copy.start()
+    for at in range(count):
+        for copy in piece_copies(at):
+            copy.wait()
+        forward_section(
+            mask_ref[at], section_weight(w_ref, at, width), at,
+            wide_ref, held_ref, state_ref, low_ref,
+        )
+        for copy in save_copies(at):
+            copy.start()
+    out_copies[2].start()
+    for at in range(count):
+        for copy in save_copies(at):
+            copy.wait()
+    for copy in out_copies:
+        copy.wait()
+
+
+def run_entry(place, features, stats, gain, bias, masks, pieces, count, total_rows):
+    rows, width = features.shape
+    depth = pieces[2].shape[2] // count
+    anywhere = pl.BlockSpec(memory_space=pl.ANY)
+    inside = pl.BlockSpec(memory_space=pltpu.VMEM)
+    return pl.pallas_call(
+        functools.partial(entry_kernel, total_rows),
+        in_specs=[pl.BlockSpec(memory_space=pltpu.SMEM)] + [inside] * 5 + [anywhere] * PIECES,
+        out_specs=[anywhere] * 8,
+        out_shape=[
+            jax.ShapeDtypeStruct((count, rows, width), kind) for kind in (F32, BF16, BF16, BF16)
+        ]
+        + [
+            jax.ShapeDtypeStruct((rows, width), F32),
+            jax.ShapeDtypeStruct((rows, width), BF16),
+            jax.ShapeDtypeStruct((width, rows), BF16),
+            jax.ShapeDtypeStruct((4, 4, 2, count, depth, 3 * width), BF16),
+        ],
+        scratch_shapes=[
+            pltpu.VMEM((count, rows, width), F32),
+            pltpu.VMEM((count, 3, rows, width), BF16),
+            pltpu.VMEM((count, 4, 4, 2, depth, 3 * width), BF16),
+            pltpu.VMEM((rows, width), BF16),
+            pltpu.VMEM((width, rows), BF16),
+            pltpu.VMEM((rows, width), F32),
+            pltpu.SemaphoreType.DMA((count, PIECES)),
+            pltpu.SemaphoreType.DMA((count, 5)),
+            pltpu.SemaphoreType.DMA((3,)),
+        ],
+        compiler_params=pltpu.CompilerParams(vmem_limit_bytes=VMEM_LIMIT),
+        name="first_sections",
+    )(place, features, stats, gain, bias, masks, *pieces)
+
+
+def upper_kernel(
+    row_scale, classes,
+    place_ref, mask_ref, b1_ref, b2_ref, label_ref, weights, state_in, low_in, turned_in, head_own, head_other,
+    grad_out, scaled_out, made_out, sum1_ref, sum2_ref,
+    wide_ref, held_ref, w_ref, head_ref, low_ref, turned_ref, state_ref, scaled_ref,
+    share_ref, made_ref, left_ref, grads_ref, w_sem, made_sem, in_sem, out_sem,
+):
+    rows, width = state_ref.shape
+    depth = w_ref.shape[3]
+    early = mask_ref.shape[0] - OPENING
+
+    def w_copy(n):
+        rows_at = pl.ds(pl.multiple_of(n * depth, depth), depth)
+        return pltpu.make_async_copy(weights.at[:, :, rows_at, :], w_ref.at[n], w_sem.at[n])
+
+    def made_copy(at):
+        rows_at = pl.ds(pl.multiple_of(at * depth, depth), depth)
+        slot = lax.rem(at, 2)
+        return pltpu.make_async_copy(
+            made_ref.at[slot], made_out.at[:, :, rows_at, :], made_sem.at[slot]
+        )
+
+    head_rows_at = pl.ds(head_own.shape[2] - HEAD_ROWS, HEAD_ROWS)
+    in_copies = [
+        pltpu.make_async_copy(state_in, state_ref, in_sem.at[0]),
+        pltpu.make_async_copy(low_in, low_ref, in_sem.at[1]),
+        pltpu.make_async_copy(turned_in, turned_ref, in_sem.at[2]),
+    ] + [
+        pltpu.make_async_copy(
+            array.at[:, :, head_rows_at], head_ref.at[:, :, side], in_sem.at[3 + which]
+        )
+        for which, (array, side) in enumerate(
+            ((head_own, place_ref[2]), (head_other, 1 - place_ref[2]))
+        )
+    ]
+    share_copy = pltpu.make_async_copy(
+        share_ref, made_out.at[:, :, pl.ds(OPENING * depth, HEAD_ROWS), :], out_sem.at[0]
+    )
+    last_copies = [
+        pltpu.make_async_copy(state_ref, grad_out, out_sem.at[1]),
+        pltpu.make_async_copy(scaled_ref, scaled_out, out_sem.at[2]),
+    ]
+    for copy in in_copies[:2]:
+        copy.start()
+    w_copy(0).start()
+    w_copy(1).start()
+    for copy in in_copies[2:]:
+        copy.start()
+    for copy in in_copies[:2]:
+        copy.wait()
 
     def forward(n, carry):
-        slot = slot_of(n)
         w_copy(n).wait()
 
-        @pl.when((n >= 1) & (n + 1 < sections))
+        @pl.when((n >= 1) & (n + 1 < OPENING))
         def _():
             w_copy(n + 1).start()
 
-        @pl.when((n >= 2) & (n < stored))
-        def _():
-            for copy in save_copies(n - 2, slot):
-                copy.wait()
-
         forward_section(
-            mask_ref[n], section_weight(w_ref, slot, width), slot,
+            mask_ref[early + n], section_weight(w_ref, n, width), n,
             wide_ref, held_ref, state_ref, low_ref,
         )
-
-        @pl.when(n < stored)
-        def _():
-            for copy in save_copies(n, slot):
-                copy.start()
-
         return carry
 
-    lax.fori_loop(0, sections, forward, 0)
-    head_copy.wait()
+    lax.fori_loop(0, OPENING, forward, 0)
+    for copy in in_copies[2:]:
+        copy.wait()
     head_rows(
-        1.0 / rows, classes, state_ref, head_ref, b1_ref, b2_ref, label_ref,
+        row_scale, classes, state_ref, head_ref, b1_ref, b2_ref, label_ref,
         state_ref, share_ref, sum1_ref, sum2_ref,
     )
     share_copy.start()
     scaled_ref[...] = jnp.zeros_like(scaled_ref)
 
     def backward(at, carry):
-        n = sections - 1 - at
-        slot = slot_of(n)
+        n = OPENING - 1 - at
+        mask = mask_ref[early + n]
         backward_rows(
-            mask_ref[n], section_weight(w_ref, slot, width), slot,
+            mask, section_weight(w_ref, n, width), n,
             wide_ref, held_ref, left_ref, grads_ref, state_ref, scaled_ref,
         )
 
@@ -290,41 +373,30 @@
         def _():
             made_copy(at - 2).wait()
 
-        backward_weights(
-            mask_ref[n], lax.rem(at, 2), left_ref, grads_ref, turned_ref, made_ref
-        )
+        backward_weights(mask, lax.rem(at, 2), left_ref, grads_ref, turned_ref, made_ref)
         made_copy(at).start()
         return carry
 
     lax.fori_loop(0, OPENING, backward, 0)
-    for n in range(max(stored - 2, 0), stored):
-        for copy in save_copies(n, n % 2):
-            copy.wait()
     for at in (OPENING - 2, OPENING - 1):
         made_copy(at).wait()
-    for copy in [share_copy, turned_copy, *last_copies]:
+    for copy in [share_copy, *last_copies]:
         copy.wait()
 
 
-def run_upper(features, stats, gain, bias, masks, b1, b2, labels, weights, classes, total_rows):
-    rows, width = features.shape
-    sections = masks.shape[0]
+def run_upper(place, masks, b1, b2, labels, weights, state, low, turned, heads, classes):
+    rows, width = state.shape
     blocks = weights.shape[0]
     depth = width // blocks
     hidden = b1.shape[1]
-    stored = sections - OPENING
-    slots = 2 + OPENING
     anywhere = pl.BlockSpec(memory_space=pl.ANY)
     inside = pl.BlockSpec(memory_space=pltpu.VMEM)
     tall = jax.ShapeDtypeStruct((rows, width), F32)
-    saved = [jax.ShapeDtypeStruct((stored, rows, width), kind) for kind in (F32, BF16, BF16, BF16)]
     return pl.pallas_call(
-        functools.partial(upper_kernel, total_rows, classes),
-        in_specs=[inside] * 8 + [anywhere],
-        out_specs=[anywhere] * 8 + [inside] * 2,
-        out_shape=saved
-        + [
-            jax.ShapeDtypeStruct((width, rows), BF16),
+        functools.partial(upper_kernel, 1.0 / rows, classes),
+        in_specs=[pl.BlockSpec(memory_space=pltpu.SMEM)] + [inside] * 4 + [anywhere] * 6,
+        out_specs=[anywhere] * 3 + [inside] * 2,
+        out_shape=[
             tall,
             tall,
             jax.ShapeDtypeStruct((blocks, 2, OPENING * depth + HEAD_ROWS, 3 * width), BF16),
@@ -332,10 +404,10 @@
             jax.ShapeDtypeStruct((1, LANES), F32),
         ],
         scratch_shapes=[
-            pltpu.VMEM((slots, rows, width), F32),
-            pltpu.VMEM((slots, 3, rows, width), BF16),
-            pltpu.VMEM((slots, blocks, 2, depth, 3 * width), BF16),
-            pltpu.VMEM((blocks, 2, HEAD_ROWS, hidden + LANES), BF16),
+            pltpu.VMEM((OPENING, rows, width), F32),
+            pltpu.VMEM((OPENING, 3, rows, width), BF16),
+            pltpu.VMEM((OPENING, blocks, 2, depth, 3 * width), BF16),
+            pltpu.VMEM((4, 4, 2, HEAD_ROWS, hidden + LANES), BF16),
             pltpu.VMEM((rows, width), BF16),
             pltpu.VMEM((width, rows), BF16),
             pltpu.VMEM((rows, width), F32),
@@ -344,20 +416,20 @@
             pltpu.VMEM((2, blocks, 2, depth, 3 * width), BF16),
             pltpu.VMEM((2, width, rows), BF16),
             pltpu.VMEM((rows, 3 * width), BF16),
-            pltpu.SemaphoreType.DMA((slots,)),
-            pltpu.SemaphoreType.DMA((2, 4)),
+            pltpu.SemaphoreType.DMA((OPENING,)),
             pltpu.SemaphoreType.DMA((2,)),
             pltpu.SemaphoreType.DMA((5,)),
+            pltpu.SemaphoreType.DMA((3,)),
         ],
         compiler_params=pltpu.CompilerParams(vmem_limit_bytes=VMEM_LIMIT),
         name="sections_and_head",
-    )(features, stats, gain, bias, masks, b1, b2, labels, weights)
+    )(place, masks, b1, b2, labels, weights, state, low, turned, *heads)
 
 
 def lower_kernel(
     total_rows,
     place_ref, mask_ref, x_ref, stat_ref, s_in, u_in, r_in, o_in, weights, turned_in, grad_in, scaled_in,
-    own_x, pass_x, own_zy, pass_zy, total_out, sums_ref,
+    own_x, pass_x, total_out, sums_ref,
     wide_ref, held_ref, w_ref, turned_ref, grad_ref, scaled_ref,
     made_ref, left_ref, grads_ref, load_sem, in_sem, made_sem, out_sem,
 ):
@@ -391,15 +463,6 @@
             for q in range(4)
         ]
 
-    def plane_copies(at, slot):
-        rows_at = pl.ds(pl.multiple_of(at * depth, depth), depth)
-        return [
-            pltpu.make_async_copy(
-                made_ref.at[slot, :, side], out.at[:, rows_at, :], made_sem.at[slot, which, 0]
-            )
-            for which, (side, out) in enumerate(((core, own_zy), (1 - core, pass_zy)))
-        ]
-
     grad_copy = pltpu.make_async_copy(grad_in, grad_ref, in_sem.at[0])
     scaled_copy = pltpu.make_async_copy(scaled_in, scaled_ref, in_sem.at[1])
     turned_copy = pltpu.make_async_copy(turned_in, turned_ref, in_sem.at[2])
@@ -434,14 +497,9 @@
         def _():
             turned_copy.wait()
 
-        @pl.when((at >= 2) & (at - 2 < COLUMN))
+        @pl.when(at >= 2)
         def _():
             for copy in column_copies(at - 2, slot):
-                copy.wait()
-
-        @pl.when(at - 2 >= COLUMN)
-        def _():
-            for copy in plane_copies(at - 2 - COLUMN, slot):
                 copy.wait()
 
         @pl.when(at == count - 1)
@@ -455,22 +513,13 @@
 
         backward_weights(mask_ref[n], slot, left_ref, grads_ref, turned_ref, made_ref)
 
-        @pl.when(at < COLUMN)
-        def _():
-            for copy in column_copies(at, slot):
-                copy.start()
-
-        @pl.when(at >= COLUMN)
-        def _():
-            for copy in plane_copies(at - COLUMN, slot):
-                copy.start()
-
+        for copy in column_copies(at, slot):
+            copy.start()
         return carry
 
     lax.fori_loop(0, count, backward, 0)
     for at in range(max(count - 2, 0), count):
-        copies = column_copies(at, at % 2) if at < COLUMN else plane_copies(at - COLUMN, at % 2)
-        for copy in copies:
+        for copy in column_copies(at, at % 2):
             copy.wait()
     total_copy.wait()
 
@@ -483,17 +532,14 @@
     columns = 3 * width
     anywhere = pl.BlockSpec(memory_space=pl.ANY)
     inside = pl.BlockSpec(memory_space=pltpu.VMEM)
-    across = jax.ShapeDtypeStruct((4, blocks, COLUMN * depth, columns // 4), BF16)
-    plane = jax.ShapeDtypeStruct((blocks, (count - COLUMN) * depth, columns), BF16)
+    across = jax.ShapeDtypeStruct((4, blocks, count * depth, columns // 4), BF16)
     return pl.pallas_call(
         functools.partial(lower_kernel, total_rows),
         in_specs=[pl.BlockSpec(memory_space=pltpu.SMEM)] + [inside] * 3 + [anywhere] * 8,
-        out_specs=[anywhere] * 5 + [inside],
+        out_specs=[anywhere] * 3 + [inside],
         out_shape=[
             across,
             across,
-            plane,
-            plane,
             jax.ShapeDtypeStruct((rows, width), F32),
             jax.ShapeDtypeStruct((2, width), F32),
         ],
@@ -526,8 +572,8 @@
     return table
 
 
-def everywhere_sum(value, sizes, names):
-    for axis in reversed(range(len(sizes))):
+def everywhere_sum(value, sizes, names, axes=(3, 2, 1, 0)):
+    for axis in axes:
         for flip in (1, 3) if sizes[axis] == 4 else (1,):
             value = value + lax.ppermute(value, names, pairs(sizes, axis, flip))
     return value
@@ -551,14 +597,43 @@
     return lax.dynamic_slice_in_dim(turned, 3 - at, 4, 0)
 
 
+def core_groups(count):
+    return [[2 * at + core for at in range(count)] for core in range(2)]
+
+
+def quarter_gather(shard, head, stats, also, sizes, names, place):
+    send = lambda value, axis, by: lax.ppermute(value, names, shifted(sizes, axis, by))
+    quarter = shard.shape[1] // 4
+    own = lax.dynamic_slice_in_dim(shard, place[3] * quarter, quarter, 1)
+    own = jnp.concatenate([own, head], 0)
+    count = sizes[1] * sizes[2]
+    plane = lax.all_to_all(
+        jnp.broadcast_to(own[None], (count, *own.shape)), "fsdp", 0, 0,
+        axis_index_groups=core_groups(count),
+    )
+    plane = plane.reshape(sizes[1], sizes[2], *own.shape)
+    stats = everywhere_sum(stats, sizes, names, (3, 0))
+    plane, stats, also = lax.optimization_barrier((plane, stats, also))
+    moved = plane[:, :, : shard.shape[0]]
+    behind, ahead = send(moved, 0, 1), send(moved, 0, 3)
+    stats = everywhere_sum(stats, sizes, names, (2, 1))
+    behind, ahead, stats = lax.optimization_barrier((behind, ahead, stats))
+    arrived = [plane, behind, ahead, send(behind[:2], 0, 1), send(ahead[2:], 0, 3)]
+    pieces = []
+    for piece in arrived:
+        pieces += [piece, lax.ppermute(piece, names, pairs(sizes, 3, 1))]
+    return pieces, stats, also
+
+
 def column_scatter(total):
     got = lax.all_to_all(total, "dp", 0, 0)
     return jnp.sum(got.astype(F32), 0).astype(BF16)
 
 
 def plane_scatter(total):
-    groups = [[2 * at + core for at in range(total.shape[0])] for core in range(2)]
-    got = lax.all_to_all(total, "fsdp", 0, 0, axis_index_groups=groups)
+    got = lax.all_to_all(
+        total, "fsdp", 0, 0, axis_index_groups=core_groups(total.shape[0])
+    )
     return jnp.sum(got.astype(F32), 0).astype(BF16)
 
 
@@ -567,22 +642,11 @@
     return jnp.concatenate(list(in_order(parts, place[3])), 1).astype(F32)
 
 
-def permute_scatter(total, sizes, names, place):
-    total = total.reshape(sizes[1], sizes[2], *total.shape[1:])
-    for axis in (1, 2):
-        pick = lambda by: lax.dynamic_index_in_dim(
-            total, (place[axis - 1] + by) % sizes[axis], 0, keepdims=False
-        )
-        arrived = [lax.ppermute(pick(by), names, shifted(sizes, axis, by)) for by in (1, 3, 2)]
-        total = add(pick(0), *arrived).astype(BF16)
-    return total
-
-
-def column_sum(value, sizes, names):
-    for flip in (1, 3):
+def column_sum(value, sizes, names, flips=(1, 3)):
+    for flip in flips:
         other = lax.ppermute(value, names, pairs(sizes, 0, flip))
         value = add(value, other)
-        if flip == 1:
+        if flip == flips[0]:
             value = value.astype(BF16)
     return value
 
@@ -613,40 +677,56 @@
 
     inputs = features.astype(F32)
     stats = jnp.stack([jnp.sum(inputs, 0), jnp.sum(inputs * inputs, 0)])
-    stats = everywhere_sum(stats.reshape(-1, LANES), sizes, names).reshape(2, width)
-
-    extra = jnp.pad(head_first, ((0, 0), (0, columns - hidden))) + jnp.pad(
-        head_second, ((0, HEAD_ROWS - head_second.shape[0]), (hidden, columns - hidden - classes))
-    )
-    weights = lax.all_gather(
-        jnp.concatenate([gate_weights.reshape(sections * depth, columns), extra], 0), "fsdp", axis=0
-    )
+    early = sections - OPENING
+    late = gate_weights[early:].reshape(OPENING * depth, columns)
+    weights = lax.all_gather(late, "fsdp", axis=0)
     weights = weights.reshape(-1, 2, *weights.shape[1:])
+    extra = jnp.pad(head_first, ((0, 0), (0, LANES))) + jnp.pad(
+        head_second, ((0, HEAD_ROWS - head_second.shape[0]), (hidden, LANES - classes))
+    )
     fsdp = lax.axis_index("fsdp")
     place = jnp.stack([fsdp // 8, fsdp // 2 % 4, fsdp % 2, lax.axis_index("dp")])
-    *saved, turned, grad_state, grad_scaled, top, sum1, sum2 = run_upper(
-        features, stats, gain, bias, masks, b1, b2, labels[:, None], weights, classes, total_rows
+    pieces, stats, also = quarter_gather(
+        gate_weights[:early].reshape(early * depth, columns), extra,
+        stats.reshape(-1, LANES), (masks, b2, place, labels[:, None]), sizes, names, place,
+    )
+    masks, b2, place, labels = also
+    stats = stats.reshape(2, width)
+    *saved, state, low, turned, full = run_entry(
+        place, features, stats, gain, bias, masks, pieces, early, total_rows
+    )
+    full = full.reshape(16, 2, early * depth, columns)
+    grad_state, grad_scaled, top, sum1, sum2 = run_upper(
+        place, masks, b1, b2, labels, weights, state, low, turned, pieces[:2], classes
     )
     top = lax.psum_scatter(top.reshape(-1, *top.shape[2:]), "fsdp", scatter_dimension=0)
-    own_x, pass_x, own_zy, pass_zy, grad_scaled, *sums = run_lower(
-        place, masks, features, stats, saved, weights, turned, grad_state, grad_scaled, total_rows
+    own_x, pass_x, grad_scaled, *sums = run_lower(
+        place, masks, features, stats, saved, full, turned, grad_state, grad_scaled, total_rows
     )
     across = add(own_x, lax.ppermute(pass_x, names, pairs(sizes, 3, 1))).astype(BF16)
-    plane = add(own_zy, lax.ppermute(pass_zy, names, pairs(sizes, 3, 1))).astype(BF16)
-    across, plane, sums = lax.optimization_barrier((across, plane, sums))
+    across, sums = lax.optimization_barrier((across, sums))
     across = column_scatter(across)
-    plane = permute_scatter(plane, sizes, names, place)
     small = jnp.concatenate([sums[0].reshape(-1), sum1[0], sum2[0]])
     small = jnp.pad(small, (0, -small.size % 1024)).reshape(-1, LANES)
-    small = everywhere_sum(small, sizes, names).reshape(-1)
-    across = column_gather(plane_scatter(across), sizes, names, place)
-    plane = column_sum(plane, sizes, names)
-    small, top = lax.optimization_barrier((small, top))
-    top = column_sum(top, sizes, names)
+    small = everywhere_sum(small, sizes, names, (3, 2))
+    small, across = lax.optimization_barrier((small, across))
+    across = plane_scatter(across)
+    small = everywhere_sum(small, sizes, names, (1, 0))
+    small, across = lax.optimization_barrier((small, across))
+    across = column_gather(across, sizes, names, place)
+    small, top, across = lax.optimization_barrier((small, top, across))
+    small = small.reshape(-1)
+    cut = top.shape[0] // 32 * 16
+    top = jnp.concatenate(
+        [
+            column_sum(top[:cut], sizes, names),
+            column_sum(top[cut:], sizes, names, (3, 1)),
+        ],
+        0,
+    )
     finished = [None] * sections
     order = list(range(sections))[::-1]
-    cuts = (OPENING, OPENING + COLUMN, sections)
-    for part, start, stop in zip((top, across, plane), (0, *cuts), cuts):
+    for part, start, stop in ((top, 0, OPENING), (across, OPENING, sections)):
         for at, n in enumerate(order[start:stop]):
             finished[n] = part[at * depth : (at + 1) * depth]
     head_grad = top[OPENING * depth :]

time: 294 us -> 274 us (0.932)
  waiting for transfers between devices: 133 us -> 118 us
  other arithmetic: 17.8 us -> 9.85 us
  starting transfers between devices: 50.6 us -> 45.2 us
  Pallas kernels: 67.3 us -> 72.5 us
    all_gather x1, waiting for transfers between devices: 56.2 us -> 0.02 us  [on_device(): weights = lax.all_gather(late, 'fsdp', axis=0)]
    all_to_all x1, waiting for transfers between devices: 0.01 us -> 27.9 us  [column_scatter(): got = lax.all_to_all(total, 'dp', 0, 0)]
    pallas_call x1 -> x2, Pallas kernels: 42 us -> 52.9 us  [the longest x1 41.8 us: run_upper(): pl.pallas_call(functools.partial(upper_kernel, 1.0 / rows, classes), in_s...]
    ppermute x14, starting transfers between devices: 23.1 us -> 14.2 us  [everywhere_sum(): value = value + lax.ppermute(value, names, pairs(sizes, axis, flip))]
    all_to_all x1 -> x2, starting transfers between devices: 4.61 us -> 12.2 us  [the longest x1 8.26 us: quarter_gather(): lax.all_to_all(jnp.broadcast_to(own[None], (count, *own.shape)), 'fsdp',...]
    reduce_scatter x1, waiting for transfers between devices: 0.01 us -> 6.93 us  [on_device(): lax.psum_scatter(top.reshape(-1, *top.shape[2:]), 'fsdp', scatter_dimensi...]
    ppermute x1, waiting for transfers between devices: 0.01 us -> 6.45 us  [on_device(): lax.ppermute(pass_x, names, pairs(sizes, 3, 1))]
    pallas_call x1, Pallas kernels: 25.3 us -> 19.6 us  [run_lower(): pl.pallas_call(functools.partial(lower_kernel, total_rows), in_specs=[pl....]
  transfers between devices with their start and end apart: 33 -> 36, of which waited for: 19 -> 25; matrix products, arithmetic and copies ran while one was open for 7% -> 5% of each run, Pallas kernels for 9% -> 11%
where the time goes in v3:
time: 274 us
  waiting for transfers between devices  118 us (43%)
  Pallas kernels  72.5 us (26%)
  starting transfers between devices  45.2 us (16%)
  between operations  15.8 us (6%)
  local copies, waits for them, and re-layouts  12.3 us (4%)
  other arithmetic  9.85 us (4%)
    ppermute x14, waiting for transfers between devices, everywhere_sum(): value = value + lax.ppermute(value, names, pairs(sizes, axis, flip))  43.5 us
    pallas_call x1, Pallas kernels, run_upper(): pl.pallas_call(functools.partial(upper_kernel, 1.0 / rows, classes), in_s...  41.8 us
    all_to_all x1, waiting for transfers between devices, column_scatter(): got = lax.all_to_all(total, 'dp', 0, 0)  27.9 us
    pallas_call x1, Pallas kernels, run_lower(): pl.pallas_call(functools.partial(lower_kernel, total_rows), in_specs=[pl....  19.6 us
    ppermute x14, starting transfers between devices, everywhere_sum(): value = value + lax.ppermute(value, names, pairs(sizes, axis, flip))  14.2 us
    pallas_call x1, Pallas kernels, run_entry(): pl.pallas_call(functools.partial(entry_kernel, total_rows), in_specs=[pl....  11.1 us
    all_to_all x1, waiting for transfers between devices, quarter_gather(): lax.all_to_all(jnp.broadcast_to(own[None], (count, *own.shape)), 'fsdp',...  9.71 us
    ppermute x4, waiting for transfers between devices, quarter_gather(): lax.ppermute(value, names, shifted(sizes, axis, by))  9.07 us
  transfers between devices with their start and end apart: 36, of which 25 were waited for; matrix products, arithmetic and copies ran while one was open for 5% of the time, Pallas kernels for 11%

profile of v3, /device:TPU:0, one launch (start us, length us, event | category | flops | bytes accessed | tf_op | source)
XLA Modules:
  0.0 273.6 jit_solution(11965632482052686821)
XLA Ops:
  7.2 1.8 slice.86
  9.2 1.0 broadcast_in_dim.26
  10.2 8.3 %all-to-all-start = ((bf16[16,80,384]{2,1,0:T(8,128)(2,1)}), bf16[16,80,384]{2,1,0:T(8,128)(2,1)S(1)}, u32[]{:S(2)}, u32[]{:S(2)}) async-start(bf16[16,80,384]{2,1,0:T(8,128)(2,1)} %broadcast_in_dim.26), calls=%async_computation | async-start | bytes 1966080 | tf_op jit(solution)/shard_map/all_to_all | solution.py:610
  18.9 1.2 collective-permute-done
  20.1 1.5 collective-permute-start.1
  22.2 1.5 collective-permute-done.1
  23.7 2.8 %collective-permute-start.2 = (f32[8,128]{1,0:T(8,128)S(1)}, f32[8,128]{1,0:T(8,128)S(1)}, u32[]{:S(2)}, u32[]{:S(2)}) collective-permute-start(f32[8,128]{1,0:T(8,128)S(1)} %add.102), channel_id=1, source_target_pairs={{0,96},{1,97},{2,98},{3,99},{4,100},{5,101},{6,102},{7,103},{8,104... | collective-permute-start | bytes 12296 | tf_op jit(solution)/shard_map/ppermute | solution.py:578
  28.5 9.7 %all-to-all-done = bf16[16,80,384]{2,1,0:T(8,128)(2,1)S(1)} async-done(((bf16[16,80,384]{2,1,0:T(8,128)(2,1)}), bf16[16,80,384]{2,1,0:T(8,128)(2,1)S(1)}, u32[]{:S(2)}, u32[]{:S(2)}) %all-to-all-start) | async-done | bytes 983072 | tf_op jit(solution)/shard_map/all_to_all | solution.py:610
  38.3 1.6 collective-permute-start.3
  40.0 1.7 collective-permute-start.4
  41.7 1.5 collective-permute-start.5
  43.2 2.1 collective-permute-done.5
  45.3 4.8 %collective-permute-done.6 = f32[8,128]{1,0:T(8,128)S(1)} collective-permute-done((f32[8,128]{1,0:T(8,128)S(1)}, f32[8,128]{1,0:T(8,128)S(1)}, u32[]{:S(2)}, u32[]{:S(2)}) %collective-permute-start.6) | collective-permute-done | bytes 4128 | tf_op jit(solution)/shard_map/ppermute | solution.py:578
  50.1 3.6 %collective-permute-done.7 = f32[8,128]{1,0:T(8,128)S(1)} collective-permute-done((f32[8,128]{1,0:T(8,128)S(1)}, f32[8,128]{1,0:T(8,128)S(1)}, u32[]{:S(2)}, u32[]{:S(2)}) %collective-permute-start.7) | collective-permute-done | bytes 4128 | tf_op jit(solution)/shard_map/ppermute | solution.py:578
  53.7 1.0 collective-permute-start.8
  54.7 3.9 %collective-permute-done.8 = f32[8,128]{1,0:T(8,128)S(1)} collective-permute-done((f32[8,128]{1,0:T(8,128)S(1)}, f32[8,128]{1,0:T(8,128)S(1)}, u32[]{:S(2)}, u32[]{:S(2)}) %collective-permute-start.8) | collective-permute-done | bytes 4128 | tf_op jit(solution)/shard_map/ppermute | solution.py:578
  59.7 2.9 %collective-permute-start.14 = (bf16[2,4,64,384]{3,2,1,0:T(8,128)(2,1)S(1)}, bf16[2,4,64,384]{3,2,1,0:T(8,128)(2,1)}, u32[]{:S(2)}, u32[]{:S(2)}) collective-permute-start(bf16[2,4,64,384]{3,2,1,0:T(8,128)(2,1)S(1)} %slice.85), channel_id=1, source_target_pairs={{0,96},{1,97},{2,98},{3,99},{4,100},{5,101},{6,102},{7,103},{8,104... | collective-permute-start | bytes 1179656 | tf_op jit(solution)/shard_map/ppermute | solution.py:605
  62.7 9.1 %collective-permute-done.12.refs_6_ = bf16[2,4,64,384]{3,2,1,0:T(8,128)(2,1)} collective-permute-done((bf16[2,4,64,384]{3,2,1,0:T(8,128)(2,1)S(1)}, bf16[2,4,64,384]{3,2,1,0:T(8,128)(2,1)}, u32[]{:S(2)}, u32[]{:S(2)}) %collective-permute-start.12) | collective-permute-done | bytes 393248 | tf_op jit(solution)/shard_map/ppermute | solution.py:605
  72.3 1.0 copy.20.label_ref
  74.8 11.1 %first_sections.1 = (f32[2,768,512]{2,1,0:T(8,128)}, bf16[2,768,512]{2,1,0:T(8,128)(2,1)}, bf16[2,768,512]{2,1,0:T(8,128)(2,1)}, bf16[2,768,512]{2,1,0:T(8,128)(...) custom-call(s32[4]{0:T(128)} %pad_add_fusion.1.place_ref, ...), custom_call_target="tpu_custom_call" | custom-call | tf_op jit(solution)/shard_map/first_sections/pallas_call | solution.py:256
  85.9 41.8 %sections_and_head.1 = (f32[768,512]{1,0:T(8,128)}, f32[768,512]{1,0:T(8,128)}, bf16[16,2,144,1536]{3,2,1,0:T(8,128)(2,1)}, f32[1,256]{1,0:T(1,128)}, f32[1,128]{1,0:T(1,128)}) custom-call(s32[4]{0:T(128)} %pad_add_fusion.1.place_ref, f32[6,1,512]{2,1,0:T(1,128)} %broadcast_in_dim.27.mask_ref, f32[1,256]{1,0:T(1,128)} %bitcast.119, ...), custom_call_target="tpu_custom_call" | custom-call | tf_op jit(solution)/shard_map/sections_and_head/pallas_call | solution.py:395
  127.8 19.6 %sections_backward.1 = (bf16[4,16,64,384]{3,2,1,0:T(8,128)(2,1)}, bf16[4,16,64,384]{3,2,1,0:T(8,128)(2,1)}, f32[768,512]{1,0:T(8,128)}, f32[2,512]{1,0:T(2,128)}) custom-call(s32[4]{0:T(128)} %pad_add_fusion.1.place_ref, f32[6,1,512]{2,1,0:T(1,128)} %broadcast_in_dim.27.mask_ref, bf16[768,512]{1,0:T(8,128)(2,1)} %x_ref.3, f32[2,512]{1,0:T(2,128)} %reshape.100.stat_ref, ...), custom_call_target="tpu_custom_call" | custom-call | tf_op jit(solution)/shard_map/sections_backward/pallas_call | solution.py:536
  147.6 6.4 %collective-permute-done.16 = bf16[4,16,64,384]{3,2,1,0:T(8,128)(2,1)S(1)} collective-permute-done((bf16[4,16,64,384]{3,2,1,0:T(8,128)(2,1)}, bf16[4,16,64,384]{3,2,1,0:T(8,128)(2,1)S(1)}, u32[]{:S(2)}, u32[]{:S(2)}) %collective-permute-start.16) | collective-permute-done | bytes 3145760 | tf_op jit(solution)/shard_map/ppermute | solution.py:706
  154.1 4.8 %add_convert_fusion = bf16[4,16,64,384]{3,2,1,0:T(8,128)(2,1)} fusion(bf16[4,16,64,384]{3,2,1,0:T(8,128)(2,1)S(1)} %collective-permute-done.16, bf16[4,16,64,384]{3,2,1,0:T(8,128)(2,1)} %get-tuple-element.63), kind=kLoop, calls=%fused_computation | loop fusion | flops 6291456 | bytes 9437184 | tf_op jit(solution)/shard_map/convert_element_type | solution.py:706
  158.9 4.7 %all-to-all-start.1 = ((bf16[4,16,64,384]{3,2,1,0:T(8,128)(2,1)}), bf16[4,16,64,384]{3,2,1,0:T(8,128)(2,1)S(1)}, u32[]{:S(2)}, u32[]{:S(2)}) async-start(bf16[4,16,64,384]{3,2,1,0:T(8,128)(2,1)} %add_convert_fusion), calls=%async_computation.1 | async-start | bytes 6291456 | tf_op jit(solution)/shard_map/all_to_all | solution.py:629
  163.7 1.2 collective-permute-done.17
  164.9 3.6 %collective-permute-done.18 = f32[16,128]{1,0:T(8,128)S(1)} collective-permute-done((f32[16,128]{1,0:T(8,128)S(1)}, f32[16,128]{1,0:T(8,128)S(1)}, u32[]{:S(2)}, u32[]{:S(2)}) %collective-permute-start.18) | collective-permute-done | bytes 8224 | tf_op jit(solution)/shard_map/ppermute | solution.py:578
  168.7 4.8 %collective-permute-done.19 = f32[16,128]{1,0:T(8,128)S(1)} collective-permute-done((f32[16,128]{1,0:T(8,128)S(1)}, f32[16,128]{1,0:T(8,128)S(1)}, u32[]{:S(2)}, u32[]{:S(2)}) %collective-permute-start.19) | collective-permute-done | bytes 8224 | tf_op jit(solution)/shard_map/ppermute | solution.py:578
  173.5 27.9 %all-to-all-done.1 = bf16[4,16,64,384]{3,2,1,0:T(8,128)(2,1)S(1)} async-done(((bf16[4,16,64,384]{3,2,1,0:T(8,128)(2,1)}), bf16[4,16,64,384]{3,2,1,0:T(8,128)(2,1)S(1)}, u32[]{:S(2)}, u32[]{:S(2)}) %all-to-all-start.1) | async-done | bytes 3145760 | tf_op jit(solution)/shard_map/all_to_all | solution.py:629
  201.4 1.6 reduce_sum.44
  203.1 3.9 %all-to-all-start.2 = ((bf16[16,64,384]{2,1,0:T(8,128)(2,1)}), bf16[16,64,384]{2,1,0:T(8,128)(2,1)S(1)}, u32[]{:S(2)}, u32[]{:S(2)}) async-start(bf16[16,64,384]{2,1,0:T(8,128)(2,1)} %reduce_sum.44), calls=%async_computation.2 | async-start | bytes 1572864 | tf_op jit(solution)/shard_map/all_to_all | solution.py:634
  207.0 1.9 collective-permute-start.20
  208.9 8.8 %collective-permute-done.20 = f32[16,128]{1,0:T(8,128)S(1)} collective-permute-done((f32[16,128]{1,0:T(8,128)S(1)}, f32[16,128]{1,0:T(8,128)S(1)}, u32[]{:S(2)}, u32[]{:S(2)}) %collective-permute-start.20) | collective-permute-done | bytes 8224 | tf_op jit(solution)/shard_map/ppermute | solution.py:578
  217.8 3.9 %collective-permute-start.21 = (f32[16,128]{1,0:T(8,128)S(1)}, f32[16,128]{1,0:T(8,128)S(1)}, u32[]{:S(2)}, u32[]{:S(2)}) collective-permute-start(f32[16,128]{1,0:T(8,128)S(1)} %add.116), channel_id=1, source_target_pairs={{0,24},{1,25},{2,26},{3,27},{4,28},{5,29},{6,30},{7,31},{8,16},{9,... | collective-permute-start | bytes 24584 | tf_op jit(solution)/shard_map/ppermute | solution.py:578
  221.7 1.7 collective-permute-done.21
  223.4 1.0 collective-permute-start.22
  227.4 4.7 %collective-permute-done.23 = f32[16,128]{1,0:T(8,128)S(1)} collective-permute-done((f32[16,128]{1,0:T(8,128)S(1)}, f32[16,128]{1,0:T(8,128)S(1)}, u32[]{:S(2)}, u32[]{:S(2)}) %collective-permute-start.23) | collective-permute-done | bytes 8224 | tf_op jit(solution)/shard_map/ppermute | solution.py:578
  232.4 1.5 collective-permute-start.25
  234.2 2.1 collective-permute-done.24
  236.3 1.7 collective-permute-done.25
  238.0 1.2 collective-permute-done.26
  239.4 6.9 %reduce-scatter.2.cloned.1.call-done = bf16[1,144,1536]{2,1,0:T(8,128)(2,1)} async-done(((bf16[32,144,1536]{2,1,0:T(8,128)(2,1)}), bf16[1,144,1536]{2,1,0:T(8,128)(2,1)}) %reduce-scatter.2.cloned.1.call-update) | async-done | bytes 442384 | tf_op jit(solution)/shard_map/reduce_scatter | solution.py:702
  246.4 1.0 slice.94
  248.9 2.8 %collective-permute-start.27 = (bf16[80,1536]{1,0:T(8,128)(2,1)S(1)}, bf16[80,1536]{1,0:T(8,128)(2,1)S(1)}, u32[]{:S(2)}, u32[]{:S(2)}) collective-permute-start(bf16[80,1536]{1,0:T(8,128)(2,1)S(1)} %slice.94), channel_id=1, source_target_pairs={{0,96},{1,97},{2,98},{3,99},{4,100},{5,101},{6,102},{7,103},{8,104... | collective-permute-start | bytes 737288 | tf_op jit(solution)/shard_map/ppermute | solution.py:647
  252.5 1.5 fusion.4
  254.5 2.8 %collective-permute-done.29 = bf16[64,1536]{1,0:T(8,128)(2,1)S(1)} collective-permute-done((bf16[64,1536]{1,0:T(8,128)(2,1)S(1)}, bf16[64,1536]{1,0:T(8,128)(2,1)S(1)}, u32[]{:S(2)}, u32[]{:S(2)}) %collective-permute-start.29) | collective-permute-done | bytes 196640 | tf_op jit(solution)/shard_map/ppermute | solution.py:647
  258.4 6.0 %collective-permute-done.30 = bf16[64,1536]{1,0:T(8,128)(2,1)S(1)} collective-permute-done((bf16[64,1536]{1,0:T(8,128)(2,1)S(1)}, bf16[64,1536]{1,0:T(8,128)(2,1)S(1)}, u32[]{:S(2)}, u32[]{:S(2)}) %collective-permute-start.30) | collective-permute-done | bytes 196640 | tf_op jit(solution)/shard_map/ppermute | solution.py:647
  265.8 1.0 copy-done.8
  (137 shorter events, 14.8 us)
Async XLA Ops:
  7.2 78.7 %all-gather.2.cloned.1.call-start = ((), (), s32[]{:S(2)}) async-start(), calls=%async_computation.4 | async-start | bytes 12976128 | tf_op jit(solution)/shard_map/all_gather | solution.py:682
  9.2 9.4 %copy-start.1 = (bf16[768,512]{1,0:T(8,128)(2,1)S(1)}, bf16[768,512]{1,0:T(8,128)(2,1)}, u32[]{:S(2)}) copy-start(bf16[768,512]{1,0:T(8,128)(2,1)} %x_ref.3) | copy-start | bytes 2359300
  10.2 11.4 %copy-start.18 = (f32[10]{0:T(128)S(1)}, f32[10]{0:T(128)}, u32[]{:S(2)}) copy-start(f32[10]{0:T(128)} %param.18) | copy-start | bytes 124
  10.2 16.9 %copy-start.9 = (s32[6,512]{1,0:T(8,128)S(1)}, s32[6,512]{1,0:T(8,128)}, u32[]{:S(2)}) copy-start(s32[6,512]{1,0:T(8,128)} %param.14) | copy-start | bytes 36868
  10.2 17.5 %copy-start.15 = (s32[768]{0:T(1024)S(1)}, s32[768]{0:T(1024)}, u32[]{:S(2)}) copy-start(s32[768]{0:T(1024)} %param.19) | copy-start | bytes 9220
  10.2 28.0 %all-to-all-start = ((bf16[16,80,384]{2,1,0:T(8,128)(2,1)}), bf16[16,80,384]{2,1,0:T(8,128)(2,1)S(1)}, u32[]{:S(2)}, u32[]{:S(2)}) async-start(bf16[16,80,384]{2,1,0:T(8,128)(2,1)} %broadcast_in_dim.26), calls=%async_computation | async-start | bytes 1966080 | tf_op jit(solution)/shard_map/all_to_all | solution.py:610
  18.5 227.9 %reduce-scatter.2.cloned.1.call-start = ((), (), s32[]{:S(2)}) async-start(), calls=%async_computation.5 | async-start | bytes 14598144 | tf_op jit(solution)/shard_map/reduce_scatter | solution.py:702
  18.8 1.2 collective-permute-start
  20.1 3.6 %collective-permute-start.1 = (f32[8,128]{1,0:T(8,128)S(1)}, f32[8,128]{1,0:T(8,128)S(1)}, u32[]{:S(2)}, u32[]{:S(2)}) collective-permute-start(f32[8,128]{1,0:T(8,128)S(1)} %add.101), channel_id=1, source_target_pairs={{0,32},{1,33},{2,34},{3,35},{4,36},{5,37},{6,38},{7,39},{8,40},{9,... | collective-permute-start | bytes 12296 | tf_op jit(solution)/shard_map/ppermute | solution.py:578
  23.7 4.8 %collective-permute-start.2 = (f32[8,128]{1,0:T(8,128)S(1)}, f32[8,128]{1,0:T(8,128)S(1)}, u32[]{:S(2)}, u32[]{:S(2)}) collective-permute-start(f32[8,128]{1,0:T(8,128)S(1)} %add.102), channel_id=1, source_target_pairs={{0,96},{1,97},{2,98},{3,99},{4,100},{5,101},{6,102},{7,103},{8,104... | collective-permute-start | bytes 12296 | tf_op jit(solution)/shard_map/ppermute | solution.py:578
  38.2 21.5 %copy-start = (bf16[16,80,384]{2,1,0:T(8,128)(2,1)}, bf16[16,80,384]{2,1,0:T(8,128)(2,1)S(1)}, u32[]{:S(2)}) copy-start(bf16[16,80,384]{2,1,0:T(8,128)(2,1)S(1)} %all-to-all-done) | copy-start | bytes 2949124
  38.3 20.2 %collective-permute-start.3 = (bf16[4,4,64,384]{3,2,1,0:T(8,128)(2,1)S(1)}, bf16[4,4,64,384]{3,2,1,0:T(8,128)(2,1)S(1)}, u32[]{:S(2)}, u32[]{:S(2)}) collective-permute-start(bf16[4,4,64,384]{3,2,1,0:T(8,128)(2,1)S(1)} %slice.81), channel_id=1, source_target_pairs={{0,32},{1,33},{2,34},{3,35},{4,36},{5,37},{6,38},{7,39},{8,40},{9,... | collective-permute-start | bytes 2359304 | tf_op jit(solution)/shard_map/ppermute | solution.py:605
  40.0 18.6 %collective-permute-start.4 = (bf16[4,4,64,384]{3,2,1,0:T(8,128)(2,1)S(1)}, bf16[4,4,64,384]{3,2,1,0:T(8,128)(2,1)S(1)}, u32[]{:S(2)}, u32[]{:S(2)}) collective-permute-start(bf16[4,4,64,384]{3,2,1,0:T(8,128)(2,1)S(1)} %slice.81), channel_id=1, source_target_pairs={{0,96},{1,97},{2,98},{3,99},{4,100},{5,101},{6,102},{7,103},{8,104... | collective-permute-start | bytes 2359304 | tf_op jit(solution)/shard_map/ppermute | solution.py:605
  41.7 32.2 %collective-permute-start.9 = (bf16[4,4,80,384]{3,2,1,0:T(8,128)(2,1)S(1)}, bf16[4,4,80,384]{3,2,1,0:T(8,128)(2,1)S(1)}, u32[]{:S(2)}, u32[]{:S(2)}) collective-permute-start(bf16[4,4,80,384]{3,2,1,0:T(8,128)(2,1)S(1)} %bitcast.92), channel_id=1, source_target_pairs={{0,1},{1,0},{2,3},{3,2},{4,5},{5,4},{6,7},{7,6},{8,9},{9,8},{10,11... | collective-permute-start | bytes 2949128 | tf_op jit(solution)/shard_map/ppermute | solution.py:624
  41.7 3.6 %collective-permute-start.5 = (f32[8,128]{1,0:T(8,128)S(1)}, f32[8,128]{1,0:T(8,128)S(1)}, u32[]{:S(2)}, u32[]{:S(2)}) collective-permute-start(f32[8,128]{1,0:T(8,128)S(1)} %add.103), channel_id=1, source_target_pairs={{0,2},{1,3},{2,0},{3,1},{4,6},{5,7},{6,4},{7,5},{8,10},{9,11},{10,... | collective-permute-start | bytes 12296 | tf_op jit(solution)/shard_map/ppermute | solution.py:578
  45.3 4.8 %collective-permute-start.6 = (f32[8,128]{1,0:T(8,128)S(1)}, f32[8,128]{1,0:T(8,128)S(1)}, u32[]{:S(2)}, u32[]{:S(2)}) collective-permute-start(f32[8,128]{1,0:T(8,128)S(1)} %add.106), channel_id=1, source_target_pairs={{0,6},{1,7},{2,4},{3,5},{4,2},{5,3},{6,0},{7,1},{8,14},{9,15},{10,... | collective-permute-start | bytes 12296 | tf_op jit(solution)/shard_map/ppermute | solution.py:578
  50.1 3.6 %collective-permute-start.7 = (f32[8,128]{1,0:T(8,128)S(1)}, f32[8,128]{1,0:T(8,128)S(1)}, u32[]{:S(2)}, u32[]{:S(2)}) collective-permute-start(f32[8,128]{1,0:T(8,128)S(1)} %add.107), channel_id=1, source_target_pairs={{0,8},{1,9},{2,10},{3,11},{4,12},{5,13},{6,14},{7,15},{8,0},{9,1},... | collective-permute-start | bytes 12296 | tf_op jit(solution)/shard_map/ppermute | solution.py:578
  53.7 4.9 %collective-permute-start.8 = (f32[8,128]{1,0:T(8,128)S(1)}, f32[8,128]{1,0:T(8,128)S(1)}, u32[]{:S(2)}, u32[]{:S(2)}) collective-permute-start(f32[8,128]{1,0:T(8,128)S(1)} %add.108), channel_id=1, source_target_pairs={{0,24},{1,25},{2,26},{3,27},{4,28},{5,29},{6,30},{7,31},{8,16},{9,... | collective-permute-start | bytes 12296 | tf_op jit(solution)/shard_map/ppermute | solution.py:578
  58.6 15.8 %copy-start.4 = (bf16[4,4,64,384]{3,2,1,0:T(8,128)(2,1)}, bf16[4,4,64,384]{3,2,1,0:T(8,128)(2,1)S(1)}, u32[]{:S(2)}) copy-start(bf16[4,4,64,384]{3,2,1,0:T(8,128)(2,1)S(1)} %collective-permute-done.3.refs_2_) | copy-start | bytes 2359300
  58.6 15.8 %copy-start.5 = (bf16[4,4,64,384]{3,2,1,0:T(8,128)(2,1)}, bf16[4,4,64,384]{3,2,1,0:T(8,128)(2,1)S(1)}, u32[]{:S(2)}) copy-start(bf16[4,4,64,384]{3,2,1,0:T(8,128)(2,1)S(1)} %collective-permute-done.4.refs_4_) | copy-start | bytes 2359300
  58.6 15.2 %collective-permute-start.10 = (bf16[4,4,64,384]{3,2,1,0:T(8,128)(2,1)S(1)}, bf16[4,4,64,384]{3,2,1,0:T(8,128)(2,1)}, u32[]{:S(2)}, u32[]{:S(2)}) collective-permute-start(bf16[4,4,64,384]{3,2,1,0:T(8,128)(2,1)S(1)} %collective-permute-done.3.refs_2_), channel_id=1, source_target_pairs={{0,1},{1,0},{2,3},{3,2},{4,5},{5,4},{6,7},{7,6},{8,9},{9,8},{10,11... | collective-permute-start | bytes 2359304 | tf_op jit(solution)/shard_map/ppermute | solution.py:624
  58.8 15.1 %collective-permute-start.11 = (bf16[4,4,64,384]{3,2,1,0:T(8,128)(2,1)S(1)}, bf16[4,4,64,384]{3,2,1,0:T(8,128)(2,1)}, u32[]{:S(2)}, u32[]{:S(2)}) collective-permute-start(bf16[4,4,64,384]{3,2,1,0:T(8,128)(2,1)S(1)} %collective-permute-done.4.refs_4_), channel_id=1, source_target_pairs={{0,1},{1,0},{2,3},{3,2},{4,5},{5,4},{6,7},{7,6},{8,9},{9,8},{10,11... | collective-permute-start | bytes 2359304 | tf_op jit(solution)/shard_map/ppermute | solution.py:624
  59.3 12.4 %collective-permute-start.12 = (bf16[2,4,64,384]{3,2,1,0:T(8,128)(2,1)S(1)}, bf16[2,4,64,384]{3,2,1,0:T(8,128)(2,1)}, u32[]{:S(2)}, u32[]{:S(2)}) collective-permute-start(bf16[2,4,64,384]{3,2,1,0:T(8,128)(2,1)S(1)} %slice.84), channel_id=1, source_target_pairs={{0,32},{1,33},{2,34},{3,35},{4,36},{5,37},{6,38},{7,39},{8,40},{9,... | collective-permute-start | bytes 1179656 | tf_op jit(solution)/shard_map/ppermute | solution.py:605
  59.7 12.0 %collective-permute-start.14 = (bf16[2,4,64,384]{3,2,1,0:T(8,128)(2,1)S(1)}, bf16[2,4,64,384]{3,2,1,0:T(8,128)(2,1)}, u32[]{:S(2)}, u32[]{:S(2)}) collective-permute-start(bf16[2,4,64,384]{3,2,1,0:T(8,128)(2,1)S(1)} %slice.85), channel_id=1, source_target_pairs={{0,96},{1,97},{2,98},{3,99},{4,100},{5,101},{6,102},{7,103},{8,104... | collective-permute-start | bytes 1179656 | tf_op jit(solution)/shard_map/ppermute | solution.py:605
  71.7 2.1 collective-permute-start.13
  71.8 2.6 collective-permute-start.15
  147.4 6.7 %collective-permute-start.16 = (bf16[4,16,64,384]{3,2,1,0:T(8,128)(2,1)}, bf16[4,16,64,384]{3,2,1,0:T(8,128)(2,1)S(1)}, u32[]{:S(2)}, u32[]{:S(2)}) collective-permute-start(bf16[4,16,64,384]{3,2,1,0:T(8,128)(2,1)} %get-tuple-element.64), channel_id=1, source_target_pairs={{0,1},{1,0},{2,3},{3,2},{4,5},{5,4},{6,7},{7,6},{8,9},{9,8},{10,11... | collective-permute-start | bytes 9437192 | tf_op jit(solution)/shard_map/ppermute | solution.py:706
  158.9 42.6 %all-to-all-start.1 = ((bf16[4,16,64,384]{3,2,1,0:T(8,128)(2,1)}), bf16[4,16,64,384]{3,2,1,0:T(8,128)(2,1)S(1)}, u32[]{:S(2)}, u32[]{:S(2)}) async-start(bf16[4,16,64,384]{3,2,1,0:T(8,128)(2,1)} %add_convert_fusion), calls=%async_computation.1 | async-start | bytes 6291456 | tf_op jit(solution)/shard_map/all_to_all | solution.py:629
  163.6 1.3 collective-permute-start.17
  164.9 3.7 %collective-permute-start.18 = (f32[16,128]{1,0:T(8,128)S(1)}, f32[16,128]{1,0:T(8,128)S(1)}, u32[]{:S(2)}, u32[]{:S(2)}) collective-permute-start(f32[16,128]{1,0:T(8,128)S(1)} %fusion.12), channel_id=1, source_target_pairs={{0,2},{1,3},{2,0},{3,1},{4,6},{5,7},{6,4},{7,5},{8,10},{9,11},{10,... | collective-permute-start | bytes 24584 | tf_op jit(solution)/shard_map/ppermute | solution.py:578
  168.6 4.9 %collective-permute-start.19 = (f32[16,128]{1,0:T(8,128)S(1)}, f32[16,128]{1,0:T(8,128)S(1)}, u32[]{:S(2)}, u32[]{:S(2)}) collective-permute-start(f32[16,128]{1,0:T(8,128)S(1)} %fusion.15), channel_id=1, source_target_pairs={{0,6},{1,7},{2,4},{3,5},{4,2},{5,3},{6,0},{7,1},{8,14},{9,15},{10,... | collective-permute-start | bytes 24584 | tf_op jit(solution)/shard_map/ppermute | solution.py:578
  203.0 21.3 %copy-start.11 = (s32[4]{0:T(128)S(1)}, s32[4]{0:T(128)}, u32[]{:S(2)}) copy-start(s32[4]{0:T(128)} %pad_add_fusion.1.place_ref) | copy-start | bytes 52
  203.0 24.3 %copy-start.12 = (f32[512]{0:T(512)S(1)}, f32[512]{0:T(512)}, u32[]{:S(2)}) copy-start(f32[512]{0:T(512)} %param.11) | copy-start | bytes 6148
  203.1 29.0 %all-to-all-start.2 = ((bf16[16,64,384]{2,1,0:T(8,128)(2,1)}), bf16[16,64,384]{2,1,0:T(8,128)(2,1)S(1)}, u32[]{:S(2)}, u32[]{:S(2)}) async-start(bf16[16,64,384]{2,1,0:T(8,128)(2,1)} %reduce_sum.44), calls=%async_computation.2 | async-start | bytes 1572864 | tf_op jit(solution)/shard_map/all_to_all | solution.py:634
  207.0 10.8 %collective-permute-start.20 = (f32[16,128]{1,0:T(8,128)S(1)}, f32[16,128]{1,0:T(8,128)S(1)}, u32[]{:S(2)}, u32[]{:S(2)}) collective-permute-start(f32[16,128]{1,0:T(8,128)S(1)} %add.115), channel_id=1, source_target_pairs={{0,8},{1,9},{2,10},{3,11},{4,12},{5,13},{6,14},{7,15},{8,0},{9,1},... | collective-permute-start | bytes 24584 | tf_op jit(solution)/shard_map/ppermute | solution.py:578
  217.8 5.6 %collective-permute-start.21 = (f32[16,128]{1,0:T(8,128)S(1)}, f32[16,128]{1,0:T(8,128)S(1)}, u32[]{:S(2)}, u32[]{:S(2)}) collective-permute-start(f32[16,128]{1,0:T(8,128)S(1)} %add.116), channel_id=1, source_target_pairs={{0,24},{1,25},{2,26},{3,27},{4,28},{5,29},{6,30},{7,31},{8,16},{9,... | collective-permute-start | bytes 24584 | tf_op jit(solution)/shard_map/ppermute | solution.py:578
  223.4 3.7 %collective-permute-start.22 = (f32[16,128]{1,0:T(8,128)S(1)}, f32[16,128]{1,0:T(8,128)S(1)}, u32[]{:S(2)}, u32[]{:S(2)}) collective-permute-start(f32[16,128]{1,0:T(8,128)S(1)} %add.117), channel_id=1, source_target_pairs={{0,32},{1,33},{2,34},{3,35},{4,36},{5,37},{6,38},{7,39},{8,40},{9,... | collective-permute-start | bytes 24584 | tf_op jit(solution)/shard_map/ppermute | solution.py:578
  227.1 4.9 %collective-permute-start.23 = (f32[16,128]{1,0:T(8,128)S(1)}, f32[16,128]{1,0:T(8,128)S(1)}, u32[]{:S(2)}, u32[]{:S(2)}) collective-permute-start(f32[16,128]{1,0:T(8,128)S(1)} %add.118), channel_id=1, source_target_pairs={{0,96},{1,97},{2,98},{3,99},{4,100},{5,101},{6,102},{7,103},{8,104... | collective-permute-start | bytes 24584 | tf_op jit(solution)/shard_map/ppermute | solution.py:578
  232.1 4.2 %collective-permute-start.24 = (bf16[64,384]{1,0:T(8,128)(2,1)S(1)}, bf16[64,384]{1,0:T(8,128)(2,1)S(1)}, u32[]{:S(2)}, u32[]{:S(2)}) collective-permute-start(bf16[64,384]{1,0:T(8,128)(2,1)S(1)} %reduce_sum.45), channel_id=1, source_target_pairs={{0,96},{1,97},{2,98},{3,99},{4,100},{5,101},{6,102},{7,103},{8,104... | collective-permute-start | bytes 147464 | tf_op jit(solution)/shard_map/ppermute | solution.py:641
  232.4 5.6 %collective-permute-start.25 = (bf16[64,384]{1,0:T(8,128)(2,1)S(1)}, bf16[64,384]{1,0:T(8,128)(2,1)S(1)}, u32[]{:S(2)}, u32[]{:S(2)}) collective-permute-start(bf16[64,384]{1,0:T(8,128)(2,1)S(1)} %reduce_sum.45), channel_id=1, source_target_pairs={{0,64},{1,65},{2,66},{3,67},{4,68},{5,69},{6,70},{7,71},{8,72},{9,... | collective-permute-start | bytes 147464 | tf_op jit(solution)/shard_map/ppermute | solution.py:641
  233.9 5.3 %collective-permute-start.26 = (bf16[64,384]{1,0:T(8,128)(2,1)S(1)}, bf16[64,384]{1,0:T(8,128)(2,1)S(1)}, u32[]{:S(2)}, u32[]{:S(2)}) collective-permute-start(bf16[64,384]{1,0:T(8,128)(2,1)S(1)} %reduce_sum.45), channel_id=1, source_target_pairs={{0,32},{1,33},{2,34},{3,35},{4,36},{5,37},{6,38},{7,39},{8,40},{9,... | collective-permute-start | bytes 147464 | tf_op jit(solution)/shard_map/ppermute | solution.py:641
  239.2 13.2 %copy-start.2 = (bf16[768,512]{1,0:T(8,128)(2,1)S(1)}, bf16[768,512]{1,0:T(8,128)(2,1)}, u32[]{:S(2)}) copy-start(bf16[768,512]{1,0:T(8,128)(2,1)} %x_ref.3) | copy-start | bytes 2359300
  239.3 13.2 %copy-start.7 = (f32[768,512]{1,0:T(8,128)S(1)}, f32[768,512]{1,0:T(8,128)}, u32[]{:S(2)}) copy-start(f32[768,512]{1,0:T(8,128)} %get-tuple-element.62) | copy-start | bytes 4718596
  248.9 9.1 %collective-permute-start.27 = (bf16[80,1536]{1,0:T(8,128)(2,1)S(1)}, bf16[80,1536]{1,0:T(8,128)(2,1)S(1)}, u32[]{:S(2)}, u32[]{:S(2)}) collective-permute-start(bf16[80,1536]{1,0:T(8,128)(2,1)S(1)} %slice.94), channel_id=1, source_target_pairs={{0,96},{1,97},{2,98},{3,99},{4,100},{5,101},{6,102},{7,103},{8,104... | collective-permute-start | bytes 737288 | tf_op jit(solution)/shard_map/ppermute | solution.py:647
  251.7 5.7 %collective-permute-start.29 = (bf16[64,1536]{1,0:T(8,128)(2,1)S(1)}, bf16[64,1536]{1,0:T(8,128)(2,1)S(1)}, u32[]{:S(2)}, u32[]{:S(2)}) collective-permute-start(bf16[64,1536]{1,0:T(8,128)(2,1)S(1)} %slice.97), channel_id=1, source_target_pairs={{0,32},{1,33},{2,34},{3,35},{4,36},{5,37},{6,38},{7,39},{8,40},{9,... | collective-permute-start | bytes 589832 | tf_op jit(solution)/shard_map/ppermute | solution.py:647
  252.5 4.9 %copy-start.6 = (bf16[1,144,1536]{2,1,0:T(8,128)(2,1)S(1)}, bf16[1,144,1536]{2,1,0:T(8,128)(2,1)}, u32[]{:S(2)}) copy-start(bf16[1,144,1536]{2,1,0:T(8,128)(2,1)} %reduce-scatter.2.cloned.1.call-done) | copy-start | bytes 1327108
  257.4 7.0 %collective-permute-start.30 = (bf16[64,1536]{1,0:T(8,128)(2,1)S(1)}, bf16[64,1536]{1,0:T(8,128)(2,1)S(1)}, u32[]{:S(2)}, u32[]{:S(2)}) collective-permute-start(bf16[64,1536]{1,0:T(8,128)(2,1)S(1)} %add_convert_fusion.2), channel_id=1, source_target_pairs={{0,96},{1,97},{2,98},{3,99},{4,100},{5,101},{6,102},{7,103},{8,104... | collective-permute-start | bytes 589832 | tf_op jit(solution)/shard_map/ppermute | solution.py:647
  258.1 6.3 %collective-permute-start.28 = (bf16[80,1536]{1,0:T(8,128)(2,1)S(1)}, bf16[80,1536]{1,0:T(8,128)(2,1)S(1)}, u32[]{:S(2)}, u32[]{:S(2)}) collective-permute-start(bf16[80,1536]{1,0:T(8,128)(2,1)S(1)} %add_convert_fusion.1), channel_id=1, source_target_pairs={{0,32},{1,33},{2,34},{3,35},{4,36},{5,37},{6,38},{7,39},{8,40},{9,... | collective-permute-start | bytes 737288 | tf_op jit(solution)/shard_map/ppermute | solution.py:647
  (8 other events, 21.9 us)
Sparse Core Ops, SparseCore 0:
  10.3 70.8 all-gather.1
  127.9 118.4 reduce-scatter.1

commit v4 on v3

--- a/solution.py
+++ b/solution.py
@@ -12,7 +12,7 @@
 epsilon = 1e-05
 F32 = jnp.float32
 BF16 = jnp.bfloat16
-VMEM_LIMIT = 60 * 1024 * 1024
+MIB = 1024 * 1024
 HEAD_ROWS = 16
 OPENING = 4
 QUARTERS = ((0, 0, 4), (1, 0, 4), (3, 0, 4), (2, 0, 2), (2, 2, 4))
@@ -256,7 +256,7 @@
     return pl.pallas_call(
         functools.partial(entry_kernel, total_rows),
         in_specs=[pl.BlockSpec(memory_space=pltpu.SMEM)] + [inside] * 5 + [anywhere] * PIECES,
-        out_specs=[anywhere] * 8,
+        out_specs=[pl.BlockSpec(memory_space=pltpu.HBM)] * 8,
         out_shape=[
             jax.ShapeDtypeStruct((count, rows, width), kind) for kind in (F32, BF16, BF16, BF16)
         ]
@@ -277,7 +277,7 @@
             pltpu.SemaphoreType.DMA((count, 5)),
             pltpu.SemaphoreType.DMA((3,)),
         ],
-        compiler_params=pltpu.CompilerParams(vmem_limit_bytes=VMEM_LIMIT),
+        compiler_params=pltpu.CompilerParams(vmem_limit_bytes=55 * MIB),
         name="first_sections",
     )(place, features, stats, gain, bias, masks, *pieces)
 
@@ -421,7 +421,7 @@
             pltpu.SemaphoreType.DMA((5,)),
             pltpu.SemaphoreType.DMA((3,)),
         ],
-        compiler_params=pltpu.CompilerParams(vmem_limit_bytes=VMEM_LIMIT),
+        compiler_params=pltpu.CompilerParams(vmem_limit_bytes=60 * MIB),
         name="sections_and_head",
     )(place, masks, b1, b2, labels, weights, state, low, turned, *heads)
 
@@ -558,7 +558,7 @@
             pltpu.SemaphoreType.DMA((2, 2, 4)),
             pltpu.SemaphoreType.DMA((1,)),
         ],
-        compiler_params=pltpu.CompilerParams(vmem_limit_bytes=VMEM_LIMIT),
+        compiler_params=pltpu.CompilerParams(vmem_limit_bytes=60 * MIB),
         name="sections_backward",
     )(place, masks, features, stats, *saved, weights, turned, grad_state, grad_scaled)
 

time: 274 us -> 274 us (level)
  no operation moved by 1% of the time
where the time goes in v4:
time: 274 us
  waiting for transfers between devices  118 us (43%)
  Pallas kernels  72.5 us (26%)
  starting transfers between devices  45.2 us (16%)
  between operations  15.8 us (6%)
  local copies, waits for them, and re-layouts  12.3 us (4%)
  other arithmetic  9.85 us (4%)
    ppermute x14, waiting for transfers between devices, everywhere_sum(): value = value + lax.ppermute(value, names, pairs(sizes, axis, flip))  43.5 us
    pallas_call x1, Pallas kernels, run_upper(): pl.pallas_call(functools.partial(upper_kernel, 1.0 / rows, classes), in_s...  41.8 us
    all_to_all x1, waiting for transfers between devices, column_scatter(): got = lax.all_to_all(total, 'dp', 0, 0)  27.9 us
    pallas_call x1, Pallas kernels, run_lower(): pl.pallas_call(functools.partial(lower_kernel, total_rows), in_specs=[pl....  19.6 us
    ppermute x14, starting transfers between devices, everywhere_sum(): value = value + lax.ppermute(value, names, pairs(sizes, axis, flip))  14.2 us
    pallas_call x1, Pallas kernels, run_entry(): pl.pallas_call(functools.partial(entry_kernel, total_rows), in_specs=[pl....  11.1 us
    all_to_all x1, waiting for transfers between devices, quarter_gather(): lax.all_to_all(jnp.broadcast_to(own[None], (count, *own.shape)), 'fsdp',...  9.71 us
    ppermute x4, waiting for transfers between devices, quarter_gather(): lax.ppermute(value, names, shifted(sizes, axis, by))  9.07 us
  transfers between devices with their start and end apart: 36, of which 25 were waited for; matrix products, arithmetic and copies ran while one was open for 5% of the time, Pallas kernels for 11%

profile of v4, /device:TPU:0, one launch (start us, length us, event | category | flops | bytes accessed | tf_op | source)
XLA Modules:
  0.0 273.6 jit_solution(11965632482052686821)
XLA Ops:
  7.2 1.8 slice.86
  9.2 1.0 broadcast_in_dim.26
  10.2 8.3 %all-to-all-start = ((bf16[16,80,384]{2,1,0:T(8,128)(2,1)}), bf16[16,80,384]{2,1,0:T(8,128)(2,1)S(1)}, u32[]{:S(2)}, u32[]{:S(2)}) async-start(bf16[16,80,384]{2,1,0:T(8,128)(2,1)} %broadcast_in_dim.26), calls=%async_computation | async-start | bytes 1966080 | tf_op jit(solution)/shard_map/all_to_all | solution.py:610
  18.9 1.2 collective-permute-done
  20.1 1.5 collective-permute-start.1
  22.2 1.5 collective-permute-done.1
  23.7 2.8 %collective-permute-start.2 = (f32[8,128]{1,0:T(8,128)S(1)}, f32[8,128]{1,0:T(8,128)S(1)}, u32[]{:S(2)}, u32[]{:S(2)}) collective-permute-start(f32[8,128]{1,0:T(8,128)S(1)} %add.102), channel_id=1, source_target_pairs={{0,96},{1,97},{2,98},{3,99},{4,100},{5,101},{6,102},{7,103},{8,104... | collective-permute-start | bytes 12296 | tf_op jit(solution)/shard_map/ppermute | solution.py:578
  28.5 9.7 %all-to-all-done = bf16[16,80,384]{2,1,0:T(8,128)(2,1)S(1)} async-done(((bf16[16,80,384]{2,1,0:T(8,128)(2,1)}), bf16[16,80,384]{2,1,0:T(8,128)(2,1)S(1)}, u32[]{:S(2)}, u32[]{:S(2)}) %all-to-all-start) | async-done | bytes 983072 | tf_op jit(solution)/shard_map/all_to_all | solution.py:610
  38.3 1.6 collective-permute-start.3
  40.0 1.7 collective-permute-start.4
  41.7 1.5 collective-permute-start.5
  43.2 2.1 collective-permute-done.5
  45.3 4.8 %collective-permute-done.6 = f32[8,128]{1,0:T(8,128)S(1)} collective-permute-done((f32[8,128]{1,0:T(8,128)S(1)}, f32[8,128]{1,0:T(8,128)S(1)}, u32[]{:S(2)}, u32[]{:S(2)}) %collective-permute-start.6) | collective-permute-done | bytes 4128 | tf_op jit(solution)/shard_map/ppermute | solution.py:578
  50.1 3.6 %collective-permute-done.7 = f32[8,128]{1,0:T(8,128)S(1)} collective-permute-done((f32[8,128]{1,0:T(8,128)S(1)}, f32[8,128]{1,0:T(8,128)S(1)}, u32[]{:S(2)}, u32[]{:S(2)}) %collective-permute-start.7) | collective-permute-done | bytes 4128 | tf_op jit(solution)/shard_map/ppermute | solution.py:578
  53.7 1.0 collective-permute-start.8
  54.7 3.9 %collective-permute-done.8 = f32[8,128]{1,0:T(8,128)S(1)} collective-permute-done((f32[8,128]{1,0:T(8,128)S(1)}, f32[8,128]{1,0:T(8,128)S(1)}, u32[]{:S(2)}, u32[]{:S(2)}) %collective-permute-start.8) | collective-permute-done | bytes 4128 | tf_op jit(solution)/shard_map/ppermute | solution.py:578
  59.7 2.9 %collective-permute-start.14 = (bf16[2,4,64,384]{3,2,1,0:T(8,128)(2,1)S(1)}, bf16[2,4,64,384]{3,2,1,0:T(8,128)(2,1)}, u32[]{:S(2)}, u32[]{:S(2)}) collective-permute-start(bf16[2,4,64,384]{3,2,1,0:T(8,128)(2,1)S(1)} %slice.85), channel_id=1, source_target_pairs={{0,96},{1,97},{2,98},{3,99},{4,100},{5,101},{6,102},{7,103},{8,104... | collective-permute-start | bytes 1179656 | tf_op jit(solution)/shard_map/ppermute | solution.py:605
  62.7 9.1 %collective-permute-done.12.refs_6_ = bf16[2,4,64,384]{3,2,1,0:T(8,128)(2,1)} collective-permute-done((bf16[2,4,64,384]{3,2,1,0:T(8,128)(2,1)S(1)}, bf16[2,4,64,384]{3,2,1,0:T(8,128)(2,1)}, u32[]{:S(2)}, u32[]{:S(2)}) %collective-permute-start.12) | collective-permute-done | bytes 393248 | tf_op jit(solution)/shard_map/ppermute | solution.py:605
  72.3 1.0 copy.20.label_ref
  74.8 11.1 %first_sections.1 = (f32[2,768,512]{2,1,0:T(8,128)}, bf16[2,768,512]{2,1,0:T(8,128)(2,1)}, bf16[2,768,512]{2,1,0:T(8,128)(2,1)}, bf16[2,768,512]{2,1,0:T(8,128)(...) custom-call(s32[4]{0:T(128)} %pad_add_fusion.1.place_ref, ...), custom_call_target="tpu_custom_call" | custom-call | tf_op jit(solution)/shard_map/first_sections/pallas_call | solution.py:256
  85.9 41.8 %sections_and_head.1 = (f32[768,512]{1,0:T(8,128)}, f32[768,512]{1,0:T(8,128)}, bf16[16,2,144,1536]{3,2,1,0:T(8,128)(2,1)}, f32[1,256]{1,0:T(1,128)}, f32[1,128]{1,0:T(1,128)}) custom-call(s32[4]{0:T(128)} %pad_add_fusion.1.place_ref, f32[6,1,512]{2,1,0:T(1,128)} %broadcast_in_dim.27.mask_ref, f32[1,256]{1,0:T(1,128)} %bitcast.119, ...), custom_call_target="tpu_custom_call" | custom-call | tf_op jit(solution)/shard_map/sections_and_head/pallas_call | solution.py:395
  127.8 19.6 %sections_backward.1 = (bf16[4,16,64,384]{3,2,1,0:T(8,128)(2,1)}, bf16[4,16,64,384]{3,2,1,0:T(8,128)(2,1)}, f32[768,512]{1,0:T(8,128)}, f32[2,512]{1,0:T(2,128)}) custom-call(s32[4]{0:T(128)} %pad_add_fusion.1.place_ref, f32[6,1,512]{2,1,0:T(1,128)} %broadcast_in_dim.27.mask_ref, bf16[768,512]{1,0:T(8,128)(2,1)} %x_ref.3, f32[2,512]{1,0:T(2,128)} %reshape.100.stat_ref, ...), custom_call_target="tpu_custom_call" | custom-call | tf_op jit(solution)/shard_map/sections_backward/pallas_call | solution.py:536
  147.6 6.4 %collective-permute-done.16 = bf16[4,16,64,384]{3,2,1,0:T(8,128)(2,1)S(1)} collective-permute-done((bf16[4,16,64,384]{3,2,1,0:T(8,128)(2,1)}, bf16[4,16,64,384]{3,2,1,0:T(8,128)(2,1)S(1)}, u32[]{:S(2)}, u32[]{:S(2)}) %collective-permute-start.16) | collective-permute-done | bytes 3145760 | tf_op jit(solution)/shard_map/ppermute | solution.py:706
  154.1 4.8 %add_convert_fusion = bf16[4,16,64,384]{3,2,1,0:T(8,128)(2,1)} fusion(bf16[4,16,64,384]{3,2,1,0:T(8,128)(2,1)S(1)} %collective-permute-done.16, bf16[4,16,64,384]{3,2,1,0:T(8,128)(2,1)} %get-tuple-element.63), kind=kLoop, calls=%fused_computation | loop fusion | flops 6291456 | bytes 9437184 | tf_op jit(solution)/shard_map/convert_element_type | solution.py:706
  158.9 4.7 %all-to-all-start.1 = ((bf16[4,16,64,384]{3,2,1,0:T(8,128)(2,1)}), bf16[4,16,64,384]{3,2,1,0:T(8,128)(2,1)S(1)}, u32[]{:S(2)}, u32[]{:S(2)}) async-start(bf16[4,16,64,384]{3,2,1,0:T(8,128)(2,1)} %add_convert_fusion), calls=%async_computation.1 | async-start | bytes 6291456 | tf_op jit(solution)/shard_map/all_to_all | solution.py:629
  163.7 1.2 collective-permute-done.17
  164.9 3.6 %collective-permute-done.18 = f32[16,128]{1,0:T(8,128)S(1)} collective-permute-done((f32[16,128]{1,0:T(8,128)S(1)}, f32[16,128]{1,0:T(8,128)S(1)}, u32[]{:S(2)}, u32[]{:S(2)}) %collective-permute-start.18) | collective-permute-done | bytes 8224 | tf_op jit(solution)/shard_map/ppermute | solution.py:578
  168.7 4.8 %collective-permute-done.19 = f32[16,128]{1,0:T(8,128)S(1)} collective-permute-done((f32[16,128]{1,0:T(8,128)S(1)}, f32[16,128]{1,0:T(8,128)S(1)}, u32[]{:S(2)}, u32[]{:S(2)}) %collective-permute-start.19) | collective-permute-done | bytes 8224 | tf_op jit(solution)/shard_map/ppermute | solution.py:578
  173.5 27.9 %all-to-all-done.1 = bf16[4,16,64,384]{3,2,1,0:T(8,128)(2,1)S(1)} async-done(((bf16[4,16,64,384]{3,2,1,0:T(8,128)(2,1)}), bf16[4,16,64,384]{3,2,1,0:T(8,128)(2,1)S(1)}, u32[]{:S(2)}, u32[]{:S(2)}) %all-to-all-start.1) | async-done | bytes 3145760 | tf_op jit(solution)/shard_map/all_to_all | solution.py:629
  201.4 1.6 reduce_sum.44
  203.1 3.9 %all-to-all-start.2 = ((bf16[16,64,384]{2,1,0:T(8,128)(2,1)}), bf16[16,64,384]{2,1,0:T(8,128)(2,1)S(1)}, u32[]{:S(2)}, u32[]{:S(2)}) async-start(bf16[16,64,384]{2,1,0:T(8,128)(2,1)} %reduce_sum.44), calls=%async_computation.2 | async-start | bytes 1572864 | tf_op jit(solution)/shard_map/all_to_all | solution.py:634
  207.0 1.9 collective-permute-start.20
  208.9 8.8 %collective-permute-done.20 = f32[16,128]{1,0:T(8,128)S(1)} collective-permute-done((f32[16,128]{1,0:T(8,128)S(1)}, f32[16,128]{1,0:T(8,128)S(1)}, u32[]{:S(2)}, u32[]{:S(2)}) %collective-permute-start.20) | collective-permute-done | bytes 8224 | tf_op jit(solution)/shard_map/ppermute | solution.py:578
  217.8 3.9 %collective-permute-start.21 = (f32[16,128]{1,0:T(8,128)S(1)}, f32[16,128]{1,0:T(8,128)S(1)}, u32[]{:S(2)}, u32[]{:S(2)}) collective-permute-start(f32[16,128]{1,0:T(8,128)S(1)} %add.116), channel_id=1, source_target_pairs={{0,24},{1,25},{2,26},{3,27},{4,28},{5,29},{6,30},{7,31},{8,16},{9,... | collective-permute-start | bytes 24584 | tf_op jit(solution)/shard_map/ppermute | solution.py:578
  221.7 1.7 collective-permute-done.21
  223.4 1.0 collective-permute-start.22
  227.4 4.7 %collective-permute-done.23 = f32[16,128]{1,0:T(8,128)S(1)} collective-permute-done((f32[16,128]{1,0:T(8,128)S(1)}, f32[16,128]{1,0:T(8,128)S(1)}, u32[]{:S(2)}, u32[]{:S(2)}) %collective-permute-start.23) | collective-permute-done | bytes 8224 | tf_op jit(solution)/shard_map/ppermute | solution.py:578
  232.4 1.5 collective-permute-start.25
  234.2 2.1 collective-permute-done.24
  236.3 1.7 collective-permute-done.25
  238.0 1.2 collective-permute-done.26
  239.4 6.9 %reduce-scatter.2.cloned.1.call-done = bf16[1,144,1536]{2,1,0:T(8,128)(2,1)} async-done(((bf16[32,144,1536]{2,1,0:T(8,128)(2,1)}), bf16[1,144,1536]{2,1,0:T(8,128)(2,1)}) %reduce-scatter.2.cloned.1.call-update) | async-done | bytes 442384 | tf_op jit(solution)/shard_map/reduce_scatter | solution.py:702
  246.4 1.0 slice.94
  248.9 2.8 %collective-permute-start.27 = (bf16[80,1536]{1,0:T(8,128)(2,1)S(1)}, bf16[80,1536]{1,0:T(8,128)(2,1)S(1)}, u32[]{:S(2)}, u32[]{:S(2)}) collective-permute-start(bf16[80,1536]{1,0:T(8,128)(2,1)S(1)} %slice.94), channel_id=1, source_target_pairs={{0,96},{1,97},{2,98},{3,99},{4,100},{5,101},{6,102},{7,103},{8,104... | collective-permute-start | bytes 737288 | tf_op jit(solution)/shard_map/ppermute | solution.py:647
  252.5 1.5 fusion.4
  254.5 2.8 %collective-permute-done.29 = bf16[64,1536]{1,0:T(8,128)(2,1)S(1)} collective-permute-done((bf16[64,1536]{1,0:T(8,128)(2,1)S(1)}, bf16[64,1536]{1,0:T(8,128)(2,1)S(1)}, u32[]{:S(2)}, u32[]{:S(2)}) %collective-permute-start.29) | collective-permute-done | bytes 196640 | tf_op jit(solution)/shard_map/ppermute | solution.py:647
  258.4 6.0 %collective-permute-done.30 = bf16[64,1536]{1,0:T(8,128)(2,1)S(1)} collective-permute-done((bf16[64,1536]{1,0:T(8,128)(2,1)S(1)}, bf16[64,1536]{1,0:T(8,128)(2,1)S(1)}, u32[]{:S(2)}, u32[]{:S(2)}) %collective-permute-start.30) | collective-permute-done | bytes 196640 | tf_op jit(solution)/shard_map/ppermute | solution.py:647
  265.8 1.0 copy-done.8
  (137 shorter events, 14.8 us)
Async XLA Ops:
  7.2 78.7 %all-gather.2.cloned.1.call-start = ((), (), s32[]{:S(2)}) async-start(), calls=%async_computation.4 | async-start | bytes 12976128 | tf_op jit(solution)/shard_map/all_gather | solution.py:682
  9.2 9.4 %copy-start.1 = (bf16[768,512]{1,0:T(8,128)(2,1)S(1)}, bf16[768,512]{1,0:T(8,128)(2,1)}, u32[]{:S(2)}) copy-start(bf16[768,512]{1,0:T(8,128)(2,1)} %x_ref.3) | copy-start | bytes 2359300
  10.2 11.4 %copy-start.18 = (f32[10]{0:T(128)S(1)}, f32[10]{0:T(128)}, u32[]{:S(2)}) copy-start(f32[10]{0:T(128)} %param.18) | copy-start | bytes 124
  10.2 16.9 %copy-start.9 = (s32[6,512]{1,0:T(8,128)S(1)}, s32[6,512]{1,0:T(8,128)}, u32[]{:S(2)}) copy-start(s32[6,512]{1,0:T(8,128)} %param.14) | copy-start | bytes 36868
  10.2 17.5 %copy-start.15 = (s32[768]{0:T(1024)S(1)}, s32[768]{0:T(1024)}, u32[]{:S(2)}) copy-start(s32[768]{0:T(1024)} %param.19) | copy-start | bytes 9220
  10.2 28.0 %all-to-all-start = ((bf16[16,80,384]{2,1,0:T(8,128)(2,1)}), bf16[16,80,384]{2,1,0:T(8,128)(2,1)S(1)}, u32[]{:S(2)}, u32[]{:S(2)}) async-start(bf16[16,80,384]{2,1,0:T(8,128)(2,1)} %broadcast_in_dim.26), calls=%async_computation | async-start | bytes 1966080 | tf_op jit(solution)/shard_map/all_to_all | solution.py:610
  18.5 227.9 %reduce-scatter.2.cloned.1.call-start = ((), (), s32[]{:S(2)}) async-start(), calls=%async_computation.5 | async-start | bytes 14598144 | tf_op jit(solution)/shard_map/reduce_scatter | solution.py:702
  18.8 1.2 collective-permute-start
  20.1 3.6 %collective-permute-start.1 = (f32[8,128]{1,0:T(8,128)S(1)}, f32[8,128]{1,0:T(8,128)S(1)}, u32[]{:S(2)}, u32[]{:S(2)}) collective-permute-start(f32[8,128]{1,0:T(8,128)S(1)} %add.101), channel_id=1, source_target_pairs={{0,32},{1,33},{2,34},{3,35},{4,36},{5,37},{6,38},{7,39},{8,40},{9,... | collective-permute-start | bytes 12296 | tf_op jit(solution)/shard_map/ppermute | solution.py:578
  23.7 4.8 %collective-permute-start.2 = (f32[8,128]{1,0:T(8,128)S(1)}, f32[8,128]{1,0:T(8,128)S(1)}, u32[]{:S(2)}, u32[]{:S(2)}) collective-permute-start(f32[8,128]{1,0:T(8,128)S(1)} %add.102), channel_id=1, source_target_pairs={{0,96},{1,97},{2,98},{3,99},{4,100},{5,101},{6,102},{7,103},{8,104... | collective-permute-start | bytes 12296 | tf_op jit(solution)/shard_map/ppermute | solution.py:578
  38.2 21.5 %copy-start = (bf16[16,80,384]{2,1,0:T(8,128)(2,1)}, bf16[16,80,384]{2,1,0:T(8,128)(2,1)S(1)}, u32[]{:S(2)}) copy-start(bf16[16,80,384]{2,1,0:T(8,128)(2,1)S(1)} %all-to-all-done) | copy-start | bytes 2949124
  38.3 20.2 %collective-permute-start.3 = (bf16[4,4,64,384]{3,2,1,0:T(8,128)(2,1)S(1)}, bf16[4,4,64,384]{3,2,1,0:T(8,128)(2,1)S(1)}, u32[]{:S(2)}, u32[]{:S(2)}) collective-permute-start(bf16[4,4,64,384]{3,2,1,0:T(8,128)(2,1)S(1)} %slice.81), channel_id=1, source_target_pairs={{0,32},{1,33},{2,34},{3,35},{4,36},{5,37},{6,38},{7,39},{8,40},{9,... | collective-permute-start | bytes 2359304 | tf_op jit(solution)/shard_map/ppermute | solution.py:605
  40.0 18.6 %collective-permute-start.4 = (bf16[4,4,64,384]{3,2,1,0:T(8,128)(2,1)S(1)}, bf16[4,4,64,384]{3,2,1,0:T(8,128)(2,1)S(1)}, u32[]{:S(2)}, u32[]{:S(2)}) collective-permute-start(bf16[4,4,64,384]{3,2,1,0:T(8,128)(2,1)S(1)} %slice.81), channel_id=1, source_target_pairs={{0,96},{1,97},{2,98},{3,99},{4,100},{5,101},{6,102},{7,103},{8,104... | collective-permute-start | bytes 2359304 | tf_op jit(solution)/shard_map/ppermute | solution.py:605
  41.7 32.2 %collective-permute-start.9 = (bf16[4,4,80,384]{3,2,1,0:T(8,128)(2,1)S(1)}, bf16[4,4,80,384]{3,2,1,0:T(8,128)(2,1)S(1)}, u32[]{:S(2)}, u32[]{:S(2)}) collective-permute-start(bf16[4,4,80,384]{3,2,1,0:T(8,128)(2,1)S(1)} %bitcast.92), channel_id=1, source_target_pairs={{0,1},{1,0},{2,3},{3,2},{4,5},{5,4},{6,7},{7,6},{8,9},{9,8},{10,11... | collective-permute-start | bytes 2949128 | tf_op jit(solution)/shard_map/ppermute | solution.py:624
  41.7 3.6 %collective-permute-start.5 = (f32[8,128]{1,0:T(8,128)S(1)}, f32[8,128]{1,0:T(8,128)S(1)}, u32[]{:S(2)}, u32[]{:S(2)}) collective-permute-start(f32[8,128]{1,0:T(8,128)S(1)} %add.103), channel_id=1, source_target_pairs={{0,2},{1,3},{2,0},{3,1},{4,6},{5,7},{6,4},{7,5},{8,10},{9,11},{10,... | collective-permute-start | bytes 12296 | tf_op jit(solution)/shard_map/ppermute | solution.py:578
  45.3 4.8 %collective-permute-start.6 = (f32[8,128]{1,0:T(8,128)S(1)}, f32[8,128]{1,0:T(8,128)S(1)}, u32[]{:S(2)}, u32[]{:S(2)}) collective-permute-start(f32[8,128]{1,0:T(8,128)S(1)} %add.106), channel_id=1, source_target_pairs={{0,6},{1,7},{2,4},{3,5},{4,2},{5,3},{6,0},{7,1},{8,14},{9,15},{10,... | collective-permute-start | bytes 12296 | tf_op jit(solution)/shard_map/ppermute | solution.py:578
  50.1 3.6 %collective-permute-start.7 = (f32[8,128]{1,0:T(8,128)S(1)}, f32[8,128]{1,0:T(8,128)S(1)}, u32[]{:S(2)}, u32[]{:S(2)}) collective-permute-start(f32[8,128]{1,0:T(8,128)S(1)} %add.107), channel_id=1, source_target_pairs={{0,8},{1,9},{2,10},{3,11},{4,12},{5,13},{6,14},{7,15},{8,0},{9,1},... | collective-permute-start | bytes 12296 | tf_op jit(solution)/shard_map/ppermute | solution.py:578
  53.7 4.9 %collective-permute-start.8 = (f32[8,128]{1,0:T(8,128)S(1)}, f32[8,128]{1,0:T(8,128)S(1)}, u32[]{:S(2)}, u32[]{:S(2)}) collective-permute-start(f32[8,128]{1,0:T(8,128)S(1)} %add.108), channel_id=1, source_target_pairs={{0,24},{1,25},{2,26},{3,27},{4,28},{5,29},{6,30},{7,31},{8,16},{9,... | collective-permute-start | bytes 12296 | tf_op jit(solution)/shard_map/ppermute | solution.py:578
  58.6 15.8 %copy-start.4 = (bf16[4,4,64,384]{3,2,1,0:T(8,128)(2,1)}, bf16[4,4,64,384]{3,2,1,0:T(8,128)(2,1)S(1)}, u32[]{:S(2)}) copy-start(bf16[4,4,64,384]{3,2,1,0:T(8,128)(2,1)S(1)} %collective-permute-done.3.refs_2_) | copy-start | bytes 2359300
  58.6 15.8 %copy-start.5 = (bf16[4,4,64,384]{3,2,1,0:T(8,128)(2,1)}, bf16[4,4,64,384]{3,2,1,0:T(8,128)(2,1)S(1)}, u32[]{:S(2)}) copy-start(bf16[4,4,64,384]{3,2,1,0:T(8,128)(2,1)S(1)} %collective-permute-done.4.refs_4_) | copy-start | bytes 2359300
  58.6 15.2 %collective-permute-start.10 = (bf16[4,4,64,384]{3,2,1,0:T(8,128)(2,1)S(1)}, bf16[4,4,64,384]{3,2,1,0:T(8,128)(2,1)}, u32[]{:S(2)}, u32[]{:S(2)}) collective-permute-start(bf16[4,4,64,384]{3,2,1,0:T(8,128)(2,1)S(1)} %collective-permute-done.3.refs_2_), channel_id=1, source_target_pairs={{0,1},{1,0},{2,3},{3,2},{4,5},{5,4},{6,7},{7,6},{8,9},{9,8},{10,11... | collective-permute-start | bytes 2359304 | tf_op jit(solution)/shard_map/ppermute | solution.py:624
  58.8 15.1 %collective-permute-start.11 = (bf16[4,4,64,384]{3,2,1,0:T(8,128)(2,1)S(1)}, bf16[4,4,64,384]{3,2,1,0:T(8,128)(2,1)}, u32[]{:S(2)}, u32[]{:S(2)}) collective-permute-start(bf16[4,4,64,384]{3,2,1,0:T(8,128)(2,1)S(1)} %collective-permute-done.4.refs_4_), channel_id=1, source_target_pairs={{0,1},{1,0},{2,3},{3,2},{4,5},{5,4},{6,7},{7,6},{8,9},{9,8},{10,11... | collective-permute-start | bytes 2359304 | tf_op jit(solution)/shard_map/ppermute | solution.py:624
  59.3 12.4 %collective-permute-start.12 = (bf16[2,4,64,384]{3,2,1,0:T(8,128)(2,1)S(1)}, bf16[2,4,64,384]{3,2,1,0:T(8,128)(2,1)}, u32[]{:S(2)}, u32[]{:S(2)}) collective-permute-start(bf16[2,4,64,384]{3,2,1,0:T(8,128)(2,1)S(1)} %slice.84), channel_id=1, source_target_pairs={{0,32},{1,33},{2,34},{3,35},{4,36},{5,37},{6,38},{7,39},{8,40},{9,... | collective-permute-start | bytes 1179656 | tf_op jit(solution)/shard_map/ppermute | solution.py:605
  59.7 12.0 %collective-permute-start.14 = (bf16[2,4,64,384]{3,2,1,0:T(8,128)(2,1)S(1)}, bf16[2,4,64,384]{3,2,1,0:T(8,128)(2,1)}, u32[]{:S(2)}, u32[]{:S(2)}) collective-permute-start(bf16[2,4,64,384]{3,2,1,0:T(8,128)(2,1)S(1)} %slice.85), channel_id=1, source_target_pairs={{0,96},{1,97},{2,98},{3,99},{4,100},{5,101},{6,102},{7,103},{8,104... | collective-permute-start | bytes 1179656 | tf_op jit(solution)/shard_map/ppermute | solution.py:605
  71.7 2.1 collective-permute-start.13
  71.8 2.6 collective-permute-start.15
  147.4 6.7 %collective-permute-start.16 = (bf16[4,16,64,384]{3,2,1,0:T(8,128)(2,1)}, bf16[4,16,64,384]{3,2,1,0:T(8,128)(2,1)S(1)}, u32[]{:S(2)}, u32[]{:S(2)}) collective-permute-start(bf16[4,16,64,384]{3,2,1,0:T(8,128)(2,1)} %get-tuple-element.64), channel_id=1, source_target_pairs={{0,1},{1,0},{2,3},{3,2},{4,5},{5,4},{6,7},{7,6},{8,9},{9,8},{10,11... | collective-permute-start | bytes 9437192 | tf_op jit(solution)/shard_map/ppermute | solution.py:706
  158.9 42.6 %all-to-all-start.1 = ((bf16[4,16,64,384]{3,2,1,0:T(8,128)(2,1)}), bf16[4,16,64,384]{3,2,1,0:T(8,128)(2,1)S(1)}, u32[]{:S(2)}, u32[]{:S(2)}) async-start(bf16[4,16,64,384]{3,2,1,0:T(8,128)(2,1)} %add_convert_fusion), calls=%async_computation.1 | async-start | bytes 6291456 | tf_op jit(solution)/shard_map/all_to_all | solution.py:629
  163.6 1.3 collective-permute-start.17
  164.9 3.7 %collective-permute-start.18 = (f32[16,128]{1,0:T(8,128)S(1)}, f32[16,128]{1,0:T(8,128)S(1)}, u32[]{:S(2)}, u32[]{:S(2)}) collective-permute-start(f32[16,128]{1,0:T(8,128)S(1)} %fusion.12), channel_id=1, source_target_pairs={{0,2},{1,3},{2,0},{3,1},{4,6},{5,7},{6,4},{7,5},{8,10},{9,11},{10,... | collective-permute-start | bytes 24584 | tf_op jit(solution)/shard_map/ppermute | solution.py:578
  168.6 4.9 %collective-permute-start.19 = (f32[16,128]{1,0:T(8,128)S(1)}, f32[16,128]{1,0:T(8,128)S(1)}, u32[]{:S(2)}, u32[]{:S(2)}) collective-permute-start(f32[16,128]{1,0:T(8,128)S(1)} %fusion.15), channel_id=1, source_target_pairs={{0,6},{1,7},{2,4},{3,5},{4,2},{5,3},{6,0},{7,1},{8,14},{9,15},{10,... | collective-permute-start | bytes 24584 | tf_op jit(solution)/shard_map/ppermute | solution.py:578
  203.0 21.3 %copy-start.11 = (s32[4]{0:T(128)S(1)}, s32[4]{0:T(128)}, u32[]{:S(2)}) copy-start(s32[4]{0:T(128)} %pad_add_fusion.1.place_ref) | copy-start | bytes 52
  203.0 24.3 %copy-start.12 = (f32[512]{0:T(512)S(1)}, f32[512]{0:T(512)}, u32[]{:S(2)}) copy-start(f32[512]{0:T(512)} %param.11) | copy-start | bytes 6148
  203.1 29.0 %all-to-all-start.2 = ((bf16[16,64,384]{2,1,0:T(8,128)(2,1)}), bf16[16,64,384]{2,1,0:T(8,128)(2,1)S(1)}, u32[]{:S(2)}, u32[]{:S(2)}) async-start(bf16[16,64,384]{2,1,0:T(8,128)(2,1)} %reduce_sum.44), calls=%async_computation.2 | async-start | bytes 1572864 | tf_op jit(solution)/shard_map/all_to_all | solution.py:634
  207.0 10.8 %collective-permute-start.20 = (f32[16,128]{1,0:T(8,128)S(1)}, f32[16,128]{1,0:T(8,128)S(1)}, u32[]{:S(2)}, u32[]{:S(2)}) collective-permute-start(f32[16,128]{1,0:T(8,128)S(1)} %add.115), channel_id=1, source_target_pairs={{0,8},{1,9},{2,10},{3,11},{4,12},{5,13},{6,14},{7,15},{8,0},{9,1},... | collective-permute-start | bytes 24584 | tf_op jit(solution)/shard_map/ppermute | solution.py:578
  217.8 5.6 %collective-permute-start.21 = (f32[16,128]{1,0:T(8,128)S(1)}, f32[16,128]{1,0:T(8,128)S(1)}, u32[]{:S(2)}, u32[]{:S(2)}) collective-permute-start(f32[16,128]{1,0:T(8,128)S(1)} %add.116), channel_id=1, source_target_pairs={{0,24},{1,25},{2,26},{3,27},{4,28},{5,29},{6,30},{7,31},{8,16},{9,... | collective-permute-start | bytes 24584 | tf_op jit(solution)/shard_map/ppermute | solution.py:578
  223.4 3.7 %collective-permute-start.22 = (f32[16,128]{1,0:T(8,128)S(1)}, f32[16,128]{1,0:T(8,128)S(1)}, u32[]{:S(2)}, u32[]{:S(2)}) collective-permute-start(f32[16,128]{1,0:T(8,128)S(1)} %add.117), channel_id=1, source_target_pairs={{0,32},{1,33},{2,34},{3,35},{4,36},{5,37},{6,38},{7,39},{8,40},{9,... | collective-permute-start | bytes 24584 | tf_op jit(solution)/shard_map/ppermute | solution.py:578
  227.1 4.9 %collective-permute-start.23 = (f32[16,128]{1,0:T(8,128)S(1)}, f32[16,128]{1,0:T(8,128)S(1)}, u32[]{:S(2)}, u32[]{:S(2)}) collective-permute-start(f32[16,128]{1,0:T(8,128)S(1)} %add.118), channel_id=1, source_target_pairs={{0,96},{1,97},{2,98},{3,99},{4,100},{5,101},{6,102},{7,103},{8,104... | collective-permute-start | bytes 24584 | tf_op jit(solution)/shard_map/ppermute | solution.py:578
  232.1 4.2 %collective-permute-start.24 = (bf16[64,384]{1,0:T(8,128)(2,1)S(1)}, bf16[64,384]{1,0:T(8,128)(2,1)S(1)}, u32[]{:S(2)}, u32[]{:S(2)}) collective-permute-start(bf16[64,384]{1,0:T(8,128)(2,1)S(1)} %reduce_sum.45), channel_id=1, source_target_pairs={{0,96},{1,97},{2,98},{3,99},{4,100},{5,101},{6,102},{7,103},{8,104... | collective-permute-start | bytes 147464 | tf_op jit(solution)/shard_map/ppermute | solution.py:641
  232.4 5.6 %collective-permute-start.25 = (bf16[64,384]{1,0:T(8,128)(2,1)S(1)}, bf16[64,384]{1,0:T(8,128)(2,1)S(1)}, u32[]{:S(2)}, u32[]{:S(2)}) collective-permute-start(bf16[64,384]{1,0:T(8,128)(2,1)S(1)} %reduce_sum.45), channel_id=1, source_target_pairs={{0,64},{1,65},{2,66},{3,67},{4,68},{5,69},{6,70},{7,71},{8,72},{9,... | collective-permute-start | bytes 147464 | tf_op jit(solution)/shard_map/ppermute | solution.py:641
  233.9 5.3 %collective-permute-start.26 = (bf16[64,384]{1,0:T(8,128)(2,1)S(1)}, bf16[64,384]{1,0:T(8,128)(2,1)S(1)}, u32[]{:S(2)}, u32[]{:S(2)}) collective-permute-start(bf16[64,384]{1,0:T(8,128)(2,1)S(1)} %reduce_sum.45), channel_id=1, source_target_pairs={{0,32},{1,33},{2,34},{3,35},{4,36},{5,37},{6,38},{7,39},{8,40},{9,... | collective-permute-start | bytes 147464 | tf_op jit(solution)/shard_map/ppermute | solution.py:641
  239.2 13.2 %copy-start.2 = (bf16[768,512]{1,0:T(8,128)(2,1)S(1)}, bf16[768,512]{1,0:T(8,128)(2,1)}, u32[]{:S(2)}) copy-start(bf16[768,512]{1,0:T(8,128)(2,1)} %x_ref.3) | copy-start | bytes 2359300
  239.3 13.2 %copy-start.7 = (f32[768,512]{1,0:T(8,128)S(1)}, f32[768,512]{1,0:T(8,128)}, u32[]{:S(2)}) copy-start(f32[768,512]{1,0:T(8,128)} %get-tuple-element.62) | copy-start | bytes 4718596
  248.9 9.1 %collective-permute-start.27 = (bf16[80,1536]{1,0:T(8,128)(2,1)S(1)}, bf16[80,1536]{1,0:T(8,128)(2,1)S(1)}, u32[]{:S(2)}, u32[]{:S(2)}) collective-permute-start(bf16[80,1536]{1,0:T(8,128)(2,1)S(1)} %slice.94), channel_id=1, source_target_pairs={{0,96},{1,97},{2,98},{3,99},{4,100},{5,101},{6,102},{7,103},{8,104... | collective-permute-start | bytes 737288 | tf_op jit(solution)/shard_map/ppermute | solution.py:647
  251.7 5.7 %collective-permute-start.29 = (bf16[64,1536]{1,0:T(8,128)(2,1)S(1)}, bf16[64,1536]{1,0:T(8,128)(2,1)S(1)}, u32[]{:S(2)}, u32[]{:S(2)}) collective-permute-start(bf16[64,1536]{1,0:T(8,128)(2,1)S(1)} %slice.97), channel_id=1, source_target_pairs={{0,32},{1,33},{2,34},{3,35},{4,36},{5,37},{6,38},{7,39},{8,40},{9,... | collective-permute-start | bytes 589832 | tf_op jit(solution)/shard_map/ppermute | solution.py:647
  252.5 4.9 %copy-start.6 = (bf16[1,144,1536]{2,1,0:T(8,128)(2,1)S(1)}, bf16[1,144,1536]{2,1,0:T(8,128)(2,1)}, u32[]{:S(2)}) copy-start(bf16[1,144,1536]{2,1,0:T(8,128)(2,1)} %reduce-scatter.2.cloned.1.call-done) | copy-start | bytes 1327108
  257.4 7.0 %collective-permute-start.30 = (bf16[64,1536]{1,0:T(8,128)(2,1)S(1)}, bf16[64,1536]{1,0:T(8,128)(2,1)S(1)}, u32[]{:S(2)}, u32[]{:S(2)}) collective-permute-start(bf16[64,1536]{1,0:T(8,128)(2,1)S(1)} %add_convert_fusion.2), channel_id=1, source_target_pairs={{0,96},{1,97},{2,98},{3,99},{4,100},{5,101},{6,102},{7,103},{8,104... | collective-permute-start | bytes 589832 | tf_op jit(solution)/shard_map/ppermute | solution.py:647
  258.1 6.3 %collective-permute-start.28 = (bf16[80,1536]{1,0:T(8,128)(2,1)S(1)}, bf16[80,1536]{1,0:T(8,128)(2,1)S(1)}, u32[]{:S(2)}, u32[]{:S(2)}) collective-permute-start(bf16[80,1536]{1,0:T(8,128)(2,1)S(1)} %add_convert_fusion.1), channel_id=1, source_target_pairs={{0,32},{1,33},{2,34},{3,35},{4,36},{5,37},{6,38},{7,39},{8,40},{9,... | collective-permute-start | bytes 737288 | tf_op jit(solution)/shard_map/ppermute | solution.py:647
  (8 other events, 21.9 us)
Sparse Core Ops, SparseCore 0:
  10.3 70.8 all-gather.1
  127.9 118.4 reduce-scatter.1
